TPU v7x, 128 devices: a whole 4x4x4 slice. The times are simulated.
128 devices in a mesh: gx: 8 (over z, core), gy: 16 (over y, x).
Axes of the slice: x: 4, y: 4, z: 4, core: 2. Of those that a mesh axis runs over, the one named last changes fastest.
Arguments:
- canopy: float32 [8, 64, 128, 1024], P(None, None, 'gy', 'gx'), may hold values from -6 to 6
- courant: float32 [2, 64], replicated, may hold values from -0.35 to 0.35
- walls: float32 [6, 128, 32768], P(None, None, ('gx', 'gy')), may hold values from -6 to 6
- inverses: float32 [8, 128, 128], replicated, as said below
- package: int32 [32768], P(('gx', 'gy')), may hold values from 0 to 7
- surf_coeff: float32 [6, 32768], P(None, ('gx', 'gy')), may hold values from 0.2 to 2
- facade_area: float32 [64, 32768], P(None, ('gx', 'gy')), may hold values from 0.05 to 1
- anchor: int32 [32768, 1], P(('gx', 'gy')), may hold values from 0 to 127; in each aligned block of 256 rows (0 to 255, 256 to 511, ...) at most 10 rows name the same one
- footprint: int32 [32768, 8], P(('gx', 'gy')), may hold values from 0 to 1023
Outputs:
- canopy_out: float32 [8, 64, 128, 1024], P(None, None, 'gy', 'gx')
- building_air: float32 [2, 64, 32768], P(None, None, ('gx', 'gy'))
- walls_out: float32 [6, 128, 32768], P(None, None, ('gx', 'gy'))
Inputs may be any that keep to these rules, and one draw needn't show every extreme that they name: The footprint of building b lies in the tile of the device with linear index anchor[b, 0] over gx and gy, gx slowest; among the 256 buildings of one device at most 10 share an anchor. `footprint`: a cell y * 128 + x with y, x local to the anchor tile. `inverses`: one matrix per retrofit package.
All inputs are finite; a program needn't handle non-finite values.
Results may differ from a plain program's by a relative error of at most 0.0003.
Values sent between devices are 32-bit elements; how exact they have to be, the bound alone decides.
No kernel may reach another device: no remote copies, remote signals or barrier semaphores. Data moves between devices by JAX's collectives and lax.ppermute only.
A program may use at most 128 MiB of HBM per device.

v0:
```python
import jax
import jax.numpy as jnp
from jax import lax
from jax.sharding import PartitionSpec as P

PKG = 8
SUB = 4


source_rate = 0.1
kappa_rate = 0.05
vertical_rate = 0.05
wall_gain = 0.5


def with_halo(value, sides, width):
    for axis, dim in sides:
        peers, length = (lax.axis_size(axis), value.shape[dim])
        up = [(i, (i + 1) % peers) for i in range(peers - 1)]
        down = [(j, i) for i, j in up]
        last = lax.slice_in_dim(value, length - width, length, axis=dim)
        leading = lax.slice_in_dim(value, 0, width, axis=dim)
        before = lax.ppermute(last, axis, up)
        after = lax.ppermute(leading, axis, down)
        value = jnp.concatenate([before, value, after], axis=dim)
    return value


def stencil(padded, courant):
    center = padded[..., 1:-1, 1:-1]
    west_cells = padded[..., 1:-1, :-2]
    east_cells = padded[..., 1:-1, 2:]
    south_cells = padded[..., :-2, 1:-1]
    north_cells = padded[..., 2:, 1:-1]
    courant_x = courant[0][:, None, None]
    courant_y = courant[1][:, None, None]
    upwind = jnp.maximum(courant_x, 0.0) * (center - west_cells) + jnp.minimum(courant_x, 0.0) * (
        east_cells - center
    )
    upwind = (
        upwind
        + jnp.maximum(courant_y, 0.0) * (center - south_cells)
        + jnp.minimum(courant_y, 0.0) * (north_cells - center)
    )
    spread = east_cells + west_cells + north_cells + south_cells - 4.0 * center
    above = jnp.concatenate([center[..., 1:, :, :], center[..., -1:, :, :]], axis=-3)
    below = jnp.concatenate([center[..., :1, :, :], center[..., :-1, :, :]], axis=-3)
    vertical = above + below - 2.0 * center
    return center - upwind + kappa_rate * spread + vertical_rate * vertical


def advance(theta, courant):
    padded = with_halo(theta, (("gx", 3), ("gy", 2)), 1)
    return stencil(padded, courant)


def select_walls(inverses, rhs_walls, package):
    result = jnp.zeros_like(rhs_walls)
    for package_id in range(PKG):
        product = jnp.einsum(
            "nm,smb->snb", inverses[package_id], rhs_walls, precision=lax.Precision.HIGHEST
        )
        result = jnp.where((package == package_id)[None, None, :], product, result)
    return result


def body(canopy, courant, walls, inverses, package, surf_coeff, facade_area, anchor, footprint):
    device_count = lax.axis_size(("gx", "gy"))
    levels = canopy.shape[1]
    rows_y = canopy.shape[2]
    cols_x = canopy.shape[3]
    tile_cells = rows_y * cols_x
    count_b = walls.shape[2]
    foot_slots = footprint.shape[1]
    capacity = max(2, 5 * count_b // device_count)
    width = 2 * levels
    surface = walls[:, 0, :]
    heat = jnp.sum(surf_coeff * surface, axis=0)
    coupling = jnp.sum(surf_coeff, axis=0)
    payload = jnp.concatenate(
        [facade_area * heat[None, :], facade_area * coupling[None, :]], axis=0
    ).T
    target = anchor[:, 0]
    onehot = (target[:, None] == jnp.arange(device_count, dtype=jnp.int32)[None, :]).astype(
        jnp.int32
    )
    before = jnp.cumsum(onehot, axis=0) - onehot
    slot_rank = jnp.sum(before * onehot, axis=1)
    slot_index = target * capacity + slot_rank
    send_flux = jnp.zeros((device_count * capacity, width), jnp.float32).at[slot_index].set(payload)
    send_cells = (
        jnp.zeros((device_count * capacity, foot_slots), jnp.float32)
        .at[slot_index]
        .set(footprint.astype(jnp.float32))
    )
    recv_flux, recv_cells = (
        lax.all_to_all(
            send_flux.reshape(device_count, capacity, width),
            ("gx", "gy"),
            split_axis=0,
            concat_axis=0,
            tiled=True,
        ),
        lax.all_to_all(
            send_cells.reshape(device_count, capacity, foot_slots),
            ("gx", "gy"),
            split_axis=0,
            concat_axis=0,
            tiled=True,
        ),
    )
    recv_flux = recv_flux.reshape(device_count * capacity, width)
    cell_table = recv_cells.reshape(device_count * capacity, foot_slots).astype(jnp.int32)
    summed = jnp.zeros((tile_cells, width), jnp.float32)
    for foot_id in range(foot_slots):
        summed = summed.at[cell_table[:, foot_id]].add(recv_flux)
    psum = summed[:, :levels].T.reshape(levels, rows_y, cols_x)
    qsum = summed[:, levels:].T.reshape(levels, rows_y, cols_x)
    theta = canopy.at[0].add(source_rate * (psum - qsum * canopy[0]) / foot_slots)
    for step in range(SUB):
        theta = advance(theta, courant)
    cell_rows = theta[:2].reshape(width, tile_cells).T
    air_total = jnp.zeros((device_count * capacity, width), jnp.float32)
    for foot_id in range(foot_slots):
        air_total = air_total + cell_rows[cell_table[:, foot_id]]
    outgoing = air_total / foot_slots
    returned = lax.all_to_all(
        outgoing.reshape(device_count, capacity, width),
        ("gx", "gy"),
        split_axis=0,
        concat_axis=0,
        tiled=True,
    )
    returned = returned.reshape(device_count * capacity, width)
    own_air = returned[slot_index]
    building_air = own_air.T.reshape(2, levels, count_b)
    air_temp = jnp.sum(facade_area * building_air[0], axis=0) / jnp.sum(facade_area, axis=0)
    wall_source = wall_gain * surf_coeff * (air_temp[None, :] - surface)
    rhs_walls = walls.at[:, 0, :].add(wall_source)
    walls_out = select_walls(inverses, rhs_walls, package)
    return (theta, building_air, walls_out)


def solution(mesh):
    placed = (
        P(None, None, "gy", "gx"),
        P(),
        P(None, None, ("gx", "gy")),
        P(),
        P(("gx", "gy")),
        P(None, ("gx", "gy")),
        P(None, ("gx", "gy")),
        P(("gx", "gy"), None),
        P(("gx", "gy"), None),
    )
    return jax.shard_map(
        body,
        mesh=mesh,
        in_specs=placed,
        out_specs=(
            P(None, None, "gy", "gx"),
            P(None, None, ("gx", "gy")),
            P(None, None, ("gx", "gy")),
        ),
        check_vma=False,
    )
```

profile of v0, /device:TPU:1, one launch (start us, length us, event | category | flops | bytes accessed | tf_op | source)
XLA Modules:
  0.0 407.5 jit_solution(6299511852439073270)
XLA Ops:
  8.4 11.5 %all-to-all-start = ((f32[128,10,8]{1,2,0:T(8,128)}), f32[128,10,8]{1,2,0:T(8,128)S(1)}, u32[]{:S(2)}, u32[]{:S(2)}) async-start(f32[128,10,8]{1,2,0:T(8,128)} %copy.104), calls=%async_computation | async-start | bytes 1048576 | tf_op jit(solution)/shard_map/all_to_all | solution.py:104
  23.1 10.8 %all-to-all-done = f32[128,10,8]{1,2,0:T(8,128)S(1)} async-done(((f32[128,10,8]{1,2,0:T(8,128)}), f32[128,10,8]{1,2,0:T(8,128)S(1)}, u32[]{:S(2)}, u32[]{:S(2)}) %all-to-all-start) | async-done | bytes 40992 | tf_op jit(solution)/shard_map/all_to_all | solution.py:104
  33.9 4.2 %all-to-all-start.1 = ((f32[128,10,128]{2,1,0:T(8,128)}), f32[128,10,128]{2,1,0:T(8,128)S(1)}, u32[]{:S(2)}, u32[]{:S(2)}) async-start(f32[128,10,128]{2,1,0:T(8,128)} %reshape.190), calls=%async_computation.1 | async-start | bytes 2097152 | tf_op jit(solution)/shard_map/all_to_all | solution.py:97
  45.7 11.3 %all-to-all-done.1 = f32[128,10,128]{2,1,0:T(8,128)S(1)} async-done(((f32[128,10,128]{2,1,0:T(8,128)}), f32[128,10,128]{2,1,0:T(8,128)S(1)}, u32[]{:S(2)}, u32[]{:S(2)}) %all-to-all-start.1) | async-done | bytes 655392 | tf_op jit(solution)/shard_map/all_to_all | solution.py:97
  57.0 9.1 %scatter_custom_fusion.2 = f32[1024,128]{1,0:T(8,128)S(1)} fusion(s32[1280]{0:T(1024)S(1)} %get-tuple-element.46, f32[1280,128]{1,0:T(8,128)S(1)} %reshape.351, f32[]{:T(128)} %constant.84.clone.1), kind=kCustom, calls=%fused_computation.166 | custom fusion | flops 163840 | bytes 524292 | tf_op jit(solution)/shard_map/scatter-add | solution.py:116
  66.1 9.1 %scatter_fusion = f32[1024,128]{1,0:T(8,128)S(1)} fusion(f32[1024,128]{1,0:T(8,128)S(1)} %scatter_custom_fusion.2, s32[1280]{0:T(1024)S(1)} %get-tuple-element.45, f32[1280,128]{1,0:T(8,128)S(1)} %reshape.351), kind=kCustom, calls=%fused_computation.12 | custom fusion | flops 163840 | bytes 1971200 | tf_op jit(solution)/shard_map/scatter-add | solution.py:116
  75.3 9.3 %scatter_fusion.1 = f32[1024,128]{1,0:T(8,128)S(1)} fusion(f32[1024,128]{1,0:T(8,128)S(1)} %scatter_fusion, s32[1280]{0:T(1024)S(1)} %get-tuple-element.44, f32[1280,128]{1,0:T(8,128)S(1)} %reshape.351), kind=kCustom, calls=%fused_computation.13 | custom fusion | flops 163840 | bytes 1971200 | tf_op jit(solution)/shard_map/scatter-add | solution.py:116
  84.6 9.1 %scatter_fusion.2 = f32[1024,128]{1,0:T(8,128)S(1)} fusion(f32[1024,128]{1,0:T(8,128)S(1)} %scatter_fusion.1, s32[1280]{0:T(1024)S(1)} %get-tuple-element.43, f32[1280,128]{1,0:T(8,128)S(1)} %reshape.351), kind=kCustom, calls=%fused_computation.14 | custom fusion | flops 163840 | bytes 1971200 | tf_op jit(solution)/shard_map/scatter-add | solution.py:116
  93.8 9.1 %scatter_fusion.3 = f32[1024,128]{1,0:T(8,128)S(1)} fusion(f32[1024,128]{1,0:T(8,128)S(1)} %scatter_fusion.2, s32[1280]{0:T(1024)S(1)} %get-tuple-element.42, f32[1280,128]{1,0:T(8,128)S(1)} %reshape.351), kind=kCustom, calls=%fused_computation.15 | custom fusion | flops 163840 | bytes 1971200 | tf_op jit(solution)/shard_map/scatter-add | solution.py:116
  102.9 9.1 %scatter_fusion.4 = f32[1024,128]{1,0:T(8,128)S(1)} fusion(f32[1024,128]{1,0:T(8,128)S(1)} %scatter_fusion.3, s32[1280]{0:T(1024)S(1)} %get-tuple-element.41, f32[1280,128]{1,0:T(8,128)S(1)} %reshape.351), kind=kCustom, calls=%fused_computation.16 | custom fusion | flops 163840 | bytes 1971200 | tf_op jit(solution)/shard_map/scatter-add | solution.py:116
  112.1 9.4 %scatter_fusion.5 = f32[1024,128]{1,0:T(8,128)S(1)} fusion(f32[1024,128]{1,0:T(8,128)S(1)} %scatter_fusion.4, s32[1280]{0:T(1024)S(1)} %get-tuple-element.40, f32[1280,128]{1,0:T(8,128)S(1)} %reshape.351), kind=kCustom, calls=%fused_computation.17 | custom fusion | flops 163840 | bytes 1971200 | tf_op jit(solution)/shard_map/scatter-add | solution.py:116
  121.4 9.1 %scatter_fusion.6 = f32[1024,128]{1,0:T(8,128)S(1)} fusion(f32[1024,128]{1,0:T(8,128)S(1)} %scatter_fusion.5, s32[1280]{0:T(1024)S(1)} %get-tuple-element.39, f32[1280,128]{1,0:T(8,128)S(1)} %reshape.351), kind=kCustom, calls=%fused_computation.18 | custom fusion | flops 163840 | bytes 1971200 | tf_op jit(solution)/shard_map/scatter-add | solution.py:116
  134.1 12.4 %collective-permute-start = (f32[8,64,8,1]{1,2,3,0:T(8,128)S(1)}, f32[8,64,8,1]{1,2,3,0:T(8,128)S(1)}, u32[]{:S(2)}, u32[]{:S(2)}) collective-permute-start(f32[8,64,8,1]{1,2,3,0:T(8,128)S(1)} %get-tuple-element.79), channel_id=1, source_target_pairs={{0,16},{16,32},{32,48},{48,64},{64,80},{80,96},{96,112},{1,17},{17... | collective-permute-start | bytes 49160 | tf_op jit(solution)/shard_map/ppermute | solution.py:23
  148.7 7.9 %fusion.135 = (f32[8,1,8,128]{1,2,3,0:T(8,128)}, f32[8,1,8,128]{1,2,3,0:T(8,128)}) fusion(f32[8,64,8,128]{1,2,3,0:T(8,128)} %constant_dynamic-update-slice_fusion), kind=kLoop, calls=%fused_computation.254 | loop fusion | bytes 131072 | tf_op jit(solution)/shard_map/slice | solution.py:47
  161.7 7.9 %fusion.136 = (f32[8,63,8,128]{1,2,3,0:T(8,128)}, f32[8,63,8,128]{1,2,3,0:T(8,128)}) fusion(f32[8,64,8,128]{1,2,3,0:T(8,128)} %constant_dynamic-update-slice_fusion), kind=kLoop, calls=%fused_computation.255 | loop fusion | bytes 8257536 | tf_op jit(solution)/shard_map/slice | solution.py:47
  170.9 4.1 collective-permute-done.3
  175.5 16.2 %fusion.63 = f32[8,64,8,128]{1,2,3,0:T(8,128)S(1)} fusion(f32[8,64,1,130]{1,2,3,0:T(1,128)S(1)} %copy.116, f32[8,64,8,1]{1,2,3,0:T(8,128)S(1)} %collective-permute-done.1, f32[8,64,8,128]{1,2,3,0:T(8,128)} %constant_dynamic-update-slice_fusion, f32[8,64,8,1]{1,2,3,0:T(8,128)S(1)} %collective-permute-done, f32[8,64,1,130]{1,2,3,0:T(1,128)S(1)} %copy.114, ...), kind=kLoop, calls=%fused_computation.109 | loop fusion | flops 17825792 | bytes 8954880 | tf_op jit(solution)/shard_map/add | solution.py:49
  197.7 4.6 %fusion.132 = (f32[8,1,8,128]{1,2,3,0:T(8,128)}, f32[8,1,8,128]{1,2,3,0:T(8,128)}) fusion(f32[8,64,8,128]{1,2,3,0:T(8,128)S(1)} %fusion.63), kind=kLoop, calls=%fused_computation.251 | loop fusion | bytes 131072 | tf_op jit(solution)/shard_map/slice | solution.py:47
  207.3 7.9 %fusion.133 = (f32[8,63,8,128]{1,2,3,0:T(8,128)}, f32[8,63,8,128]{1,2,3,0:T(8,128)}) fusion(f32[8,64,8,128]{1,2,3,0:T(8,128)} %copy-done.2), kind=kLoop, calls=%fused_computation.252 | loop fusion | bytes 8257536 | tf_op jit(solution)/shard_map/slice | solution.py:47
  216.1 4.1 collective-permute-done.7
  220.8 16.2 %fusion.44 = f32[8,64,8,128]{1,2,3,0:T(8,128)S(1)} fusion(f32[8,64,1,130]{1,2,3,0:T(1,128)S(1)} %copy.120, f32[8,64,8,1]{1,2,3,0:T(8,128)S(1)} %collective-permute-done.5, f32[8,64,8,128]{1,2,3,0:T(8,128)} %copy-done.2, f32[8,64,8,1]{1,2,3,0:T(8,128)S(1)} %collective-permute-done.4, f32[8,64,1,130]{1,2,3,0:T(1,128)S(1)} %copy.118, ...), kind=kLoop, calls=%fused_computation.82 | loop fusion | flops 17825792 | bytes 8954880 | tf_op jit(solution)/shard_map/add | solution.py:49
  237.0 4.0 collective-permute-start.8
  243.0 4.6 %fusion.129 = (f32[8,1,8,128]{1,2,3,0:T(8,128)}, f32[8,1,8,128]{1,2,3,0:T(8,128)}) fusion(f32[8,64,8,128]{1,2,3,0:T(8,128)S(1)} %fusion.44), kind=kLoop, calls=%fused_computation.248 | loop fusion | bytes 131072 | tf_op jit(solution)/shard_map/slice | solution.py:47
  248.8 5.4 %collective-permute-start.10 = (f32[8,64,1,130]{3,1,2,0:T(8,128)S(1)}, f32[8,64,1,130]{3,1,2,0:T(8,128)S(1)}, u32[]{:S(2)}, u32[]{:S(2)}) collective-permute-start(f32[8,64,1,130]{3,1,2,0:T(8,128)S(1)} %copy.121), channel_id=1, source_target_pairs={{0,1},{1,2},{2,3},{3,4},{4,5},{5,6},{6,7},{7,8},{8,9},{9,10},{10,1... | collective-permute-start | bytes 798728 | tf_op jit(solution)/shard_map/ppermute | solution.py:23
  256.2 7.9 %fusion.130 = (f32[8,63,8,128]{1,2,3,0:T(8,128)}, f32[8,63,8,128]{1,2,3,0:T(8,128)}) fusion(f32[8,64,8,128]{1,2,3,0:T(8,128)} %copy-done.3), kind=kLoop, calls=%fused_computation.249 | loop fusion | bytes 8257536 | tf_op jit(solution)/shard_map/slice | solution.py:47
  268.1 16.2 %fusion.25 = f32[8,64,8,128]{1,2,3,0:T(8,128)S(1)} fusion(f32[8,64,1,130]{1,2,3,0:T(1,128)S(1)} %copy.124, f32[8,64,8,1]{1,2,3,0:T(8,128)S(1)} %collective-permute-done.9, f32[8,64,8,128]{1,2,3,0:T(8,128)} %copy-done.3, f32[8,64,8,1]{1,2,3,0:T(8,128)S(1)} %collective-permute-done.8, f32[8,64,1,130]{1,2,3,0:T(1,128)S(1)} %copy.122, ...), kind=kLoop, calls=%fused_computation.55 | loop fusion | flops 17825792 | bytes 8954880 | tf_op jit(solution)/shard_map/add | solution.py:49
  284.4 5.9 %collective-permute-start.12 = (f32[8,64,8,1]{1,2,3,0:T(8,128)S(1)}, f32[8,64,8,1]{1,2,3,0:T(8,128)S(1)}, u32[]{:S(2)}, u32[]{:S(2)}) collective-permute-start(f32[8,64,8,1]{1,2,3,0:T(8,128)S(1)} %get-tuple-element.61), channel_id=1, source_target_pairs={{0,16},{16,32},{32,48},{48,64},{64,80},{80,96},{96,112},{1,17},{17... | collective-permute-start | bytes 49160 | tf_op jit(solution)/shard_map/ppermute | solution.py:23
  292.2 4.6 %fusion.126 = (f32[8,1,8,128]{1,2,3,0:T(8,128)}, f32[8,1,8,128]{1,2,3,0:T(8,128)}) fusion(f32[8,64,8,128]{1,2,3,0:T(8,128)S(1)} %fusion.25), kind=kLoop, calls=%fused_computation.245 | loop fusion | bytes 131072 | tf_op jit(solution)/shard_map/slice | solution.py:47
  304.1 7.9 %fusion.127 = (f32[8,63,8,128]{1,2,3,0:T(8,128)}, f32[8,63,8,128]{1,2,3,0:T(8,128)}) fusion(f32[8,64,8,128]{1,2,3,0:T(8,128)} %copy-done.1), kind=kLoop, calls=%fused_computation.246 | loop fusion | bytes 8257536 | tf_op jit(solution)/shard_map/slice | solution.py:47
  316.0 16.2 %fusion.6 = f32[8,64,8,128]{1,2,3,0:T(8,128)S(1)} fusion(f32[8,64,1,130]{1,2,3,0:T(1,128)S(1)} %copy.128, f32[8,64,8,1]{1,2,3,0:T(8,128)S(1)} %collective-permute-done.13, f32[8,64,8,128]{1,2,3,0:T(8,128)} %copy-done.1, f32[8,64,8,1]{1,2,3,0:T(8,128)S(1)} %collective-permute-done.12, f32[8,64,1,130]{1,2,3,0:T(1,128)S(1)} %copy.126, ...), kind=kLoop, calls=%fused_computation.28 | loop fusion | flops 17825792 | bytes 8954880 | tf_op jit(solution)/shard_map/add | solution.py:49
  362.6 11.2 %all-to-all-start.2 = ((f32[128,10,128]{2,1,0:T(8,128)}), f32[128,10,128]{2,1,0:T(8,128)S(1)}, u32[]{:S(2)}, u32[]{:S(2)}) async-start(f32[128,10,128]{2,1,0:T(8,128)} %reshape.202), calls=%async_computation.2 | async-start | bytes 2097152 | tf_op jit(solution)/shard_map/all_to_all | solution.py:127
  377.8 14.8 %all-to-all-done.2 = f32[128,10,128]{2,1,0:T(8,128)S(1)} async-done(((f32[128,10,128]{2,1,0:T(8,128)}), f32[128,10,128]{2,1,0:T(8,128)S(1)}, u32[]{:S(2)}, u32[]{:S(2)}) %all-to-all-start.2) | async-done | bytes 655392 | tf_op jit(solution)/shard_map/all_to_all | solution.py:127
  (170 shorter events, 114.4 us)
Async XLA Ops:
  0.6 19.3 %copy-start.15 = (f32[6,256]{1,0:T(8,128)S(1)}, f32[6,256]{1,0:T(8,128)}, u32[]{:S(2)}) copy-start(f32[6,256]{1,0:T(8,128)} %param.18) | copy-start | bytes 18436
  0.6 19.3 %copy-start.6 = (f32[64,256]{1,0:T(8,128)S(1)}, f32[64,256]{1,0:T(8,128)}, u32[]{:S(2)}) copy-start(f32[64,256]{1,0:T(8,128)} %param.19) | copy-start | bytes 196612
  4.5 29.4 %copy-start.18 = (s32[256,1]{0,1:T(1,128)}, s32[256,1]{0,1:T(1,128)S(1)}, u32[]{:S(2)}) copy-start(s32[256,1]{0,1:T(1,128)S(1)} %compare_select_fusion.8) | copy-start | bytes 3076
  6.6 31.4 %copy-start.20 = (f32[2,64]{1,0:T(2,128)S(1)}, f32[2,64]{1,0:T(2,128)}, u32[]{:S(2)}) copy-start(f32[2,64]{1,0:T(2,128)} %param.14) | copy-start | bytes 1540
  8.4 25.4 %all-to-all-start = ((f32[128,10,8]{1,2,0:T(8,128)}), f32[128,10,8]{1,2,0:T(8,128)S(1)}, u32[]{:S(2)}, u32[]{:S(2)}) async-start(f32[128,10,8]{1,2,0:T(8,128)} %copy.104), calls=%async_computation | async-start | bytes 1048576 | tf_op jit(solution)/shard_map/all_to_all | solution.py:104
  33.9 23.1 %all-to-all-start.1 = ((f32[128,10,128]{2,1,0:T(8,128)}), f32[128,10,128]{2,1,0:T(8,128)S(1)}, u32[]{:S(2)}, u32[]{:S(2)}) async-start(f32[128,10,128]{2,1,0:T(8,128)} %reshape.190), calls=%async_computation.1 | async-start | bytes 2097152 | tf_op jit(solution)/shard_map/all_to_all | solution.py:97
  134.1 22.6 %collective-permute-start = (f32[8,64,8,1]{1,2,3,0:T(8,128)S(1)}, f32[8,64,8,1]{1,2,3,0:T(8,128)S(1)}, u32[]{:S(2)}, u32[]{:S(2)}) collective-permute-start(f32[8,64,8,1]{1,2,3,0:T(8,128)S(1)} %get-tuple-element.79), channel_id=1, source_target_pairs={{0,16},{16,32},{32,48},{48,64},{64,80},{80,96},{96,112},{1,17},{17... | collective-permute-start | bytes 49160 | tf_op jit(solution)/shard_map/ppermute | solution.py:23
  146.5 10.1 %copy-start = (f32[8,64,8,128]{1,2,3,0:T(8,128)S(1)}, f32[8,64,8,128]{1,2,3,0:T(8,128)}, u32[]{:S(2)}) copy-start(f32[8,64,8,128]{1,2,3,0:T(8,128)} %constant_dynamic-update-slice_fusion) | copy-start | bytes 6291460
  146.5 10.1 %collective-permute-start.1 = (f32[8,64,8,1]{1,2,3,0:T(8,128)S(1)}, f32[8,64,8,1]{1,2,3,0:T(8,128)S(1)}, u32[]{:S(2)}, u32[]{:S(2)}) collective-permute-start(f32[8,64,8,1]{1,2,3,0:T(8,128)S(1)} %get-tuple-element.80), channel_id=1, source_target_pairs={{16,0},{32,16},{48,32},{64,48},{80,64},{96,80},{112,96},{17,1},{33... | collective-permute-start | bytes 49160 | tf_op jit(solution)/shard_map/ppermute | solution.py:24
  157.9 12.4 %collective-permute-start.2 = (f32[8,64,1,130]{3,1,2,0:T(8,128)S(1)}, f32[8,64,1,130]{3,1,2,0:T(8,128)S(1)}, u32[]{:S(2)}, u32[]{:S(2)}) collective-permute-start(f32[8,64,1,130]{3,1,2,0:T(8,128)S(1)} %copy.113), channel_id=1, source_target_pairs={{0,1},{1,2},{2,3},{3,4},{4,5},{5,6},{6,7},{7,8},{8,9},{9,10},{10,1... | collective-permute-start | bytes 798728 | tf_op jit(solution)/shard_map/ppermute | solution.py:23
  160.4 14.6 %collective-permute-start.3 = (f32[8,64,1,130]{3,1,2,0:T(8,128)S(1)}, f32[8,64,1,130]{3,1,2,0:T(8,128)S(1)}, u32[]{:S(2)}, u32[]{:S(2)}) collective-permute-start(f32[8,64,1,130]{3,1,2,0:T(8,128)S(1)} %copy.115), channel_id=1, source_target_pairs={{1,0},{2,1},{3,2},{4,3},{5,4},{6,5},{7,6},{8,7},{9,8},{10,9},{11,1... | collective-permute-start | bytes 798728 | tf_op jit(solution)/shard_map/ppermute | solution.py:24
  191.7 10.6 %copy-start.2 = (f32[8,64,8,128]{1,2,3,0:T(8,128)}, f32[8,64,8,128]{1,2,3,0:T(8,128)S(1)}, u32[]{:S(2)}) copy-start(f32[8,64,8,128]{1,2,3,0:T(8,128)S(1)} %fusion.63) | copy-start | bytes 6291460
  191.8 10.5 %collective-permute-start.4 = (f32[8,64,8,1]{1,2,3,0:T(8,128)S(1)}, f32[8,64,8,1]{1,2,3,0:T(8,128)S(1)}, u32[]{:S(2)}, u32[]{:S(2)}) collective-permute-start(f32[8,64,8,1]{1,2,3,0:T(8,128)S(1)} %get-tuple-element.73), channel_id=1, source_target_pairs={{0,16},{16,32},{32,48},{48,64},{64,80},{80,96},{96,112},{1,17},{17... | collective-permute-start | bytes 49160 | tf_op jit(solution)/shard_map/ppermute | solution.py:23
  195.3 6.9 %collective-permute-start.5 = (f32[8,64,8,1]{1,2,3,0:T(8,128)S(1)}, f32[8,64,8,1]{1,2,3,0:T(8,128)S(1)}, u32[]{:S(2)}, u32[]{:S(2)}) collective-permute-start(f32[8,64,8,1]{1,2,3,0:T(8,128)S(1)} %get-tuple-element.74), channel_id=1, source_target_pairs={{16,0},{32,16},{48,32},{64,48},{80,64},{96,80},{112,96},{17,1},{33... | collective-permute-start | bytes 49160 | tf_op jit(solution)/shard_map/ppermute | solution.py:24
  203.6 12.0 %collective-permute-start.6 = (f32[8,64,1,130]{3,1,2,0:T(8,128)S(1)}, f32[8,64,1,130]{3,1,2,0:T(8,128)S(1)}, u32[]{:S(2)}, u32[]{:S(2)}) collective-permute-start(f32[8,64,1,130]{3,1,2,0:T(8,128)S(1)} %copy.117), channel_id=1, source_target_pairs={{0,1},{1,2},{2,3},{3,4},{4,5},{5,6},{6,7},{7,8},{8,9},{9,10},{10,1... | collective-permute-start | bytes 798728 | tf_op jit(solution)/shard_map/ppermute | solution.py:23
  206.0 14.2 %collective-permute-start.7 = (f32[8,64,1,130]{3,1,2,0:T(8,128)S(1)}, f32[8,64,1,130]{3,1,2,0:T(8,128)S(1)}, u32[]{:S(2)}, u32[]{:S(2)}) collective-permute-start(f32[8,64,1,130]{3,1,2,0:T(8,128)S(1)} %copy.119), channel_id=1, source_target_pairs={{1,0},{2,1},{3,2},{4,3},{5,4},{6,5},{7,6},{8,7},{9,8},{10,9},{11,1... | collective-permute-start | bytes 798728 | tf_op jit(solution)/shard_map/ppermute | solution.py:24
  236.9 10.6 %copy-start.3 = (f32[8,64,8,128]{1,2,3,0:T(8,128)}, f32[8,64,8,128]{1,2,3,0:T(8,128)S(1)}, u32[]{:S(2)}) copy-start(f32[8,64,8,128]{1,2,3,0:T(8,128)S(1)} %fusion.44) | copy-start | bytes 6291460
  237.0 10.6 %collective-permute-start.8 = (f32[8,64,8,1]{1,2,3,0:T(8,128)S(1)}, f32[8,64,8,1]{1,2,3,0:T(8,128)S(1)}, u32[]{:S(2)}, u32[]{:S(2)}) collective-permute-start(f32[8,64,8,1]{1,2,3,0:T(8,128)S(1)} %get-tuple-element.67), channel_id=1, source_target_pairs={{0,16},{16,32},{32,48},{48,64},{64,80},{80,96},{96,112},{1,17},{17... | collective-permute-start | bytes 49160 | tf_op jit(solution)/shard_map/ppermute | solution.py:23
  241.0 6.5 %collective-permute-start.9 = (f32[8,64,8,1]{1,2,3,0:T(8,128)S(1)}, f32[8,64,8,1]{1,2,3,0:T(8,128)S(1)}, u32[]{:S(2)}, u32[]{:S(2)}) collective-permute-start(f32[8,64,8,1]{1,2,3,0:T(8,128)S(1)} %get-tuple-element.68), channel_id=1, source_target_pairs={{16,0},{32,16},{48,32},{64,48},{80,64},{96,80},{112,96},{17,1},{33... | collective-permute-start | bytes 49160 | tf_op jit(solution)/shard_map/ppermute | solution.py:24
  248.8 15.2 %collective-permute-start.10 = (f32[8,64,1,130]{3,1,2,0:T(8,128)S(1)}, f32[8,64,1,130]{3,1,2,0:T(8,128)S(1)}, u32[]{:S(2)}, u32[]{:S(2)}) collective-permute-start(f32[8,64,1,130]{3,1,2,0:T(8,128)S(1)} %copy.121), channel_id=1, source_target_pairs={{0,1},{1,2},{2,3},{3,4},{4,5},{5,6},{6,7},{7,8},{8,9},{9,10},{10,1... | collective-permute-start | bytes 798728 | tf_op jit(solution)/shard_map/ppermute | solution.py:23
  254.7 12.8 %collective-permute-start.11 = (f32[8,64,1,130]{3,1,2,0:T(8,128)S(1)}, f32[8,64,1,130]{3,1,2,0:T(8,128)S(1)}, u32[]{:S(2)}, u32[]{:S(2)}) collective-permute-start(f32[8,64,1,130]{3,1,2,0:T(8,128)S(1)} %copy.123), channel_id=1, source_target_pairs={{1,0},{2,1},{3,2},{4,3},{5,4},{6,5},{7,6},{8,7},{9,8},{10,9},{11,1... | collective-permute-start | bytes 798728 | tf_op jit(solution)/shard_map/ppermute | solution.py:24
  284.3 12.5 %copy-start.1 = (f32[8,64,8,128]{1,2,3,0:T(8,128)}, f32[8,64,8,128]{1,2,3,0:T(8,128)S(1)}, u32[]{:S(2)}) copy-start(f32[8,64,8,128]{1,2,3,0:T(8,128)S(1)} %fusion.25) | copy-start | bytes 6291460
  284.4 12.4 %collective-permute-start.12 = (f32[8,64,8,1]{1,2,3,0:T(8,128)S(1)}, f32[8,64,8,1]{1,2,3,0:T(8,128)S(1)}, u32[]{:S(2)}, u32[]{:S(2)}) collective-permute-start(f32[8,64,8,1]{1,2,3,0:T(8,128)S(1)} %get-tuple-element.61), channel_id=1, source_target_pairs={{0,16},{16,32},{32,48},{48,64},{64,80},{80,96},{96,112},{1,17},{17... | collective-permute-start | bytes 49160 | tf_op jit(solution)/shard_map/ppermute | solution.py:23
  290.3 6.5 %collective-permute-start.13 = (f32[8,64,8,1]{1,2,3,0:T(8,128)S(1)}, f32[8,64,8,1]{1,2,3,0:T(8,128)S(1)}, u32[]{:S(2)}, u32[]{:S(2)}) collective-permute-start(f32[8,64,8,1]{1,2,3,0:T(8,128)S(1)} %get-tuple-element.62), channel_id=1, source_target_pairs={{16,0},{32,16},{48,32},{64,48},{80,64},{96,80},{112,96},{17,1},{33... | collective-permute-start | bytes 49160 | tf_op jit(solution)/shard_map/ppermute | solution.py:24
  298.1 13.9 %collective-permute-start.14 = (f32[8,64,1,130]{3,1,2,0:T(8,128)S(1)}, f32[8,64,1,130]{3,1,2,0:T(8,128)S(1)}, u32[]{:S(2)}, u32[]{:S(2)}) collective-permute-start(f32[8,64,1,130]{3,1,2,0:T(8,128)S(1)} %copy.125), channel_id=1, source_target_pairs={{0,1},{1,2},{2,3},{3,4},{4,5},{5,6},{6,7},{7,8},{8,9},{9,10},{10,1... | collective-permute-start | bytes 798728 | tf_op jit(solution)/shard_map/ppermute | solution.py:23
  302.6 12.8 %collective-permute-start.15 = (f32[8,64,1,130]{3,1,2,0:T(8,128)S(1)}, f32[8,64,1,130]{3,1,2,0:T(8,128)S(1)}, u32[]{:S(2)}, u32[]{:S(2)}) collective-permute-start(f32[8,64,1,130]{3,1,2,0:T(8,128)S(1)} %copy.127), channel_id=1, source_target_pairs={{1,0},{2,1},{3,2},{4,3},{5,4},{6,5},{7,6},{8,7},{9,8},{10,9},{11,1... | collective-permute-start | bytes 798728 | tf_op jit(solution)/shard_map/ppermute | solution.py:24
  359.2 14.7 %copy-start.19 = (s32[256,1]{0,1:T(1,128)S(1)}, s32[256,1]{0,1:T(1,128)}, u32[]{:S(2)}) copy-start(s32[256,1]{0,1:T(1,128)} %copy-done.18) | copy-start | bytes 3076
  359.2 14.7 %copy-start.21 = (s32[256]{0:T(256)S(1)}, s32[256]{0:T(256)}, u32[]{:S(2)}) copy-start(s32[256]{0:T(256)} %param.17) | copy-start | bytes 3076
  362.6 30.0 %all-to-all-start.2 = ((f32[128,10,128]{2,1,0:T(8,128)}), f32[128,10,128]{2,1,0:T(8,128)S(1)}, u32[]{:S(2)}, u32[]{:S(2)}) async-start(f32[128,10,128]{2,1,0:T(8,128)} %reshape.202), calls=%async_computation.2 | async-start | bytes 2097152 | tf_op jit(solution)/shard_map/all_to_all | solution.py:127
  373.9 20.3 %copy-start.17 = (f32[256]{0:T(256)S(1)}, f32[256]{0:T(256)}, u32[]{:S(2)}) copy-start(f32[256]{0:T(256)} %get-tuple-element.83) | copy-start | bytes 3076
  373.9 20.3 %copy-start.16 = (f32[6,256]{1,0:T(8,128)S(1)}, f32[6,256]{1,0:T(8,128)}, u32[]{:S(2)}) copy-start(f32[6,256]{1,0:T(8,128)} %param.18) | copy-start | bytes 18436
  373.9 20.7 %copy-start.5 = (f32[8,128,128]{2,1,0:T(8,128)S(1)}, f32[8,128,128]{2,1,0:T(8,128)}, u32[]{:S(2)}) copy-start(f32[8,128,128]{2,1,0:T(8,128)} %param.16) | copy-start | bytes 1572868
  (9 other events, 26.4 us)
where the time goes:
time: 416 us; the launch traced here: 407 us
  other arithmetic  151 us (36%)
  local copies, waits for them, and re-layouts  111 us (27%)
  starting transfers between devices  80.1 us (19%)
  waiting for transfers between devices  51.9 us (12%)
  matrix products  11.2 us (3%)
    scatter-add x8, other arithmetic, body(): summed = summed.at[cell_table[:, foot_id]].add(recv_flux)  73.5 us
    add x4, other arithmetic, stencil(): return center - upwind + kappa_rate * spread + vertical_rate * vertical  64.7 us
    ppermute x8, starting transfers between devices, with_halo(): before = lax.ppermute(last, axis, up)  39.3 us
    slice x4, local copies, waits for them, and re-layouts, stencil(): center[..., :-1, :, :]  31.5 us
    gather x8, local copies, waits for them, and re-layouts, body(): air_total = air_total + cell_rows[cell_table[:, foot_id]]  23.6 us
    slice x4, local copies, waits for them, and re-layouts, stencil(): center[..., :1, :, :]  21.7 us
    all_to_all x1, waiting for transfers between devices, body(): lax.all_to_all(outgoing.reshape(device_count, capacity, width), ('gx', 'g...  14.8 us
    ppermute x8, waiting for transfers between devices, with_halo(): after = lax.ppermute(leading, axis, down)  13.9 us
  transfers between devices with their start and end apart: 19, of which 9 were waited for; matrix products, arithmetic and copies ran while one was open for 18% of the time, Pallas kernels for 0%

commit v1 on v0

v1 whole, which is shorter than its diff:
```python
import functools

import jax
import jax.numpy as jnp
from jax import lax
from jax.experimental import pallas as pl
from jax.experimental.pallas import tpu as pltpu
from jax.sharding import PartitionSpec as P

PKG = 8
SUB = 4
HALO = 4
CAP = 10
FOOT = 8
DEV = 128
LEV = 64
NB = 256
ROWS_Y = 8
LANES = 128
FLUX_ROWS = 6
STRIP = 8
AUX = 2 + FOOT
EARLY = 1

source_rate = 0.1
kappa_rate = 0.05
vertical_rate = 0.05
wall_gain = 0.5

f32 = jnp.float32
bf16 = jnp.bfloat16
VMEM = 32 * 1024 * 1024
NT = (((1,), (1,)), ((), ()))
NN = (((1,), (0,)), ((), ()))


def params(**kw):
    return pltpu.CompilerParams(vmem_limit_bytes=VMEM, **kw)


def whole(shape):
    return pl.BlockSpec(shape, lambda *_: (0,) * len(shape))


def halves(x):
    hi = x.astype(bf16)
    lo = (x - hi.astype(f32)).astype(bf16)
    return hi, lo


def mm(a, b, dims):
    return lax.dot_general(a, b, dims, preferred_element_type=f32)


def payload_kernel(anchor, foot, coeff, walls, facade, out, code_out, aux):
    owner = lax.broadcasted_iota(jnp.int32, (DEV, NB), 0) == anchor[...]
    earlier = lax.broadcasted_iota(jnp.int32, (NB, NB), 0) < lax.broadcasted_iota(
        jnp.int32, (NB, NB), 1
    )
    rank = mm(jnp.where(owner, 1.0, 0.0).astype(bf16), jnp.where(earlier, 1.0, 0.0).astype(bf16), NN)
    code = jnp.where(owner, rank, -1.0)
    code_out[...] = code
    heat = jnp.sum(coeff[...] * walls[:, 0, :], axis=0, keepdims=True)
    coupling = jnp.sum(coeff[...], axis=0, keepdims=True)
    cells = foot[...].astype(f32)
    picks = [jnp.where(code == float(r), 1.0, 0.0).astype(bf16) for r in range(CAP)]
    hi, lo = halves(facade[...])
    zero = jnp.zeros((LEV, NB), bf16)
    even = jnp.concatenate([picks[2 * p] for p in range(CAP // 2)], axis=0)
    odd = jnp.concatenate([picks[2 * p + 1] for p in range(CAP // 2)], axis=0)
    rows = (
        mm(even, jnp.concatenate([hi, zero], axis=0), NT)
        + mm(odd, jnp.concatenate([zero, hi], axis=0), NT)
        + mm(even, jnp.concatenate([lo, zero], axis=0), NT)
        + mm(odd, jnp.concatenate([zero, lo], axis=0), NT)
    )
    for p in range(CAP // 2):
        out[pl.ds(p, DEV, stride=FLUX_ROWS), :] = rows[p * DEV : (p + 1) * DEV]
    aux[...] = jnp.zeros_like(aux)
    for r in range(CAP):
        aux[r, AUX * r : AUX * r + 1, :] = heat
        aux[r, AUX * r + 1 : AUX * r + 2, :] = coupling
        aux[r, AUX * r + 2 : AUX * r + AUX, :] = cells
    total = jnp.zeros((DEV, LANES), f32)
    for r in range(CAP):
        hi, lo = halves(aux[r])
        total = total + mm(picks[r], hi, NT) + mm(picks[r], lo, NT)
    out[pl.ds(CAP // 2, DEV, stride=FLUX_ROWS), :] = total


def payload(anchor, foot, coeff, walls, facade):
    return pl.pallas_call(
        payload_kernel,
        grid=(1,),
        in_specs=[
            whole((1, NB)),
            whole((FOOT, NB)),
            whole((6, NB)),
            pl.BlockSpec((6, 8, NB), lambda _: (0, 0, 0)),
            whole((LEV, NB)),
        ],
        out_specs=[whole((DEV * FLUX_ROWS, LANES)), whole((DEV, NB))],
        out_shape=[
            jax.ShapeDtypeStruct((DEV * FLUX_ROWS, LANES), f32),
            jax.ShapeDtypeStruct((DEV, NB), f32),
        ],
        scratch_shapes=[pltpu.VMEM((CAP, LANES, NB), f32)],
        compiler_params=params(),
        name="payload",
    )(anchor, foot, coeff, walls, facade)


def lane_slot():
    return lax.broadcasted_iota(jnp.int32, (8, LANES), 1)


def pack_row(blocks):
    lane = lane_slot()
    slot = lane % 16
    out = jnp.zeros((8, LANES), f32)
    for i, block in enumerate(blocks):
        here = lane // 16 == i
        west = here & (slot >= 4) & (slot < 8)
        east = here & (slot >= 8) & (slot < 12)
        out = jnp.where(west, pltpu.roll(block, (16 * i + 4) % LANES, 1), out)
        out = jnp.where(east, pltpu.roll(block, (16 * i + 12) % LANES, 1), out)
    return out


def emit_row(y, field, low, high, pack):
    dst = low if y < HALO else high
    dst[0, y % HALO, :, :] = field
    pack[0, y] = pack_row([field[8 * i : 8 * i + 8] for i in range(8)])


def prep_kernel(canopy, low, high, pack):
    for y in range(ROWS_Y):
        emit_row(y, canopy[0, pl.ds(y, LEV, stride=ROWS_Y), :], low, high, pack)


def half_spec():
    return pl.BlockSpec((1, HALO, LEV, LANES), lambda i: (i, 0, 0, 0))


def pack_spec():
    return pl.BlockSpec((1, ROWS_Y, STRIP, LANES), lambda i: (i, 0, 0, 0))


def half_shape(n):
    return jax.ShapeDtypeStruct((n, HALO, LEV + STRIP, LANES), f32)


def pack_shape(n):
    return jax.ShapeDtypeStruct((n, ROWS_Y, STRIP, LANES), f32)


def prep(canopy, first, n):
    return pl.pallas_call(
        prep_kernel,
        grid=(n,),
        in_specs=[pl.BlockSpec((1, LEV * ROWS_Y, LANES), lambda i: (i + first, 0, 0))],
        out_specs=[half_spec(), half_spec(), pack_spec()],
        out_shape=[half_shape(n), half_shape(n), pack_shape(n)],
        compiler_params=params(),
        name="prep",
    )(canopy)


def scatter_kernel(recv, canopy, counts, low, high, pack, aux_s, xt):
    aux = recv[pl.ds(CAP // 2, DEV, stride=FLUX_ROWS), :]
    aux_s[...] = aux

    def group(g, carry):
        start = pl.multiple_of(g * 16, 16)
        mine = aux_s[pl.ds(start, 16), :]
        lane = lax.broadcasted_iota(jnp.int32, (16, LANES), 1).astype(f32)
        for r in range(CAP):
            cols = [
                jnp.broadcast_to(mine[:, AUX * r + 2 + f : AUX * r + 3 + f], (16, LANES)) - lane
                for f in range(FOOT)
            ]
            for y in range(ROWS_Y):
                n = jnp.zeros((16, LANES), f32)
                for c in cols:
                    n = n + jnp.where(c == float(y * LANES), 1.0, 0.0)
                counts[r, pl.ds(start, 16), y * LANES : (y + 1) * LANES] = n.astype(bf16)
        return carry

    lax.fori_loop(0, DEV // 16, group, 0)
    left = lax.broadcasted_iota(jnp.int32, (DEV, LANES), 1) < LEV
    for p in range(CAP // 2):
        rows = recv[pl.ds(p, DEV, stride=FLUX_ROWS), :]
        turned = pltpu.roll(rows, LEV, 1)
        for odd in range(2):
            r = 2 * p + odd
            area = jnp.where(left, turned, rows) if odd else jnp.where(left, rows, turned)
            factor = jnp.where(
                left,
                jnp.broadcast_to(aux[:, AUX * r : AUX * r + 1], (DEV, LANES)),
                jnp.broadcast_to(aux[:, AUX * r + 1 : AUX * r + 2], (DEV, LANES)),
            )
            hi, lo = halves((area * factor).T)
            xt[:DEV, r * DEV : (r + 1) * DEV] = hi
            xt[DEV:, r * DEV : (r + 1) * DEV] = lo
    table = counts[...].reshape(CAP * DEV, ROWS_Y * LANES)
    both = mm(xt[...], table, NN)
    sums = both[:DEV] + both[DEV:]
    for y in range(ROWS_Y):
        c = canopy[0, pl.ds(y, LEV, stride=ROWS_Y), :]
        p = sums[:LEV, y * LANES : (y + 1) * LANES]
        q = sums[LEV:, y * LANES : (y + 1) * LANES]
        emit_row(y, c + (source_rate / FOOT) * (p - q * c), low, high, pack)


def scatter(recv, canopy):
    return pl.pallas_call(
        scatter_kernel,
        grid=(1,),
        in_specs=[
            whole((DEV * FLUX_ROWS, LANES)),
            pl.BlockSpec((1, LEV * ROWS_Y, LANES), lambda i: (0, 0, 0)),
        ],
        out_specs=[whole((CAP, DEV, ROWS_Y * LANES)), half_spec(), half_spec(), pack_spec()],
        out_shape=[
            jax.ShapeDtypeStruct((CAP, DEV, ROWS_Y * LANES), bf16),
            half_shape(1),
            half_shape(1),
            pack_shape(1),
        ],
        scratch_shapes=[pltpu.VMEM((DEV, LANES), f32), pltpu.VMEM((2 * DEV, CAP * DEV), bf16)],
        compiler_params=params(),
        name="scatter",
    )(recv, canopy)


def merge_kernel(pack, west, east, low_in, high_in, low, high):
    slot = lane_slot() % 16
    for y in range(ROWS_Y):
        strip = jnp.where(
            slot < 4,
            pltpu.roll(west[0, y], LANES - 8, 1),
            jnp.where(slot < 12, pack[0, y], pltpu.roll(east[0, y], 8, 1)),
        )
        dst = low if y < HALO else high
        dst[0, y % HALO] = strip


def merge(pack, west, east, low, high):
    n = pack.shape[0]
    strip_spec = pl.BlockSpec((1, HALO, STRIP, LANES), lambda i: (i, 0, LEV // STRIP, 0))
    anywhere = pl.BlockSpec(memory_space=pl.ANY)
    return pl.pallas_call(
        merge_kernel,
        grid=(n,),
        in_specs=[pack_spec(), pack_spec(), pack_spec(), anywhere, anywhere],
        out_specs=[strip_spec, strip_spec],
        out_shape=[half_shape(n), half_shape(n)],
        input_output_aliases={3: 0, 4: 1},
        compiler_params=params(),
        name="merge",
    )(pack, west, east, low, high)


def exchange(low, high, pack):
    def shifts(axis):
        up = [(i, i + 1) for i in range(lax.axis_size(axis) - 1)]
        return up, [(j, i) for i, j in up]

    up, down = shifts("gx")
    west, east = lax.ppermute(pack, "gx", up), lax.ppermute(pack, "gx", down)
    low, high = merge(pack, west, east, low, high)
    up, down = shifts("gy")
    south, north = lax.ppermute(high, "gy", up), lax.ppermute(low, "gy", down)
    return south, low, high, north


def substeps(parts, coef, coef_strip, edge, buf, strips, put):
    lane = lane_slot()
    sub = lax.broadcasted_iota(jnp.int32, (8, LANES), 0)
    slot = lane % 16
    first, last = lane == 0, lane == LANES - 1
    inside = jnp.where(slot < 4, edge[2], jnp.where(slot < 12, 1.0, edge[3]))
    total = ROWS_Y + 2 * HALO

    def keep(row, value):
        if row < HALO:
            return value * edge[0]
        if row >= HALO + ROWS_Y:
            return value * edge[1]
        return value

    for step in range(1, SUB + 1):
        old, new = (step + 1) % 2, step % 2

        def main(row, start):
            if step == 1:
                return parts[row // HALO][0, row % HALO, start : start + 8, :]
            return buf[old, row, start : start + 8, :]

        def strip(row):
            if step == 1:
                return parts[row // HALO][0, row % HALO, LEV : LEV + STRIP, :]
            return strips[old, row]

        rows = range(step, total - step)
        for i in range(8):
            at = 8 * i
            c0, cw, ce, cs, cn = (coef[k, at : at + 8, :] for k in range(5))
            here, after = main(step - 1, at), main(step, at)
            for row in rows:
                before, here, after = here, after, main(row + 1, at)
                if i == 0:
                    below = jnp.where(sub == 0, here, pltpu.roll(here, 1, 0))
                else:
                    below = main(row, at - 1)
                if i == 7:
                    above = jnp.where(sub == 7, here, pltpu.roll(here, 7, 0))
                else:
                    above = main(row, at + 1)
                side = strip(row)
                left = jnp.where(first, pltpu.roll(side, (LANES - 16 * i - 3) % LANES, 1), pltpu.roll(here, 1, 1))
                right = jnp.where(
                    last,
                    pltpu.roll(side, (LANES - 1 - 16 * i - 12) % LANES, 1),
                    pltpu.roll(here, LANES - 1, 1),
                )
                value = (
                    (c0 * here + cw * left)
                    + (ce * right + cs * before)
                    + (cn * after + vertical_rate * (above + below))
                )
                if step == SUB:
                    put(row - HALO, at, value)
                else:
                    buf[new, row, at : at + 8, :] = keep(row, value)
        if step == SUB:
            break
        c0, cw, ce, cs, cn = (coef_strip[k] for k in range(5))
        here, after = strip(step - 1), strip(step)
        for row in rows:
            before, here, after = here, after, strip(row + 1)
            down = pltpu.roll(here, 1, 0)
            below = jnp.where(sub == 0, jnp.where(lane < 16, here, pltpu.roll(down, 16, 1)), down)
            lift = pltpu.roll(here, 7, 0)
            above = jnp.where(sub == 7, jnp.where(lane >= LANES - 16, here, pltpu.roll(lift, LANES - 16, 1)), lift)
            value = (
                (c0 * here + cw * pltpu.roll(here, 1, 1))
                + (ce * pltpu.roll(here, LANES - 1, 1) + cs * before)
                + (cn * after + vertical_rate * (above + below))
            )
            strips[new, row] = keep(row, value * inside)


def quarter_spec(first):
    return pl.BlockSpec((1, HALO, LEV + STRIP, LANES), lambda i: (i + first, 0, 0, 0))


STENCIL_SCRATCH = [
    (2, ROWS_Y + 2 * HALO, LEV, LANES),
    (2, ROWS_Y + 2 * HALO, STRIP, LANES),
]


def coef_specs():
    return [
        whole((5, LEV, LANES)),
        whole((5, STRIP, LANES)),
        pl.BlockSpec(memory_space=pltpu.SMEM),
    ]


def fields_kernel(*refs):
    south, low, high, north, coef, coef_strip, edge = refs[:7]
    out, buf, strips = refs[-3:]

    def put(y, at, value):
        out[0, pl.ds(at * ROWS_Y + y, 8, stride=ROWS_Y), :] = value

    substeps((south, low, high, north), coef, coef_strip, edge, buf, strips, put)


def fields(parts, coefs, first, n, into=None):
    operands = [*parts, *coefs]
    specs = [quarter_spec(first) for _ in parts] + coef_specs()
    alias = {}
    if into is not None:
        alias = {len(operands): 0}
        operands.append(into)
        specs.append(pl.BlockSpec(memory_space=pl.ANY))
    return pl.pallas_call(
        fields_kernel,
        grid=(n,),
        in_specs=specs,
        out_specs=pl.BlockSpec((1, LEV * ROWS_Y, LANES), lambda i: (i + first + 1, 0, 0)),
        out_shape=jax.ShapeDtypeStruct((8, LEV * ROWS_Y, LANES), f32),
        scratch_shapes=[pltpu.VMEM(s, f32) for s in STENCIL_SCRATCH],
        input_output_aliases=alias,
        compiler_params=params(),
        name="fields",
    )(*operands)


def gather_kernel(south, low, high, north, coef, coef_strip, edge, counts, humid, out, back, buf, strips, table):
    def put(y, at, value):
        out[0, pl.ds(at * ROWS_Y + y, 8, stride=ROWS_Y), :] = value

    substeps((south, low, high, north), coef, coef_strip, edge, buf, strips, put)
    for y in range(ROWS_Y):
        cols = slice(y * LANES, (y + 1) * LANES)
        for k, src in enumerate((out, humid)):
            hi, lo = halves(src[0, pl.ds(y, LEV, stride=ROWS_Y), :] * (1.0 / FOOT))
            table[k * LEV : (k + 1) * LEV, cols] = hi
            table[2 * LEV + k * LEV : 2 * LEV + (k + 1) * LEV, cols] = lo
    for r in range(CAP):
        both = mm(counts[r], table[...], NT)
        back[pl.ds(r, DEV, stride=CAP), :] = both[:, : 2 * LEV] + both[:, 2 * LEV :]


def gather(parts, coefs, counts, into):
    field_block = (1, LEV * ROWS_Y, LANES)
    return pl.pallas_call(
        gather_kernel,
        grid=(1,),
        in_specs=[quarter_spec(0) for _ in parts]
        + coef_specs()
        + [whole((CAP, DEV, ROWS_Y * LANES)), pl.BlockSpec(field_block, lambda i: (1, 0, 0))],
        out_specs=[pl.BlockSpec(field_block, lambda i: (0, 0, 0)), whole((DEV * CAP, LANES))],
        out_shape=[
            jax.ShapeDtypeStruct((8, LEV * ROWS_Y, LANES), f32),
            jax.ShapeDtypeStruct((DEV * CAP, LANES), f32),
        ],
        scratch_shapes=[pltpu.VMEM(s, f32) for s in STENCIL_SCRATCH]
        + [pltpu.VMEM((4 * LEV, ROWS_Y * LANES), bf16)],
        input_output_aliases={8: 0},
        compiler_params=params(),
        name="gather",
    )(*parts, *coefs, counts, into)


def walls_kernel(inverses, walls, package, out, column, a, b_hi, b_lo):
    n = walls.shape[1]

    @pl.when(pl.program_id(0) == 0)
    def _():
        chosen = jnp.zeros((n, NB), f32)
        for p in range(PKG):
            inv = inverses[p]
            hi, lo = halves(inv)
            a[:n, p * n : (p + 1) * n] = hi
            a[n:, p * n : (p + 1) * n] = lo
            chosen = jnp.where(package[...] == p, jnp.broadcast_to(inv[:, 0:1], (n, NB)), chosen)
        column[...] = chosen

    w = walls[0]
    w_hi = w.astype(bf16).astype(f32)
    w_lo = w - w_hi
    for p in range(PKG):
        mine = package[...] == p
        b_hi[p * n : (p + 1) * n, :] = jnp.where(mine, w_hi, 0.0).astype(bf16)
        b_lo[p * n : (p + 1) * n, :] = jnp.where(mine, w_lo, 0.0).astype(bf16)
    both = mm(a[...], b_hi[...], NN)
    out[0] = both[:n] + both[n:] + mm(a[:n, :], b_lo[...], NN)


def walls_product(inverses, walls, package):
    s, n, _ = walls.shape
    return pl.pallas_call(
        walls_kernel,
        grid=(s,),
        in_specs=[
            whole((PKG, n, n)),
            pl.BlockSpec((1, n, NB), lambda i: (i, 0, 0)),
            whole((1, NB)),
        ],
        out_specs=[pl.BlockSpec((1, n, NB), lambda i: (i, 0, 0)), whole((n, NB))],
        out_shape=[jax.ShapeDtypeStruct((s, n, NB), f32), jax.ShapeDtypeStruct((n, NB), f32)],
        scratch_shapes=[
            pltpu.VMEM((2 * n, PKG * n), bf16),
            pltpu.VMEM((PKG * n, NB), bf16),
            pltpu.VMEM((PKG * n, NB), bf16),
        ],
        compiler_params=params(),
        name="walls",
    )(inverses, walls, package)


def final_kernel(recv, code, facade, coeff, walls, product, column, air_out, walls_out, xt):
    picks = []
    for r in range(CAP):
        hi, lo = halves(recv[pl.ds(r, DEV, stride=CAP), :].T)
        xt[:LANES, r * DEV : (r + 1) * DEV] = hi
        xt[LANES:, r * DEV : (r + 1) * DEV] = lo
        picks.append(jnp.where(code[...] == float(r), 1.0, 0.0).astype(bf16))
    both = mm(xt[...], jnp.concatenate(picks, axis=0), NN)
    air = both[:LANES] + both[LANES:]
    air_out[...] = air
    area = facade[...]
    temp = jnp.sum(area * air[:LEV], axis=0, keepdims=True) / jnp.sum(area, axis=0, keepdims=True)
    for s in range(walls_out.shape[0]):
        source = wall_gain * coeff[s : s + 1, :] * (temp - walls[s, 0:1, :])
        walls_out[s] = product[s] + column[...] * source


def final(recv, code, facade, coeff, walls, product, column):
    s, n, _ = walls.shape
    return pl.pallas_call(
        final_kernel,
        grid=(1,),
        in_specs=[
            whole((DEV * CAP, LANES)),
            whole((DEV, NB)),
            whole((LEV, NB)),
            whole((s, NB)),
            pl.BlockSpec((s, 8, NB), lambda _: (0, 0, 0)),
            whole((s, n, NB)),
            whole((n, NB)),
        ],
        out_specs=[whole((2 * LEV, NB)), whole((s, n, NB))],
        out_shape=[
            jax.ShapeDtypeStruct((2 * LEV, NB), f32),
            jax.ShapeDtypeStruct((s, n, NB), f32),
        ],
        scratch_shapes=[pltpu.VMEM((2 * LANES, CAP * DEV), bf16)],
        compiler_params=params(),
        name="final",
    )(recv, code, facade, coeff, walls, product, column)


def transpose_all(x, rows):
    y = lax.all_to_all(
        x.reshape(DEV, 1, rows * LANES), ("gx", "gy"), split_axis=0, concat_axis=0, tiled=True
    )
    return y.reshape(DEV * rows, LANES)


def coefficients(courant):
    cx, cy = courant[0], courant[1]
    c = jnp.stack(
        [
            1.0 - jnp.abs(cx) - jnp.abs(cy) - 4.0 * kappa_rate - 2.0 * vertical_rate,
            jnp.maximum(cx, 0.0) + kappa_rate,
            kappa_rate - jnp.minimum(cx, 0.0),
            jnp.maximum(cy, 0.0) + kappa_rate,
            kappa_rate - jnp.minimum(cy, 0.0),
        ]
    )
    main = jnp.broadcast_to(c[:, :, None], (5, LEV, LANES))
    strip = jnp.broadcast_to(c.reshape(5, 8, 8).transpose(0, 2, 1)[..., None], (5, 8, 8, 16))
    gx, gy = lax.axis_index("gx"), lax.axis_index("gy")
    edge = jnp.stack(
        [gy > 0, gy < lax.axis_size("gy") - 1, gx > 0, gx < lax.axis_size("gx") - 1]
    ).astype(f32)
    return main, strip.reshape(5, STRIP, LANES), edge


def body(canopy, courant, walls, inverses, package, surf_coeff, facade_area, anchor, footprint):
    shape = canopy.shape
    canopy = canopy.reshape(shape[0], LEV * ROWS_Y, LANES)
    send, code = payload(anchor.T, footprint.T, surf_coeff, walls, facade_area)
    recv = transpose_all(send, FLUX_ROWS)
    coefs = coefficients(courant)
    rest = exchange(*prep(canopy, 1, shape[0] - 1))
    out = fields(rest, coefs, 0, EARLY)
    product, column = walls_product(inverses, walls, package[None, :])
    counts, low, high, pack = scatter(recv, canopy)
    zeroth = exchange(low, high, pack)
    out, back = gather(zeroth, coefs, counts, out)
    returned = transpose_all(back, CAP)
    if EARLY < shape[0] - 1:
        out = fields(rest, coefs, EARLY, shape[0] - 1 - EARLY, out)
    air, walls_out = final(returned, code, facade_area, surf_coeff, walls, product, column)
    return out.reshape(shape), air.reshape(2, LEV, NB), walls_out


def solution(mesh):
    placed = (
        P(None, None, "gy", "gx"),
        P(),
        P(None, None, ("gx", "gy")),
        P(),
        P(("gx", "gy")),
        P(None, ("gx", "gy")),
        P(None, ("gx", "gy")),
        P(("gx", "gy"), None),
        P(("gx", "gy"), None),
    )
    return jax.shard_map(
        body,
        mesh=mesh,
        in_specs=placed,
        out_specs=(
            P(None, None, "gy", "gx"),
            P(None, None, ("gx", "gy")),
            P(None, None, ("gx", "gy")),
        ),
        check_vma=False,
    )
```

time: 416 us -> 125 us (0.30); the launches traced: 407 us -> 124 us
  other arithmetic: 151 us -> 1.31 us
  local copies, waits for them, and re-layouts: 111 us -> 21.5 us
  starting transfers between devices: 80.1 us -> 39.4 us
  Pallas kernels: 0 us -> 35.9 us
  waiting for transfers between devices: 51.9 us -> 24.7 us
  matrix products: 11.2 us -> 0 us
    scatter-add x8 -> x0, other arithmetic: 73.5 us -> none  [body(): summed = summed.at[cell_table[:, foot_id]].add(recv_flux)]
    add x6 -> x0, other arithmetic: 65.7 us -> none  [the longest x4 64.7 us: stencil(): return center - upwind + kappa_rate * spread + vertical_rate * vertical]
    slice x23 -> x0, local copies, waits for them, and re-layouts: 58.1 us -> none  [the longest x4 31.5 us: stencil(): center[..., :-1, :, :]]
    pallas_call x0 -> x10, Pallas kernels: none -> 35.9 us  [the longest x2 16.2 us: fields(): pl.pallas_call(fields_kernel, grid=(n,), in_specs=specs, out_specs=pl.Blo...]
    ppermute x16 -> x8, starting transfers between devices: 53.2 us -> 21.6 us  [the longest x4 11.2 us: exchange(): west, east = (lax.ppermute(pack, 'gx', up), lax.ppermute(pack, 'gx', down))]
    gather x9 -> x0, local copies, waits for them, and re-layouts: 24.3 us -> none  [the longest x8 23.6 us: body(): air_total = air_total + cell_rows[cell_table[:, foot_id]]]
    all_to_all x3 -> x2, waiting for transfers between devices: 36.8 us -> 16.5 us  [transpose_all(): lax.all_to_all(x.reshape(DEV, 1, rows * LANES), ('gx', 'gy'), split_axis=...]
    dot_general x8 -> x0, matrix products: 11.2 us -> none  [select_walls(): jnp.einsum('nm,smb->snb', inverses[package_id], rhs_walls, precision=lax....]
  transfers between devices with their start and end apart: 19 -> 10, of which waited for: 9 -> 4; matrix products, arithmetic and copies ran while one was open for 18% -> 7% of each run, Pallas kernels for 0% -> 22%
where the time goes in v1:
time: 125 us; the launch traced here: 124 us
  starting transfers between devices  39.4 us (32%)
  Pallas kernels  35.9 us (29%)
  waiting for transfers between devices  24.7 us (20%)
  local copies, waits for them, and re-layouts  21.5 us (17%)
  other arithmetic  1.31 us (1%)
    all_to_all x2, starting transfers between devices, transpose_all(): lax.all_to_all(x.reshape(DEV, 1, rows * LANES), ('gx', 'gy'), split_axis=...  17.8 us
    unnamed x50, local copies, waits for them, and re-layouts  16.6 us
    all_to_all x2, waiting for transfers between devices, transpose_all(): lax.all_to_all(x.reshape(DEV, 1, rows * LANES), ('gx', 'gy'), split_axis=...  16.5 us
    pallas_call x2, Pallas kernels, fields(): pl.pallas_call(fields_kernel, grid=(n,), in_specs=specs, out_specs=pl.Blo...  16.2 us
    ppermute x4, starting transfers between devices, exchange(): west, east = (lax.ppermute(pack, 'gx', up), lax.ppermute(pack, 'gx', down))  11.2 us
    ppermute x4, starting transfers between devices, exchange(): south, north = (lax.ppermute(high, 'gy', up), lax.ppermute(low, 'gy', down))  10.3 us
    ppermute x4, waiting for transfers between devices, exchange(): west, east = (lax.ppermute(pack, 'gx', up), lax.ppermute(pack, 'gx', down))  8.25 us
    pallas_call x1, Pallas kernels, scatter(): pl.pallas_call(scatter_kernel, grid=(1,), in_specs=[whole((DEV * FLUX_ROW...  7.11 us
  transfers between devices with their start and end apart: 10, of which 4 were waited for; matrix products, arithmetic and copies ran while one was open for 7% of the time, Pallas kernels for 22%

profile of v1, /device:TPU:1, one launch (start us, length us, event | category | flops | bytes accessed | tf_op | source)
XLA Modules:
  0.0 123.7 jit_solution(15363398938588919304)
XLA Ops:
  0.6 1.6 %copy-done = f32[8,64,8,128]{3,2,1,0:T(8,128)S(1)} copy-done((f32[8,64,8,128]{3,2,1,0:T(8,128)S(1)}, f32[8,64,8,128]{3,2,1,0:T(8,128)}, u32[]{:S(2)}) %copy-start) | copy-done | bytes 2097176
  2.2 1.6 %prep.1 = (f32[7,4,72,128]{3,2,1,0:T(8,128)S(1)}, f32[7,4,72,128]{3,2,1,0:T(8,128)S(1)}, f32[7,8,8,128]{3,2,1,0:T(8,128)S(1)}) custom-call(f32[8,512,128]{2,1,0:T(8,128)S(1)} %bitcast.17), custom_call_target="tpu_custom_call" | custom-call | tf_op jit(solution)/shard_map/prep/pallas_call | solution.py:158
  3.9 4.9 %collective-permute-start = (f32[7,8,8,128]{3,2,1,0:T(8,128)S(1)}, f32[7,8,8,128]{3,2,1,0:T(8,128)S(1)}, u32[]{:S(2)}, u32[]{:S(2)}) collective-permute-start(f32[7,8,8,128]{3,2,1,0:T(8,128)S(1)} %get-tuple-element.22.pack), channel_id=1, source_target_pairs={{0,16},{16,32},{32,48},{48,64},{64,80},{80,96},{96,112},{1,17},{17... | collective-permute-start | bytes 688136 | tf_op jit(solution)/shard_map/ppermute | solution.py:270
  8.8 1.9 %collective-permute-start.1 = (f32[7,8,8,128]{3,2,1,0:T(8,128)S(1)}, f32[7,8,8,128]{3,2,1,0:T(8,128)S(1)}, u32[]{:S(2)}, u32[]{:S(2)}) collective-permute-start(f32[7,8,8,128]{3,2,1,0:T(8,128)S(1)} %get-tuple-element.22.pack), channel_id=1, source_target_pairs={{16,0},{32,16},{48,32},{64,48},{80,64},{96,80},{112,96},{17,1},{33... | collective-permute-start | bytes 688136 | tf_op jit(solution)/shard_map/ppermute | solution.py:270
  10.7 1.0 collective-permute-done.west
  11.7 4.4 %collective-permute-done.1.east = f32[7,8,8,128]{3,2,1,0:T(8,128)S(1)} collective-permute-done((f32[7,8,8,128]{3,2,1,0:T(8,128)S(1)}, f32[7,8,8,128]{3,2,1,0:T(8,128)S(1)}, u32[]{:S(2)}, u32[]{:S(2)}) %collective-permute-start.1) | collective-permute-done | bytes 229408 | tf_op jit(solution)/shard_map/ppermute | solution.py:270
  16.8 4.1 %collective-permute-start.2 = (f32[7,4,72,128]{3,2,1,0:T(8,128)S(1)}, f32[7,4,72,128]{3,2,1,0:T(8,128)}, u32[]{:S(2)}, u32[]{:S(2)}) collective-permute-start(f32[7,4,72,128]{3,2,1,0:T(8,128)S(1)} %get-tuple-element.25.refs_2_), channel_id=1, source_target_pairs={{0,1},{1,2},{2,3},{3,4},{4,5},{5,6},{6,7},{7,8},{8,9},{9,10},{10,1... | collective-permute-start | bytes 3096584 | tf_op jit(solution)/shard_map/ppermute | solution.py:273
  20.9 1.3 %collective-permute-start.3 = (f32[7,4,72,128]{3,2,1,0:T(8,128)S(1)}, f32[7,4,72,128]{3,2,1,0:T(8,128)}, u32[]{:S(2)}, u32[]{:S(2)}) collective-permute-start(f32[7,4,72,128]{3,2,1,0:T(8,128)S(1)} %get-tuple-element.26.refs_1_), channel_id=1, source_target_pairs={{1,0},{2,1},{3,2},{4,3},{5,4},{6,5},{7,6},{8,7},{9,8},{10,9},{11,1... | collective-permute-start | bytes 3096584 | tf_op jit(solution)/shard_map/ppermute | solution.py:273
  22.3 1.0 payload.1
  24.7 10.0 %all-to-all-start = ((f32[128,1,768]{2,1,0:T(1,128)}), f32[128,1,768]{2,1,0:T(1,128)S(1)}, u32[]{:S(2)}, u32[]{:S(2)}) async-start(f32[128,1,768]{2,1,0:T(1,128)} %bitcast.22), calls=%async_computation | async-start | bytes 786432 | tf_op jit(solution)/shard_map/all_to_all | solution.py:530
  35.3 1.2 fusion.3
  38.6 16.5 %all-to-all-done = f32[128,1,768]{2,1,0:T(1,128)S(1)} async-done(((f32[128,1,768]{2,1,0:T(1,128)}), f32[128,1,768]{2,1,0:T(1,128)S(1)}, u32[]{:S(2)}, u32[]{:S(2)}) %all-to-all-start) | async-done | bytes 393248 | tf_op jit(solution)/shard_map/all_to_all | solution.py:530
  55.1 1.6 %copy-done.1 = f32[8,64,8,128]{3,2,1,0:T(8,128)S(1)} copy-done((f32[8,64,8,128]{3,2,1,0:T(8,128)S(1)}, f32[8,64,8,128]{3,2,1,0:T(8,128)}, u32[]{:S(2)}) %copy-start.1) | copy-done | bytes 2097176
  56.7 7.1 %scatter.1 = (bf16[10,128,1024]{2,1,0:T(8,128)(2,1)S(1)}, f32[1,4,72,128]{3,2,1,0:T(8,128)S(1)}, f32[1,4,72,128]{3,2,1,0:T(8,128)S(1)}, f32[1,8,8,128]{3,2,1,0:T(8,128)}) custom-call(f32[768,128]{1,0:T(8,128)S(1)} %bitcast.20, f32[8,512,128]{2,1,0:T(8,128)S(1)} %bitcast.18), custom_call_target="tpu_custom_call" | custom-call | tf_op jit(solution)/shard_map/scatter/pallas_call | solution.py:216
  63.8 1.5 %copy-done.3 = bf16[10,128,1024]{2,1,0:T(8,128)(2,1)} copy-done((bf16[10,128,1024]{2,1,0:T(8,128)(2,1)}, bf16[10,128,1024]{2,1,0:T(8,128)(2,1)S(1)}, u32[]{:S(2)}) %copy-start.3) | copy-done | bytes 2621464
  65.3 2.4 %collective-permute-start.4 = (f32[1,8,8,128]{3,2,1,0:T(8,128)}, f32[1,8,8,128]{3,2,1,0:T(8,128)S(1)}, u32[]{:S(2)}, u32[]{:S(2)}) collective-permute-start(f32[1,8,8,128]{3,2,1,0:T(8,128)} %get-tuple-element.28.pack), channel_id=1, source_target_pairs={{0,16},{16,32},{32,48},{48,64},{64,80},{80,96},{96,112},{1,17},{17... | collective-permute-start | bytes 98312 | tf_op jit(solution)/shard_map/ppermute | solution.py:270
  67.7 1.9 %collective-permute-start.5 = (f32[1,8,8,128]{3,2,1,0:T(8,128)}, f32[1,8,8,128]{3,2,1,0:T(8,128)S(1)}, u32[]{:S(2)}, u32[]{:S(2)}) collective-permute-start(f32[1,8,8,128]{3,2,1,0:T(8,128)} %get-tuple-element.28.pack), channel_id=1, source_target_pairs={{16,0},{32,16},{48,32},{64,48},{80,64},{96,80},{112,96},{17,1},{33... | collective-permute-start | bytes 98312 | tf_op jit(solution)/shard_map/ppermute | solution.py:270
  70.3 2.8 %collective-permute-done.5.east = f32[1,8,8,128]{3,2,1,0:T(8,128)S(1)} collective-permute-done((f32[1,8,8,128]{3,2,1,0:T(8,128)}, f32[1,8,8,128]{3,2,1,0:T(8,128)S(1)}, u32[]{:S(2)}, u32[]{:S(2)}) %collective-permute-start.5) | collective-permute-done | bytes 32800 | tf_op jit(solution)/shard_map/ppermute | solution.py:270
  74.0 3.7 %collective-permute-start.6 = (f32[1,4,72,128]{3,2,1,0:T(8,128)S(1)}, f32[1,4,72,128]{3,2,1,0:T(8,128)S(1)}, u32[]{:S(2)}, u32[]{:S(2)}) collective-permute-start(f32[1,4,72,128]{3,2,1,0:T(8,128)S(1)} %get-tuple-element.31.high), channel_id=1, source_target_pairs={{0,1},{1,2},{2,3},{3,4},{4,5},{5,6},{6,7},{7,8},{8,9},{9,10},{10,1... | collective-permute-start | bytes 442376 | tf_op jit(solution)/shard_map/ppermute | solution.py:273
  77.7 1.3 %collective-permute-start.7 = (f32[1,4,72,128]{3,2,1,0:T(8,128)S(1)}, f32[1,4,72,128]{3,2,1,0:T(8,128)S(1)}, u32[]{:S(2)}, u32[]{:S(2)}) collective-permute-start(f32[1,4,72,128]{3,2,1,0:T(8,128)S(1)} %get-tuple-element.32.low), channel_id=1, source_target_pairs={{1,0},{2,1},{3,2},{4,3},{5,4},{6,5},{7,6},{8,7},{9,8},{10,9},{11,1... | collective-permute-start | bytes 442376 | tf_op jit(solution)/shard_map/ppermute | solution.py:273
  81.2 1.0 reshape.39.refs_5_.coef_strip
  83.1 3.6 %fields.2.humid = f32[8,512,128]{2,1,0:T(8,128)} custom-call(f32[7,4,72,128]{3,2,1,0:T(8,128)} %collective-permute-done.2.refs_0_, f32[7,4,72,128]{3,2,1,0:T(8,128)S(1)} %get-tuple-element.26.refs_1_, f32[7,4,72,128]{3,2,1,0:T(8,128)S(1)} %get-tuple-element.25.refs_2_, f32[7,4,72,128]{3,2,1,0:T(8,128)} %collective-permute-done.3.refs_3_, ...), custom_call_target="tpu_custom_call" | custom-call | tf_op jit(solution)/shard_map/fields/pallas_call | solution.py:390
  86.8 4.4 %gather.1 = (f32[8,512,128]{2,1,0:T(8,128)}, f32[1280,128]{1,0:T(8,128)S(1)}) custom-call(f32[1,4,72,128]{3,2,1,0:T(8,128)S(1)} %collective-permute-done.6.south, f32[1,4,72,128]{3,2,1,0:T(8,128)S(1)} %get-tuple-element.32.low, f32[1,4,72,128]{3,2,1,0:T(8,128)S(1)} %get-tuple-element.31.high, ...), custom_call_target="tpu_custom_call", output_to_operand_aliasing={{0}: (8, {})} | custom-call | tf_op jit(solution)/shard_map/gather/pallas_call | solution.py:421
  92.0 7.8 %all-to-all-start.1 = ((f32[128,1,1280]{2,1,0:T(1,128)}), f32[128,1,1280]{2,1,0:T(1,128)S(1)}, u32[]{:S(2)}, u32[]{:S(2)}) async-start(f32[128,1,1280]{2,1,0:T(1,128)} %bitcast.21), calls=%async_computation.1 | async-start | bytes 1310720 | tf_op jit(solution)/shard_map/all_to_all | solution.py:530
  99.8 1.0 copy-done.10
  100.9 2.6 %walls.5 = (f32[6,128,256]{2,1,0:T(8,128)S(1)}, f32[128,256]{1,0:T(8,128)S(1)}) custom-call(f32[8,128,128]{2,1,0:T(8,128)S(1)} %copy-done.10, f32[6,128,256]{2,1,0:T(8,128)S(1)} %copy-done.2, s32[1,256]{1,0:T(1,128)S(1)} %bitcast.25), custom_call_target="tpu_custom_call" | custom-call | tf_op jit(solution)/shard_map/walls/pallas_call | solution.py:467
  105.0 0.9 copy-done.6
  105.9 12.6 %fields.3 = f32[8,512,128]{2,1,0:T(8,128)} custom-call(f32[7,4,72,128]{3,2,1,0:T(8,128)} %collective-permute-done.2.refs_0_, f32[7,4,72,128]{3,2,1,0:T(8,128)S(1)} %get-tuple-element.26.refs_1_, f32[7,4,72,128]{3,2,1,0:T(8,128)S(1)} %get-tuple-element.25.refs_2_, f32[7,4,72,128]{3,2,1,0:T(8,128)} %collective-permute-done.3.refs_3_, ...), custom_call_target="tpu_custom_call", output_to_operand_aliasing={{}: (7, {})} | custom-call | tf_op jit(solution)/shard_map/fields/pallas_call | solution.py:390
  118.5 1.1 copy-done.8
  120.4 0.9 copy-done.15
  121.3 0.9 copy-done.17
  122.2 1.5 %final.1 = (f32[128,256]{1,0:T(8,128)}, f32[6,128,256]{2,1,0:T(8,128)}) custom-call(f32[1280,128]{1,0:T(8,128)S(1)} %bitcast.19, f32[128,256]{1,0:T(8,128)S(1)} %copy-done.15, f32[64,256]{1,0:T(8,128)S(1)} %copy-done.13, f32[6,256]{1,0:T(8,128)S(1)} %copy-done.18, f32[6,128,256]{2,1,0:T(8,128)S(1)} %copy-done.2, f32[6,128,256]{2,1,0:T(8,128)S(1)} %copy-done.8, ...), custom_call_target="tpu_custom_call" | custom-call | tf_op jit(solution)/shard_map/final/pallas_call | solution.py:506
  (62 shorter events, 12.5 us)
Async XLA Ops:
  0.6 1.6 %copy-start = (f32[8,64,8,128]{3,2,1,0:T(8,128)S(1)}, f32[8,64,8,128]{3,2,1,0:T(8,128)}, u32[]{:S(2)}) copy-start(f32[8,64,8,128]{3,2,1,0:T(8,128)} %param.9) | copy-start | bytes 6291460
  2.2 20.0 %copy-start.2 = (f32[6,128,256]{2,1,0:T(8,128)S(1)}, f32[6,128,256]{2,1,0:T(8,128)}, u32[]{:S(2)}) copy-start(f32[6,128,256]{2,1,0:T(8,128)} %walls.7) | copy-start | bytes 2359300
  2.2 20.0 %copy-start.12 = (f32[64,256]{1,0:T(8,128)S(1)}, f32[64,256]{1,0:T(8,128)}, u32[]{:S(2)}) copy-start(f32[64,256]{1,0:T(8,128)} %facade.3) | copy-start | bytes 196612
  2.2 20.0 %copy-start.18 = (f32[6,256]{1,0:T(8,128)S(1)}, f32[6,256]{1,0:T(8,128)}, u32[]{:S(2)}) copy-start(f32[6,256]{1,0:T(8,128)} %coeff.3) | copy-start | bytes 18436
  2.2 20.0 %copy-start.19 = (s32[256,8]{0,1:T(8,128)S(1)}, s32[256,8]{0,1:T(8,128)}, u32[]{:S(2)}) copy-start(s32[256,8]{0,1:T(8,128)} %param.17) | copy-start | bytes 24580
  2.2 20.0 %copy-start.20 = (s32[256,1]{0,1:T(1,128)S(1)}, s32[256,1]{0,1:T(1,128)}, u32[]{:S(2)}) copy-start(s32[256,1]{0,1:T(1,128)} %param.16) | copy-start | bytes 3076
  3.9 7.9 %collective-permute-start = (f32[7,8,8,128]{3,2,1,0:T(8,128)S(1)}, f32[7,8,8,128]{3,2,1,0:T(8,128)S(1)}, u32[]{:S(2)}, u32[]{:S(2)}) collective-permute-start(f32[7,8,8,128]{3,2,1,0:T(8,128)S(1)} %get-tuple-element.22.pack), channel_id=1, source_target_pairs={{0,16},{16,32},{32,48},{48,64},{64,80},{80,96},{96,112},{1,17},{17... | collective-permute-start | bytes 688136 | tf_op jit(solution)/shard_map/ppermute | solution.py:270
  8.8 7.3 %collective-permute-start.1 = (f32[7,8,8,128]{3,2,1,0:T(8,128)S(1)}, f32[7,8,8,128]{3,2,1,0:T(8,128)S(1)}, u32[]{:S(2)}, u32[]{:S(2)}) collective-permute-start(f32[7,8,8,128]{3,2,1,0:T(8,128)S(1)} %get-tuple-element.22.pack), channel_id=1, source_target_pairs={{16,0},{32,16},{48,32},{64,48},{80,64},{96,80},{112,96},{17,1},{33... | collective-permute-start | bytes 688136 | tf_op jit(solution)/shard_map/ppermute | solution.py:270
  16.1 19.1 %copy-start.22 = (f32[2,64]{1,0:T(2,128)S(1)}, f32[2,64]{1,0:T(2,128)}, u32[]{:S(2)}) copy-start(f32[2,64]{1,0:T(2,128)} %param.10) | copy-start | bytes 1540
  16.8 66.1 %collective-permute-start.2 = (f32[7,4,72,128]{3,2,1,0:T(8,128)S(1)}, f32[7,4,72,128]{3,2,1,0:T(8,128)}, u32[]{:S(2)}, u32[]{:S(2)}) collective-permute-start(f32[7,4,72,128]{3,2,1,0:T(8,128)S(1)} %get-tuple-element.25.refs_2_), channel_id=1, source_target_pairs={{0,1},{1,2},{2,3},{3,4},{4,5},{5,6},{6,7},{7,8},{8,9},{9,10},{10,1... | collective-permute-start | bytes 3096584 | tf_op jit(solution)/shard_map/ppermute | solution.py:273
  20.9 62.1 %collective-permute-start.3 = (f32[7,4,72,128]{3,2,1,0:T(8,128)S(1)}, f32[7,4,72,128]{3,2,1,0:T(8,128)}, u32[]{:S(2)}, u32[]{:S(2)}) collective-permute-start(f32[7,4,72,128]{3,2,1,0:T(8,128)S(1)} %get-tuple-element.26.refs_1_), channel_id=1, source_target_pairs={{1,0},{2,1},{3,2},{4,3},{5,4},{6,5},{7,6},{8,7},{9,8},{10,9},{11,1... | collective-permute-start | bytes 3096584 | tf_op jit(solution)/shard_map/ppermute | solution.py:273
  23.3 0.7 copy-start.11
  24.0 0.7 copy-start.14
  24.7 30.4 %all-to-all-start = ((f32[128,1,768]{2,1,0:T(1,128)}), f32[128,1,768]{2,1,0:T(1,128)S(1)}, u32[]{:S(2)}, u32[]{:S(2)}) async-start(f32[128,1,768]{2,1,0:T(1,128)} %bitcast.22), calls=%async_computation | async-start | bytes 786432 | tf_op jit(solution)/shard_map/all_to_all | solution.py:530
  55.1 1.6 %copy-start.1 = (f32[8,64,8,128]{3,2,1,0:T(8,128)S(1)}, f32[8,64,8,128]{3,2,1,0:T(8,128)}, u32[]{:S(2)}) copy-start(f32[8,64,8,128]{3,2,1,0:T(8,128)} %param.9) | copy-start | bytes 6291460
  63.8 1.5 %copy-start.3 = (bf16[10,128,1024]{2,1,0:T(8,128)(2,1)}, bf16[10,128,1024]{2,1,0:T(8,128)(2,1)S(1)}, u32[]{:S(2)}) copy-start(bf16[10,128,1024]{2,1,0:T(8,128)(2,1)S(1)} %get-tuple-element.33.counts) | copy-start | bytes 7864324
  65.3 5.1 %collective-permute-start.4 = (f32[1,8,8,128]{3,2,1,0:T(8,128)}, f32[1,8,8,128]{3,2,1,0:T(8,128)S(1)}, u32[]{:S(2)}, u32[]{:S(2)}) collective-permute-start(f32[1,8,8,128]{3,2,1,0:T(8,128)} %get-tuple-element.28.pack), channel_id=1, source_target_pairs={{0,16},{16,32},{32,48},{48,64},{64,80},{80,96},{96,112},{1,17},{17... | collective-permute-start | bytes 98312 | tf_op jit(solution)/shard_map/ppermute | solution.py:270
  67.7 5.4 %collective-permute-start.5 = (f32[1,8,8,128]{3,2,1,0:T(8,128)}, f32[1,8,8,128]{3,2,1,0:T(8,128)S(1)}, u32[]{:S(2)}, u32[]{:S(2)}) collective-permute-start(f32[1,8,8,128]{3,2,1,0:T(8,128)} %get-tuple-element.28.pack), channel_id=1, source_target_pairs={{16,0},{32,16},{48,32},{64,48},{80,64},{96,80},{112,96},{17,1},{33... | collective-permute-start | bytes 98312 | tf_op jit(solution)/shard_map/ppermute | solution.py:270
  74.0 12.7 %collective-permute-start.6 = (f32[1,4,72,128]{3,2,1,0:T(8,128)S(1)}, f32[1,4,72,128]{3,2,1,0:T(8,128)S(1)}, u32[]{:S(2)}, u32[]{:S(2)}) collective-permute-start(f32[1,4,72,128]{3,2,1,0:T(8,128)S(1)} %get-tuple-element.31.high), channel_id=1, source_target_pairs={{0,1},{1,2},{2,3},{3,4},{4,5},{5,6},{6,7},{7,8},{8,9},{9,10},{10,1... | collective-permute-start | bytes 442376 | tf_op jit(solution)/shard_map/ppermute | solution.py:273
  77.7 9.0 %collective-permute-start.7 = (f32[1,4,72,128]{3,2,1,0:T(8,128)S(1)}, f32[1,4,72,128]{3,2,1,0:T(8,128)S(1)}, u32[]{:S(2)}, u32[]{:S(2)}) collective-permute-start(f32[1,4,72,128]{3,2,1,0:T(8,128)S(1)} %get-tuple-element.32.low), channel_id=1, source_target_pairs={{1,0},{2,1},{3,2},{4,3},{5,4},{6,5},{7,6},{8,7},{9,8},{10,9},{11,1... | collective-permute-start | bytes 442376 | tf_op jit(solution)/shard_map/ppermute | solution.py:273
  83.1 3.7 %copy-start.5 = (f32[5,64,128]{2,1,0:T(8,128)}, f32[5,64,128]{2,1,0:T(8,128)S(1)}, u32[]{:S(2)}) copy-start(f32[5,64,128]{2,1,0:T(8,128)S(1)} %broadcast_in_dim.6.refs_4_.coef) | copy-start | bytes 491524
  83.1 3.6 %copy-start.4 = (bf16[10,128,1024]{2,1,0:T(8,128)(2,1)S(1)}, bf16[10,128,1024]{2,1,0:T(8,128)(2,1)}, u32[]{:S(2)}) copy-start(bf16[10,128,1024]{2,1,0:T(8,128)(2,1)} %copy-done.3) | copy-start | bytes 7864324
  86.8 13.1 %copy-start.21 = (s32[256]{0:T(256)S(1)}, s32[256]{0:T(256)}, u32[]{:S(2)}) copy-start(s32[256]{0:T(256)} %param.13) | copy-start | bytes 3076
  91.2 0.8 copy-start.9
  92.0 26.5 %all-to-all-start.1 = ((f32[128,1,1280]{2,1,0:T(1,128)}), f32[128,1,1280]{2,1,0:T(1,128)S(1)}, u32[]{:S(2)}, u32[]{:S(2)}) async-start(f32[128,1,1280]{2,1,0:T(1,128)} %bitcast.21), calls=%async_computation.1 | async-start | bytes 1310720 | tf_op jit(solution)/shard_map/all_to_all | solution.py:530
  99.8 1.0 copy-start.10
  103.4 0.9 copy-start.7
  105.0 0.9 copy-start.6
  118.5 1.1 copy-start.8
  119.6 0.8 copy-start.13
  120.4 0.9 copy-start.15
  121.3 0.9 copy-start.17
  (1 other events, 0.6 us)

commit v2 on v1

--- a/solution.py
+++ b/solution.py
@@ -29,7 +29,7 @@
 
 f32 = jnp.float32
 bf16 = jnp.bfloat16
-VMEM = 32 * 1024 * 1024
+VMEM = 16 * 1024 * 1024
 NT = (((1,), (1,)), ((), ()))
 NN = (((1,), (0,)), ((), ()))
 
@@ -101,8 +101,8 @@
         ],
         out_specs=[whole((DEV * FLUX_ROWS, LANES)), whole((DEV, NB))],
         out_shape=[
-            jax.ShapeDtypeStruct((DEV * FLUX_ROWS, LANES), f32),
-            jax.ShapeDtypeStruct((DEV, NB), f32),
+            pltpu.HBM((DEV * FLUX_ROWS, LANES), f32),
+            pltpu.HBM((DEV, NB), f32),
         ],
         scratch_shapes=[pltpu.VMEM((CAP, LANES, NB), f32)],
         compiler_params=params(),
@@ -133,10 +133,35 @@
     pack[0, y] = pack_row([field[8 * i : 8 * i + 8] for i in range(8)])
 
 
-def prep_kernel(canopy, low, high, pack):
+def prep_kernel(courant, canopy, low, high, pack, coef, coef_strip):
     for y in range(ROWS_Y):
         emit_row(y, canopy[0, pl.ds(y, LEV, stride=ROWS_Y), :], low, high, pack)
 
+    @pl.when(pl.program_id(0) == 0)
+    def _():
+        square = (LEV, LEV)
+        diagonal = lax.broadcasted_iota(jnp.int32, square, 0) == lax.broadcasted_iota(jnp.int32, square, 1)
+
+        def column(row):
+            picked = jnp.where(diagonal, jnp.broadcast_to(courant[row : row + 1, :], square), 0.0)
+            return jnp.broadcast_to(jnp.sum(picked, axis=1, keepdims=True), (LEV, LANES))
+
+        cx, cy = column(0), column(1)
+        values = (
+            1.0 - jnp.abs(cx) - jnp.abs(cy) - (4.0 * kappa_rate + 2.0 * vertical_rate),
+            jnp.maximum(cx, 0.0) + kappa_rate,
+            kappa_rate - jnp.minimum(cx, 0.0),
+            jnp.maximum(cy, 0.0) + kappa_rate,
+            kappa_rate - jnp.minimum(cy, 0.0),
+        )
+        block = lane_slot() // 16
+        for k, v in enumerate(values):
+            coef[k] = v
+            strip = v[0:8]
+            for i in range(1, 8):
+                strip = jnp.where(block == i, v[8 * i : 8 * i + 8], strip)
+            coef_strip[k] = strip
+
 
 def half_spec():
     return pl.BlockSpec((1, HALO, LEV, LANES), lambda i: (i, 0, 0, 0))
@@ -154,80 +179,98 @@
     return jax.ShapeDtypeStruct((n, ROWS_Y, STRIP, LANES), f32)
 
 
-def prep(canopy, first, n):
+def prep(courant, canopy, first, n):
     return pl.pallas_call(
         prep_kernel,
         grid=(n,),
-        in_specs=[pl.BlockSpec((1, LEV * ROWS_Y, LANES), lambda i: (i + first, 0, 0))],
-        out_specs=[half_spec(), half_spec(), pack_spec()],
-        out_shape=[half_shape(n), half_shape(n), pack_shape(n)],
+        in_specs=[
+            whole((2, LEV)),
+            pl.BlockSpec((1, LEV * ROWS_Y, LANES), lambda i: (i + first, 0, 0)),
+        ],
+        out_specs=[
+            half_spec(),
+            half_spec(),
+            pack_spec(),
+            whole((5, LEV, LANES)),
+            whole((5, STRIP, LANES)),
+        ],
+        out_shape=[
+            half_shape(n),
+            half_shape(n),
+            pack_shape(n),
+            jax.ShapeDtypeStruct((5, LEV, LANES), f32),
+            jax.ShapeDtypeStruct((5, STRIP, LANES), f32),
+        ],
         compiler_params=params(),
         name="prep",
-    )(canopy)
-
-
-def scatter_kernel(recv, canopy, counts, low, high, pack, aux_s, xt):
-    aux = recv[pl.ds(CAP // 2, DEV, stride=FLUX_ROWS), :]
-    aux_s[...] = aux
+    )(courant, canopy)
+
+
+def scatter_kernel(recv, canopy, counts_out, low, high, pack, counts, column_s, field_s, xt, field0, sems):
+    load = pltpu.make_async_copy(canopy.at[0], field0, sems.at[0])
+    load.start()
+    aux = recv[pl.ds(CAP // 2, DEV, stride=FLUX_ROWS), :].T
+    cell = aux.astype(jnp.int32)
+    column_s[...] = cell & (LANES - 1)
+    field_s[...] = lax.shift_left(jnp.ones_like(cell), lax.shift_right_logical(cell, jnp.full_like(cell, 5)) & 28)
 
     def group(g, carry):
         start = pl.multiple_of(g * 16, 16)
-        mine = aux_s[pl.ds(start, 16), :]
-        lane = lax.broadcasted_iota(jnp.int32, (16, LANES), 1).astype(f32)
+        x = lax.broadcasted_iota(jnp.int32, (16, LANES), 0) + start
         for r in range(CAP):
-            cols = [
-                jnp.broadcast_to(mine[:, AUX * r + 2 + f : AUX * r + 3 + f], (16, LANES)) - lane
-                for f in range(FOOT)
-            ]
+            packed = jnp.zeros((16, LANES), jnp.int32)
+            for k in range(AUX * r + 2, AUX * r + AUX):
+                here = jnp.broadcast_to(column_s[k : k + 1, :], (16, LANES)) == x
+                packed = packed + jnp.where(here, jnp.broadcast_to(field_s[k : k + 1, :], (16, LANES)), 0)
             for y in range(ROWS_Y):
-                n = jnp.zeros((16, LANES), f32)
-                for c in cols:
-                    n = n + jnp.where(c == float(y * LANES), 1.0, 0.0)
-                counts[r, pl.ds(start, 16), y * LANES : (y + 1) * LANES] = n.astype(bf16)
+                n = lax.shift_right_logical(packed, jnp.full_like(packed, 4 * y)) & 15
+                row = pl.multiple_of(y * LANES + start, 16)
+                counts[pl.ds(row, 16), r * DEV : (r + 1) * DEV] = n.astype(f32).astype(bf16)
         return carry
 
-    lax.fori_loop(0, DEV // 16, group, 0)
-    left = lax.broadcasted_iota(jnp.int32, (DEV, LANES), 1) < LEV
+    lax.fori_loop(0, LANES // 16, group, 0)
+    save = pltpu.make_async_copy(counts, counts_out, sems.at[1])
+    save.start()
     for p in range(CAP // 2):
-        rows = recv[pl.ds(p, DEV, stride=FLUX_ROWS), :]
-        turned = pltpu.roll(rows, LEV, 1)
+        rows = recv[pl.ds(p, DEV, stride=FLUX_ROWS), :].T
         for odd in range(2):
             r = 2 * p + odd
-            area = jnp.where(left, turned, rows) if odd else jnp.where(left, rows, turned)
-            factor = jnp.where(
-                left,
-                jnp.broadcast_to(aux[:, AUX * r : AUX * r + 1], (DEV, LANES)),
-                jnp.broadcast_to(aux[:, AUX * r + 1 : AUX * r + 2], (DEV, LANES)),
-            )
-            hi, lo = halves((area * factor).T)
-            xt[:DEV, r * DEV : (r + 1) * DEV] = hi
-            xt[DEV:, r * DEV : (r + 1) * DEV] = lo
-    table = counts[...].reshape(CAP * DEV, ROWS_Y * LANES)
-    both = mm(xt[...], table, NN)
+            area = rows[LEV * odd : LEV * (odd + 1)]
+            for q in range(2):
+                hi, lo = halves(area * aux[AUX * r + q : AUX * r + q + 1, :])
+                xt[q * LEV : (q + 1) * LEV, r * DEV : (r + 1) * DEV] = hi
+                xt[DEV + q * LEV : DEV + (q + 1) * LEV, r * DEV : (r + 1) * DEV] = lo
+    both = mm(xt[...], counts[...], NT)
     sums = both[:DEV] + both[DEV:]
+    load.wait()
     for y in range(ROWS_Y):
-        c = canopy[0, pl.ds(y, LEV, stride=ROWS_Y), :]
+        c = field0[pl.ds(y, LEV, stride=ROWS_Y), :]
         p = sums[:LEV, y * LANES : (y + 1) * LANES]
         q = sums[LEV:, y * LANES : (y + 1) * LANES]
         emit_row(y, c + (source_rate / FOOT) * (p - q * c), low, high, pack)
+    save.wait()
 
 
 def scatter(recv, canopy):
     return pl.pallas_call(
         scatter_kernel,
         grid=(1,),
-        in_specs=[
-            whole((DEV * FLUX_ROWS, LANES)),
-            pl.BlockSpec((1, LEV * ROWS_Y, LANES), lambda i: (0, 0, 0)),
-        ],
-        out_specs=[whole((CAP, DEV, ROWS_Y * LANES)), half_spec(), half_spec(), pack_spec()],
+        in_specs=[whole((DEV * FLUX_ROWS, LANES)), pl.BlockSpec(memory_space=pltpu.HBM)],
+        out_specs=[pl.BlockSpec(memory_space=pltpu.HBM), half_spec(), half_spec(), pack_spec()],
         out_shape=[
-            jax.ShapeDtypeStruct((CAP, DEV, ROWS_Y * LANES), bf16),
+            pltpu.HBM((ROWS_Y * LANES, CAP * DEV), bf16),
             half_shape(1),
             half_shape(1),
             pack_shape(1),
         ],
-        scratch_shapes=[pltpu.VMEM((DEV, LANES), f32), pltpu.VMEM((2 * DEV, CAP * DEV), bf16)],
+        scratch_shapes=[
+            pltpu.VMEM((ROWS_Y * LANES, CAP * DEV), bf16),
+            pltpu.VMEM((LANES, DEV), jnp.int32),
+            pltpu.VMEM((LANES, DEV), jnp.int32),
+            pltpu.VMEM((2 * DEV, CAP * DEV), bf16),
+            pltpu.VMEM((LEV * ROWS_Y, LANES), f32),
+            pltpu.SemaphoreType.DMA((2,)),
+        ],
         compiler_params=params(),
         name="scatter",
     )(recv, canopy)
@@ -261,20 +304,24 @@
     )(pack, west, east, low, high)
 
 
-def exchange(low, high, pack):
-    def shifts(axis):
-        up = [(i, i + 1) for i in range(lax.axis_size(axis) - 1)]
-        return up, [(j, i) for i, j in up]
-
+def shifts(axis):
+    up = [(i, i + 1) for i in range(lax.axis_size(axis) - 1)]
+    return up, [(j, i) for i, j in up]
+
+
+def across_x(low, high, pack):
     up, down = shifts("gx")
     west, east = lax.ppermute(pack, "gx", up), lax.ppermute(pack, "gx", down)
-    low, high = merge(pack, west, east, low, high)
+    return merge(pack, west, east, low, high)
+
+
+def across_y(low, high):
     up, down = shifts("gy")
     south, north = lax.ppermute(high, "gy", up), lax.ppermute(low, "gy", down)
     return south, low, high, north
 
 
-def substeps(parts, coef, coef_strip, edge, buf, strips, put):
+def substeps(parts, coef, coef_strip, edge, buf, strips, ends, put):
     lane = lane_slot()
     sub = lax.broadcasted_iota(jnp.int32, (8, LANES), 0)
     slot = lane % 16
@@ -303,6 +350,9 @@
             return strips[old, row]
 
         rows = range(step, total - step)
+        for row in rows:
+            side = strip(row)
+            ends[row] = jnp.where(slot == 3, side, pltpu.roll(side, LANES - 10, 1))
         for i in range(8):
             at = 8 * i
             c0, cw, ce, cs, cn = (coef[k, at : at + 8, :] for k in range(5))
@@ -312,18 +362,14 @@
                 if i == 0:
                     below = jnp.where(sub == 0, here, pltpu.roll(here, 1, 0))
                 else:
-                    below = main(row, at - 1)
+                    below = pltpu.roll(jnp.where(sub == 7, main(row, at - 8), here), 1, 0)
                 if i == 7:
                     above = jnp.where(sub == 7, here, pltpu.roll(here, 7, 0))
                 else:
-                    above = main(row, at + 1)
-                side = strip(row)
-                left = jnp.where(first, pltpu.roll(side, (LANES - 16 * i - 3) % LANES, 1), pltpu.roll(here, 1, 1))
-                right = jnp.where(
-                    last,
-                    pltpu.roll(side, (LANES - 1 - 16 * i - 12) % LANES, 1),
-                    pltpu.roll(here, LANES - 1, 1),
-                )
+                    above = pltpu.roll(jnp.where(sub == 0, main(row, at + 8), here), 7, 0)
+                side = pltpu.roll(ends[row], (LANES - 16 * i - 3) % LANES, 1)
+                left = jnp.where(first, side, pltpu.roll(here, 1, 1))
+                right = jnp.where(last, side, pltpu.roll(here, LANES - 1, 1))
                 value = (
                     (c0 * here + cw * left)
                     + (ce * right + cs * before)
@@ -358,6 +404,7 @@
 STENCIL_SCRATCH = [
     (2, ROWS_Y + 2 * HALO, LEV, LANES),
     (2, ROWS_Y + 2 * HALO, STRIP, LANES),
+    (ROWS_Y + 2 * HALO, STRIP, LANES),
 ]
 
 
@@ -371,12 +418,12 @@
 
 def fields_kernel(*refs):
     south, low, high, north, coef, coef_strip, edge = refs[:7]
-    out, buf, strips = refs[-3:]
+    out, buf, strips, ends = refs[-4:]
 
     def put(y, at, value):
         out[0, pl.ds(at * ROWS_Y + y, 8, stride=ROWS_Y), :] = value
 
-    substeps((south, low, high, north), coef, coef_strip, edge, buf, strips, put)
+    substeps((south, low, high, north), coef, coef_strip, edge, buf, strips, ends, put)
 
 
 def fields(parts, coefs, first, n, into=None):
@@ -392,7 +439,7 @@
         grid=(n,),
         in_specs=specs,
         out_specs=pl.BlockSpec((1, LEV * ROWS_Y, LANES), lambda i: (i + first + 1, 0, 0)),
-        out_shape=jax.ShapeDtypeStruct((8, LEV * ROWS_Y, LANES), f32),
+        out_shape=pltpu.HBM((8, LEV * ROWS_Y, LANES), f32),
         scratch_shapes=[pltpu.VMEM(s, f32) for s in STENCIL_SCRATCH],
         input_output_aliases=alias,
         compiler_params=params(),
@@ -400,37 +447,53 @@
     )(*operands)
 
 
-def gather_kernel(south, low, high, north, coef, coef_strip, edge, counts, humid, out, back, buf, strips, table):
+def gather_kernel(
+    south, low, high, north, coef, coef_strip, edge, counts_in, fields_in, out, back, *scratch
+):
+    buf, strips, ends, table, counts, humid, sems = scratch
+    fetch = pltpu.make_async_copy(counts_in, counts, sems.at[0])
+    fetch.start()
+    other = pltpu.make_async_copy(fields_in.at[1], humid, sems.at[1])
+    other.start()
+
     def put(y, at, value):
         out[0, pl.ds(at * ROWS_Y + y, 8, stride=ROWS_Y), :] = value
 
-    substeps((south, low, high, north), coef, coef_strip, edge, buf, strips, put)
+    substeps((south, low, high, north), coef, coef_strip, edge, buf, strips, ends, put)
+    other.wait()
     for y in range(ROWS_Y):
         cols = slice(y * LANES, (y + 1) * LANES)
-        for k, src in enumerate((out, humid)):
-            hi, lo = halves(src[0, pl.ds(y, LEV, stride=ROWS_Y), :] * (1.0 / FOOT))
+        pick = pl.ds(y, LEV, stride=ROWS_Y)
+        for k, field in enumerate((out[0, pick, :], humid[pick, :])):
+            hi, lo = halves(field * (1.0 / FOOT))
             table[k * LEV : (k + 1) * LEV, cols] = hi
             table[2 * LEV + k * LEV : 2 * LEV + (k + 1) * LEV, cols] = lo
+    fetch.wait()
+    both = mm(table[...], counts[...], NN)
+    sums = both[: 2 * LEV] + both[2 * LEV :]
     for r in range(CAP):
-        both = mm(counts[r], table[...], NT)
-        back[pl.ds(r, DEV, stride=CAP), :] = both[:, : 2 * LEV] + both[:, 2 * LEV :]
+        back[pl.ds(r, DEV, stride=CAP), :] = sums[:, r * DEV : (r + 1) * DEV].T
 
 
 def gather(parts, coefs, counts, into):
     field_block = (1, LEV * ROWS_Y, LANES)
+    remote = pl.BlockSpec(memory_space=pltpu.HBM)
     return pl.pallas_call(
         gather_kernel,
         grid=(1,),
-        in_specs=[quarter_spec(0) for _ in parts]
-        + coef_specs()
-        + [whole((CAP, DEV, ROWS_Y * LANES)), pl.BlockSpec(field_block, lambda i: (1, 0, 0))],
+        in_specs=[quarter_spec(0) for _ in parts] + coef_specs() + [remote, remote],
         out_specs=[pl.BlockSpec(field_block, lambda i: (0, 0, 0)), whole((DEV * CAP, LANES))],
         out_shape=[
-            jax.ShapeDtypeStruct((8, LEV * ROWS_Y, LANES), f32),
-            jax.ShapeDtypeStruct((DEV * CAP, LANES), f32),
+            pltpu.HBM((8, LEV * ROWS_Y, LANES), f32),
+            pltpu.HBM((DEV * CAP, LANES), f32),
         ],
         scratch_shapes=[pltpu.VMEM(s, f32) for s in STENCIL_SCRATCH]
-        + [pltpu.VMEM((4 * LEV, ROWS_Y * LANES), bf16)],
+        + [
+            pltpu.VMEM((4 * LEV, ROWS_Y * LANES), bf16),
+            pltpu.VMEM((ROWS_Y * LANES, CAP * DEV), bf16),
+            pltpu.VMEM((LEV * ROWS_Y, LANES), f32),
+            pltpu.SemaphoreType.DMA((2,)),
+        ],
         input_output_aliases={8: 0},
         compiler_params=params(),
         name="gather",
@@ -473,7 +536,7 @@
             whole((1, NB)),
         ],
         out_specs=[pl.BlockSpec((1, n, NB), lambda i: (i, 0, 0)), whole((n, NB))],
-        out_shape=[jax.ShapeDtypeStruct((s, n, NB), f32), jax.ShapeDtypeStruct((n, NB), f32)],
+        out_shape=[pltpu.HBM((s, n, NB), f32), pltpu.HBM((n, NB), f32)],
         scratch_shapes=[
             pltpu.VMEM((2 * n, PKG * n), bf16),
             pltpu.VMEM((PKG * n, NB), bf16),
@@ -484,7 +547,15 @@
     )(inverses, walls, package)
 
 
-def final_kernel(recv, code, facade, coeff, walls, product, column, air_out, walls_out, xt):
+def final_kernel(recv, code, facade, coeff, walls, product, column, air_out, walls_out, xt, value, col, first, sems):
+    surfaces = value.shape[0]
+    loads = [
+        pltpu.make_async_copy(product, value, sems.at[0]),
+        pltpu.make_async_copy(column, col, sems.at[1]),
+        pltpu.make_async_copy(walls.at[:, pl.ds(0, 8), :], first, sems.at[2]),
+    ]
+    for c in loads:
+        c.start()
     picks = []
     for r in range(CAP):
         hi, lo = halves(recv[pl.ds(r, DEV, stride=CAP), :].T)
@@ -496,13 +567,21 @@
     air_out[...] = air
     area = facade[...]
     temp = jnp.sum(area * air[:LEV], axis=0, keepdims=True) / jnp.sum(area, axis=0, keepdims=True)
-    for s in range(walls_out.shape[0]):
-        source = wall_gain * coeff[s : s + 1, :] * (temp - walls[s, 0:1, :])
-        walls_out[s] = product[s] + column[...] * source
+    for c in loads:
+        c.wait()
+    saves = []
+    for s in range(surfaces):
+        source = wall_gain * coeff[s : s + 1, :] * (temp - first[s, 0:1, :])
+        value[s] = value[s] + col[...] * source
+        saves.append(pltpu.make_async_copy(value.at[s], walls_out.at[s], sems.at[3 + s]))
+        saves[s].start()
+    for c in saves:
+        c.wait()
 
 
 def final(recv, code, facade, coeff, walls, product, column):
     s, n, _ = walls.shape
+    remote = pl.BlockSpec(memory_space=pltpu.HBM)
     return pl.pallas_call(
         final_kernel,
         grid=(1,),
@@ -511,16 +590,22 @@
             whole((DEV, NB)),
             whole((LEV, NB)),
             whole((s, NB)),
-            pl.BlockSpec((s, 8, NB), lambda _: (0, 0, 0)),
-            whole((s, n, NB)),
-            whole((n, NB)),
-        ],
-        out_specs=[whole((2 * LEV, NB)), whole((s, n, NB))],
+            remote,
+            remote,
+            remote,
+        ],
+        out_specs=[whole((2 * LEV, NB)), remote],
         out_shape=[
             jax.ShapeDtypeStruct((2 * LEV, NB), f32),
-            jax.ShapeDtypeStruct((s, n, NB), f32),
-        ],
-        scratch_shapes=[pltpu.VMEM((2 * LANES, CAP * DEV), bf16)],
+            pltpu.HBM((s, n, NB), f32),
+        ],
+        scratch_shapes=[
+            pltpu.VMEM((2 * LANES, CAP * DEV), bf16),
+            pltpu.VMEM((s, n, NB), f32),
+            pltpu.VMEM((n, NB), f32),
+            pltpu.VMEM((s, 8, NB), f32),
+            pltpu.SemaphoreType.DMA((3 + s,)),
+        ],
         compiler_params=params(),
         name="final",
     )(recv, code, facade, coeff, walls, product, column)
@@ -533,42 +618,39 @@
     return y.reshape(DEV * rows, LANES)
 
 
-def coefficients(courant):
-    cx, cy = courant[0], courant[1]
-    c = jnp.stack(
-        [
-            1.0 - jnp.abs(cx) - jnp.abs(cy) - 4.0 * kappa_rate - 2.0 * vertical_rate,
-            jnp.maximum(cx, 0.0) + kappa_rate,
-            kappa_rate - jnp.minimum(cx, 0.0),
-            jnp.maximum(cy, 0.0) + kappa_rate,
-            kappa_rate - jnp.minimum(cy, 0.0),
-        ]
-    )
-    main = jnp.broadcast_to(c[:, :, None], (5, LEV, LANES))
-    strip = jnp.broadcast_to(c.reshape(5, 8, 8).transpose(0, 2, 1)[..., None], (5, 8, 8, 16))
+def inside_edges():
     gx, gy = lax.axis_index("gx"), lax.axis_index("gy")
-    edge = jnp.stack(
-        [gy > 0, gy < lax.axis_size("gy") - 1, gx > 0, gx < lax.axis_size("gx") - 1]
-    ).astype(f32)
-    return main, strip.reshape(5, STRIP, LANES), edge
+    side = jnp.arange(4, dtype=jnp.int32)
+    place = jnp.where(side < 2, gy, gx)
+    limit = jnp.where(side < 2, lax.axis_size("gy") - 1, lax.axis_size("gx") - 1)
+    return jnp.where(side % 2 == 0, place > 0, place < limit).astype(f32)
+
+
+def hbm(x):
+    return pltpu.with_memory_space_constraint(x, pltpu.HBM)
 
 
 def body(canopy, courant, walls, inverses, package, surf_coeff, facade_area, anchor, footprint):
     shape = canopy.shape
     canopy = canopy.reshape(shape[0], LEV * ROWS_Y, LANES)
-    send, code = payload(anchor.T, footprint.T, surf_coeff, walls, facade_area)
+    edge = inside_edges()
+    send, code = payload(anchor.T, footprint.T, surf_coeff, hbm(walls), facade_area)
     recv = transpose_all(send, FLUX_ROWS)
-    coefs = coefficients(courant)
-    rest = exchange(*prep(canopy, 1, shape[0] - 1))
+    later, code = lax.optimization_barrier((canopy, code))
+    low, high, pack, coef, coef_strip = prep(courant, later, 1, shape[0] - 1)
+    coefs = (coef, coef_strip, edge)
+    low, high = across_x(low, high, pack)
+    recv, low, high = lax.optimization_barrier((recv, low, high))
+    rest = across_y(low, high)
     out = fields(rest, coefs, 0, EARLY)
     product, column = walls_product(inverses, walls, package[None, :])
-    counts, low, high, pack = scatter(recv, canopy)
-    zeroth = exchange(low, high, pack)
+    counts, low, high, pack = scatter(recv, hbm(canopy))
+    zeroth = across_y(*across_x(low, high, pack))
     out, back = gather(zeroth, coefs, counts, out)
     returned = transpose_all(back, CAP)
     if EARLY < shape[0] - 1:
         out = fields(rest, coefs, EARLY, shape[0] - 1 - EARLY, out)
-    air, walls_out = final(returned, code, facade_area, surf_coeff, walls, product, column)
+    air, walls_out = final(returned, code, facade_area, surf_coeff, hbm(walls), product, column)
     return out.reshape(shape), air.reshape(2, LEV, NB), walls_out
 
 

time: 125 us -> 109 us (0.87)
  local copies, waits for them, and re-layouts: 21.5 us -> 11.1 us
  waiting for transfers between devices: 24.7 us -> 14.6 us
  starting transfers between devices: 39.4 us -> 43.8 us
  Pallas kernels: 35.9 us -> 37.4 us
  other arithmetic: 1.31 us -> 0.01 us
    all_to_all x2, waiting for transfers between devices: 16.5 us -> 0.01 us  [transpose_all(): lax.all_to_all(x.reshape(DEV, 1, rows * LANES), ('gx', 'gy'), split_axis=...]
    ppermute x8, waiting for transfers between devices: 8.26 us -> 14.6 us  [the longest x4 8.73 us: across_x(): west, east = (lax.ppermute(pack, 'gx', up), lax.ppermute(pack, 'gx', down))]
    all_to_all x2, starting transfers between devices: 17.8 us -> 23.9 us  [transpose_all(): lax.all_to_all(x.reshape(DEV, 1, rows * LANES), ('gx', 'gy'), split_axis=...]
    unnamed x50 -> x40, local copies, waits for them, and re-layouts: 16.6 us -> 11.1 us
    pallas_call x1, Pallas kernels: 7.11 us -> 3.76 us  [scatter(): pl.pallas_call(scatter_kernel, grid=(1,), in_specs=[whole((DEV * FLUX_ROW...]
    another operation x7 -> x0, local copies, waits for them, and re-layouts: 1.68 us -> none  [coefficients(): jnp.stack([1.0 - jnp.abs(cx) - jnp.abs(cy) - 4.0 * kappa_rate - 2.0 * ver...]
    ppermute x8, starting transfers between devices: 21.6 us -> 19.9 us  [the longest x4 10 us: across_y(): south, north = (lax.ppermute(high, 'gy', up), lax.ppermute(low, 'gy', down))]
    pallas_call x1, Pallas kernels: 1 us -> 2.55 us  [payload(): pl.pallas_call(payload_kernel, grid=(1,), in_specs=[whole((1, NB)), whole...]
  transfers between devices with their start and end apart: 10 -> 10, of which waited for: 4 -> 5; matrix products, arithmetic and copies ran while one was open for 7% -> 0% of each run, Pallas kernels for 22% -> 24%
where the time goes in v2:
time: 109 us; the launch traced here: 108 us
  starting transfers between devices  43.8 us (40%)
  Pallas kernels  37.4 us (34%)
  waiting for transfers between devices  14.6 us (13%)
  local copies, waits for them, and re-layouts  11.1 us (10%)
    all_to_all x2, starting transfers between devices, transpose_all(): lax.all_to_all(x.reshape(DEV, 1, rows * LANES), ('gx', 'gy'), split_axis=...  23.9 us
    pallas_call x2, Pallas kernels, fields(): pl.pallas_call(fields_kernel, grid=(n,), in_specs=specs, out_specs=pl.Blo...  15.6 us
    unnamed x40, local copies, waits for them, and re-layouts  11.1 us
    ppermute x4, starting transfers between devices, across_y(): south, north = (lax.ppermute(high, 'gy', up), lax.ppermute(low, 'gy', down))  10 us
    ppermute x4, starting transfers between devices, across_x(): west, east = (lax.ppermute(pack, 'gx', up), lax.ppermute(pack, 'gx', down))  9.89 us
    ppermute x4, waiting for transfers between devices, across_x(): west, east = (lax.ppermute(pack, 'gx', up), lax.ppermute(pack, 'gx', down))  8.73 us
    ppermute x4, waiting for transfers between devices, across_y(): south, north = (lax.ppermute(high, 'gy', up), lax.ppermute(low, 'gy', down))  5.9 us
    pallas_call x1, Pallas kernels, gather(): pl.pallas_call(gather_kernel, grid=(1,), in_specs=[quarter_spec(0) for _...  5.81 us
  transfers between devices with their start and end apart: 10, of which 5 were waited for; matrix products, arithmetic and copies ran while one was open for 0% of the time, Pallas kernels for 24%

profile of v2, /device:TPU:1, one launch (start us, length us, event | category | flops | bytes accessed | tf_op | source)
XLA Modules:
  0.0 107.8 jit_solution(12851436368654520390)
XLA Ops:
  0.6 0.8 copy-done.10
  1.5 0.7 copy-done.14
  2.2 0.7 copy-done.16
  3.5 2.5 %payload.1 = (f32[768,128]{1,0:T(8,128)}, f32[128,256]{1,0:T(8,128)}) custom-call(s32[1,256]{1,0:T(1,128)S(1)} %bitcast.15, s32[8,256]{1,0:T(8,128)S(1)} %bitcast.14, f32[6,256]{1,0:T(8,128)S(1)} %copy-done.14, f32[6,128,256]{2,1,0:T(8,128)} %walls.7, f32[64,256]{1,0:T(8,128)S(1)} %copy-done.10), custom_call_target="tpu_custom_call" | custom-call | tf_op jit(solution)/shard_map/payload/pallas_call | solution.py:92
  6.1 11.5 %all-to-all-start = ((f32[128,1,768]{2,1,0:T(1,128)}), f32[128,1,768]{2,1,0:T(1,128)S(1)}, u32[]{:S(2)}, u32[]{:S(2)}) async-start(f32[128,1,768]{2,1,0:T(1,128)} %bitcast.19), calls=%async_computation | async-start | bytes 786432 | tf_op jit(solution)/shard_map/all_to_all | solution.py:615
  17.6 1.6 %copy-done = f32[8,64,8,128]{3,2,1,0:T(8,128)S(1)} copy-done((f32[8,64,8,128]{3,2,1,0:T(8,128)S(1)}, f32[8,64,8,128]{3,2,1,0:T(8,128)}, u32[]{:S(2)}) %copy-start) | copy-done | bytes 2097176
  19.9 1.7 %prep.1 = (f32[7,4,72,128]{3,2,1,0:T(8,128)S(1)}, f32[7,4,72,128]{3,2,1,0:T(8,128)S(1)}, f32[7,8,8,128]{3,2,1,0:T(8,128)S(1)}, f32[5,64,128]{2,1,0:T(8,128)S(1)}, f32[5,8,128]{2,1,0:T(8,128)S(1)}) custom-call(f32[2,64]{1,0:T(2,128)S(1)} %copy-done.18, f32[8,512,128]{2,1,0:T(8,128)S(1)} %bitcast.11), custom_call_target="tpu_custom_call" | custom-call | tf_op jit(solution)/shard_map/prep/pallas_call | solution.py:183
  22.3 3.6 %collective-permute-start = (f32[7,8,8,128]{3,2,1,0:T(8,128)S(1)}, f32[7,8,8,128]{3,2,1,0:T(8,128)S(1)}, u32[]{:S(2)}, u32[]{:S(2)}) collective-permute-start(f32[7,8,8,128]{3,2,1,0:T(8,128)S(1)} %get-tuple-element.32.pack), channel_id=1, source_target_pairs={{0,16},{16,32},{32,48},{48,64},{64,80},{80,96},{96,112},{1,17},{17... | collective-permute-start | bytes 688136 | tf_op jit(solution)/shard_map/ppermute | solution.py:314
  25.9 1.9 %collective-permute-start.1 = (f32[7,8,8,128]{3,2,1,0:T(8,128)S(1)}, f32[7,8,8,128]{3,2,1,0:T(8,128)S(1)}, u32[]{:S(2)}, u32[]{:S(2)}) collective-permute-start(f32[7,8,8,128]{3,2,1,0:T(8,128)S(1)} %get-tuple-element.32.pack), channel_id=1, source_target_pairs={{16,0},{32,16},{48,32},{64,48},{80,64},{96,80},{112,96},{17,1},{33... | collective-permute-start | bytes 688136 | tf_op jit(solution)/shard_map/ppermute | solution.py:314
  27.9 1.0 collective-permute-done.west
  28.9 4.4 %collective-permute-done.1.east = f32[7,8,8,128]{3,2,1,0:T(8,128)S(1)} collective-permute-done((f32[7,8,8,128]{3,2,1,0:T(8,128)S(1)}, f32[7,8,8,128]{3,2,1,0:T(8,128)S(1)}, u32[]{:S(2)}, u32[]{:S(2)}) %collective-permute-start.1) | collective-permute-done | bytes 229408 | tf_op jit(solution)/shard_map/ppermute | solution.py:314
  34.0 3.2 %collective-permute-start.2 = (f32[7,4,72,128]{3,2,1,0:T(8,128)S(1)}, f32[7,4,72,128]{3,2,1,0:T(8,128)S(1)}, u32[]{:S(2)}, u32[]{:S(2)}) collective-permute-start(f32[7,4,72,128]{3,2,1,0:T(8,128)S(1)} %get-tuple-element.37.refs_2_), channel_id=1, source_target_pairs={{0,1},{1,2},{2,3},{3,4},{4,5},{5,6},{6,7},{7,8},{8,9},{9,10},{10,1... | collective-permute-start | bytes 3096584 | tf_op jit(solution)/shard_map/ppermute | solution.py:320
  37.2 1.3 %collective-permute-start.3 = (f32[7,4,72,128]{3,2,1,0:T(8,128)S(1)}, f32[7,4,72,128]{3,2,1,0:T(8,128)}, u32[]{:S(2)}, u32[]{:S(2)}) collective-permute-start(f32[7,4,72,128]{3,2,1,0:T(8,128)S(1)} %get-tuple-element.38.refs_1_), channel_id=1, source_target_pairs={{1,0},{2,1},{3,2},{4,3},{5,4},{6,5},{7,6},{8,7},{9,8},{10,9},{11,1... | collective-permute-start | bytes 3096584 | tf_op jit(solution)/shard_map/ppermute | solution.py:320
  38.5 3.8 %scatter.1 = (bf16[1024,1280]{1,0:T(8,128)(2,1)}, f32[1,4,72,128]{3,2,1,0:T(8,128)}, f32[1,4,72,128]{3,2,1,0:T(8,128)}, f32[1,8,8,128]{3,2,1,0:T(8,128)S(1)}) custom-call(f32[768,128]{1,0:T(8,128)S(1)} %bitcast.13, f32[8,512,128]{2,1,0:T(8,128)} %bitcast.10), custom_call_target="tpu_custom_call" | custom-call | tf_op jit(solution)/shard_map/scatter/pallas_call | solution.py:255
  42.2 2.0 %collective-permute-start.4 = (f32[1,8,8,128]{3,2,1,0:T(8,128)S(1)}, f32[1,8,8,128]{3,2,1,0:T(8,128)S(1)}, u32[]{:S(2)}, u32[]{:S(2)}) collective-permute-start(f32[1,8,8,128]{3,2,1,0:T(8,128)S(1)} %get-tuple-element.42.pack), channel_id=1, source_target_pairs={{0,16},{16,32},{32,48},{48,64},{64,80},{80,96},{96,112},{1,17},{17... | collective-permute-start | bytes 98312 | tf_op jit(solution)/shard_map/ppermute | solution.py:314
  44.3 2.3 %collective-permute-start.5 = (f32[1,8,8,128]{3,2,1,0:T(8,128)S(1)}, f32[1,8,8,128]{3,2,1,0:T(8,128)S(1)}, u32[]{:S(2)}, u32[]{:S(2)}) collective-permute-start(f32[1,8,8,128]{3,2,1,0:T(8,128)S(1)} %get-tuple-element.42.pack), channel_id=1, source_target_pairs={{16,0},{32,16},{48,32},{64,48},{80,64},{96,80},{112,96},{17,1},{33... | collective-permute-start | bytes 98312 | tf_op jit(solution)/shard_map/ppermute | solution.py:314
  46.6 3.3 %collective-permute-done.5.east = f32[1,8,8,128]{3,2,1,0:T(8,128)S(1)} collective-permute-done((f32[1,8,8,128]{3,2,1,0:T(8,128)S(1)}, f32[1,8,8,128]{3,2,1,0:T(8,128)S(1)}, u32[]{:S(2)}, u32[]{:S(2)}) %collective-permute-start.5) | collective-permute-done | bytes 32800 | tf_op jit(solution)/shard_map/ppermute | solution.py:314
  50.6 4.3 %collective-permute-start.6 = (f32[1,4,72,128]{3,2,1,0:T(8,128)}, f32[1,4,72,128]{3,2,1,0:T(8,128)S(1)}, u32[]{:S(2)}, u32[]{:S(2)}) collective-permute-start(f32[1,4,72,128]{3,2,1,0:T(8,128)} %get-tuple-element.45.high), channel_id=1, source_target_pairs={{0,1},{1,2},{2,3},{3,4},{4,5},{5,6},{6,7},{7,8},{8,9},{9,10},{10,1... | collective-permute-start | bytes 442376 | tf_op jit(solution)/shard_map/ppermute | solution.py:320
  54.9 1.3 %collective-permute-start.7 = (f32[1,4,72,128]{3,2,1,0:T(8,128)}, f32[1,4,72,128]{3,2,1,0:T(8,128)S(1)}, u32[]{:S(2)}, u32[]{:S(2)}) collective-permute-start(f32[1,4,72,128]{3,2,1,0:T(8,128)} %get-tuple-element.46.low), channel_id=1, source_target_pairs={{1,0},{2,1},{3,2},{4,3},{5,4},{6,5},{7,6},{8,7},{9,8},{10,9},{11,1... | collective-permute-start | bytes 442376 | tf_op jit(solution)/shard_map/ppermute | solution.py:320
  56.2 1.6 %collective-permute-done.2.refs_0_ = f32[7,4,72,128]{3,2,1,0:T(8,128)S(1)} collective-permute-done((f32[7,4,72,128]{3,2,1,0:T(8,128)S(1)}, f32[7,4,72,128]{3,2,1,0:T(8,128)S(1)}, u32[]{:S(2)}, u32[]{:S(2)}) %collective-permute-start.2) | collective-permute-done | bytes 1032224 | tf_op jit(solution)/shard_map/ppermute | solution.py:320
  57.8 4.3 %collective-permute-done.3.refs_3_ = f32[7,4,72,128]{3,2,1,0:T(8,128)} collective-permute-done((f32[7,4,72,128]{3,2,1,0:T(8,128)S(1)}, f32[7,4,72,128]{3,2,1,0:T(8,128)}, u32[]{:S(2)}, u32[]{:S(2)}) %collective-permute-start.3) | collective-permute-done | bytes 1032224 | tf_op jit(solution)/shard_map/ppermute | solution.py:320
  62.1 0.9 copy-done.6
  63.0 3.5 %fields.2.fields_in = f32[8,512,128]{2,1,0:T(8,128)} custom-call(f32[7,4,72,128]{3,2,1,0:T(8,128)S(1)} %collective-permute-done.2.refs_0_, f32[7,4,72,128]{3,2,1,0:T(8,128)S(1)} %get-tuple-element.38.refs_1_, f32[7,4,72,128]{3,2,1,0:T(8,128)S(1)} %get-tuple-element.37.refs_2_, f32[7,4,72,128]{3,2,1,0:T(8,128)} %collective-permute-done.3.refs_3_, ...), custom_call_target="tpu_custom_call" | custom-call | tf_op jit(solution)/shard_map/fields/pallas_call | solution.py:437
  66.5 5.8 %gather.1 = (f32[8,512,128]{2,1,0:T(8,128)}, f32[1280,128]{1,0:T(8,128)}) custom-call(f32[1,4,72,128]{3,2,1,0:T(8,128)S(1)} %collective-permute-done.6.south, f32[1,4,72,128]{3,2,1,0:T(8,128)} %get-tuple-element.46.low, f32[1,4,72,128]{3,2,1,0:T(8,128)} %get-tuple-element.45.high, ...), custom_call_target="tpu_custom_call", output_to_operand_aliasing={{0}: (8, {})} | custom-call | tf_op jit(solution)/shard_map/gather/pallas_call | solution.py:481
  72.3 12.4 %all-to-all-start.1 = ((f32[128,1,1280]{2,1,0:T(1,128)}), f32[128,1,1280]{2,1,0:T(1,128)S(1)}, u32[]{:S(2)}, u32[]{:S(2)}) async-start(f32[128,1,1280]{2,1,0:T(1,128)} %bitcast.18), calls=%async_computation.1 | async-start | bytes 1310720 | tf_op jit(solution)/shard_map/all_to_all | solution.py:615
  84.8 1.0 copy-done.9
  85.8 3.7 %walls.5 = (f32[6,128,256]{2,1,0:T(8,128)}, f32[128,256]{1,0:T(8,128)}) custom-call(f32[8,128,128]{2,1,0:T(8,128)S(1)} %copy-done.9, f32[6,128,256]{2,1,0:T(8,128)S(1)} %copy-done.1, s32[1,256]{1,0:T(1,128)S(1)} %bitcast.16), custom_call_target="tpu_custom_call" | custom-call | tf_op jit(solution)/shard_map/walls/pallas_call | solution.py:530
  89.5 1.2 %copy-done.3 = f32[7,4,72,128]{3,2,1,0:T(8,128)S(1)} copy-done((f32[7,4,72,128]{3,2,1,0:T(8,128)S(1)}, f32[7,4,72,128]{3,2,1,0:T(8,128)}, u32[]{:S(2)}) %copy-start.3) | copy-done | bytes 1032216
  90.8 0.9 copy-done.7
  91.7 12.1 %fields.3 = f32[8,512,128]{2,1,0:T(8,128)} custom-call(f32[7,4,72,128]{3,2,1,0:T(8,128)S(1)} %copy-done.3, f32[7,4,72,128]{3,2,1,0:T(8,128)S(1)} %get-tuple-element.38.refs_1_, f32[7,4,72,128]{3,2,1,0:T(8,128)S(1)} %get-tuple-element.37.refs_2_, f32[7,4,72,128]{3,2,1,0:T(8,128)} %collective-permute-done.3.refs_3_, ...), custom_call_target="tpu_custom_call", output_to_operand_aliasing={{}: (7, {})} | custom-call | tf_op jit(solution)/shard_map/fields/pallas_call | solution.py:437
  103.8 1.1 %copy-done.8 = f32[6,128,256]{2,1,0:T(8,128)S(1)} copy-done((f32[6,128,256]{2,1,0:T(8,128)S(1)}, f32[6,128,256]{2,1,0:T(8,128)}, u32[]{:S(2)}) %copy-start.8) | copy-done | bytes 786456
  105.0 2.8 %final.1 = (f32[128,256]{1,0:T(8,128)}, f32[6,128,256]{2,1,0:T(8,128)}) custom-call(f32[1280,128]{1,0:T(8,128)S(1)} %bitcast.12, f32[128,256]{1,0:T(8,128)S(1)} %copy-done.12, f32[64,256]{1,0:T(8,128)S(1)} %copy-done.11, f32[6,256]{1,0:T(8,128)S(1)} %copy-done.15, f32[6,128,256]{2,1,0:T(8,128)} %walls.7, f32[6,128,256]{2,1,0:T(8,128)S(1)} %copy-done.8, ...), custom_call_target="tpu_custom_call" | custom-call | tf_op jit(solution)/shard_map/final/pallas_call | solution.py:585
  (39 shorter events, 3.5 us)
Async XLA Ops:
  0.6 0.8 copy-start.10
  1.5 0.7 copy-start.14
  2.2 0.7 copy-start.16
  2.9 0.7 copy-start.17
  6.1 27.9 %all-to-all-start = ((f32[128,1,768]{2,1,0:T(1,128)}), f32[128,1,768]{2,1,0:T(1,128)S(1)}, u32[]{:S(2)}, u32[]{:S(2)}) async-start(f32[128,1,768]{2,1,0:T(1,128)} %bitcast.19), calls=%async_computation | async-start | bytes 786432 | tf_op jit(solution)/shard_map/all_to_all | solution.py:615
  17.6 1.6 %copy-start = (f32[8,64,8,128]{3,2,1,0:T(8,128)S(1)}, f32[8,64,8,128]{3,2,1,0:T(8,128)}, u32[]{:S(2)}) copy-start(f32[8,64,8,128]{3,2,1,0:T(8,128)} %param.9) | copy-start | bytes 6291460
  19.2 0.7 copy-start.18
  21.6 0.7 copy-start.5
  22.3 6.6 %collective-permute-start = (f32[7,8,8,128]{3,2,1,0:T(8,128)S(1)}, f32[7,8,8,128]{3,2,1,0:T(8,128)S(1)}, u32[]{:S(2)}, u32[]{:S(2)}) collective-permute-start(f32[7,8,8,128]{3,2,1,0:T(8,128)S(1)} %get-tuple-element.32.pack), channel_id=1, source_target_pairs={{0,16},{16,32},{32,48},{48,64},{64,80},{80,96},{96,112},{1,17},{17... | collective-permute-start | bytes 688136 | tf_op jit(solution)/shard_map/ppermute | solution.py:314
  25.9 7.3 %collective-permute-start.1 = (f32[7,8,8,128]{3,2,1,0:T(8,128)S(1)}, f32[7,8,8,128]{3,2,1,0:T(8,128)S(1)}, u32[]{:S(2)}, u32[]{:S(2)}) collective-permute-start(f32[7,8,8,128]{3,2,1,0:T(8,128)S(1)} %get-tuple-element.32.pack), channel_id=1, source_target_pairs={{16,0},{32,16},{48,32},{64,48},{80,64},{96,80},{112,96},{17,1},{33... | collective-permute-start | bytes 688136 | tf_op jit(solution)/shard_map/ppermute | solution.py:314
  34.0 23.8 %collective-permute-start.2 = (f32[7,4,72,128]{3,2,1,0:T(8,128)S(1)}, f32[7,4,72,128]{3,2,1,0:T(8,128)S(1)}, u32[]{:S(2)}, u32[]{:S(2)}) collective-permute-start(f32[7,4,72,128]{3,2,1,0:T(8,128)S(1)} %get-tuple-element.37.refs_2_), channel_id=1, source_target_pairs={{0,1},{1,2},{2,3},{3,4},{4,5},{5,6},{6,7},{7,8},{8,9},{9,10},{10,1... | collective-permute-start | bytes 3096584 | tf_op jit(solution)/shard_map/ppermute | solution.py:320
  37.2 24.9 %collective-permute-start.3 = (f32[7,4,72,128]{3,2,1,0:T(8,128)S(1)}, f32[7,4,72,128]{3,2,1,0:T(8,128)}, u32[]{:S(2)}, u32[]{:S(2)}) collective-permute-start(f32[7,4,72,128]{3,2,1,0:T(8,128)S(1)} %get-tuple-element.38.refs_1_), channel_id=1, source_target_pairs={{1,0},{2,1},{3,2},{4,3},{5,4},{6,5},{7,6},{8,7},{9,8},{10,9},{11,1... | collective-permute-start | bytes 3096584 | tf_op jit(solution)/shard_map/ppermute | solution.py:320
  42.2 4.3 %collective-permute-start.4 = (f32[1,8,8,128]{3,2,1,0:T(8,128)S(1)}, f32[1,8,8,128]{3,2,1,0:T(8,128)S(1)}, u32[]{:S(2)}, u32[]{:S(2)}) collective-permute-start(f32[1,8,8,128]{3,2,1,0:T(8,128)S(1)} %get-tuple-element.42.pack), channel_id=1, source_target_pairs={{0,16},{16,32},{32,48},{48,64},{64,80},{80,96},{96,112},{1,17},{17... | collective-permute-start | bytes 98312 | tf_op jit(solution)/shard_map/ppermute | solution.py:314
  44.3 5.6 %collective-permute-start.5 = (f32[1,8,8,128]{3,2,1,0:T(8,128)S(1)}, f32[1,8,8,128]{3,2,1,0:T(8,128)S(1)}, u32[]{:S(2)}, u32[]{:S(2)}) collective-permute-start(f32[1,8,8,128]{3,2,1,0:T(8,128)S(1)} %get-tuple-element.42.pack), channel_id=1, source_target_pairs={{16,0},{32,16},{48,32},{64,48},{80,64},{96,80},{112,96},{17,1},{33... | collective-permute-start | bytes 98312 | tf_op jit(solution)/shard_map/ppermute | solution.py:314
  50.6 15.9 %collective-permute-start.6 = (f32[1,4,72,128]{3,2,1,0:T(8,128)}, f32[1,4,72,128]{3,2,1,0:T(8,128)S(1)}, u32[]{:S(2)}, u32[]{:S(2)}) collective-permute-start(f32[1,4,72,128]{3,2,1,0:T(8,128)} %get-tuple-element.45.high), channel_id=1, source_target_pairs={{0,1},{1,2},{2,3},{3,4},{4,5},{5,6},{6,7},{7,8},{8,9},{9,10},{10,1... | collective-permute-start | bytes 442376 | tf_op jit(solution)/shard_map/ppermute | solution.py:320
  54.9 11.6 %collective-permute-start.7 = (f32[1,4,72,128]{3,2,1,0:T(8,128)}, f32[1,4,72,128]{3,2,1,0:T(8,128)S(1)}, u32[]{:S(2)}, u32[]{:S(2)}) collective-permute-start(f32[1,4,72,128]{3,2,1,0:T(8,128)} %get-tuple-element.46.low), channel_id=1, source_target_pairs={{1,0},{2,1},{3,2},{4,3},{5,4},{6,5},{7,6},{8,7},{9,8},{10,9},{11,1... | collective-permute-start | bytes 442376 | tf_op jit(solution)/shard_map/ppermute | solution.py:320
  57.8 8.7 %copy-start.2 = (f32[7,4,72,128]{3,2,1,0:T(8,128)}, f32[7,4,72,128]{3,2,1,0:T(8,128)S(1)}, u32[]{:S(2)}) copy-start(f32[7,4,72,128]{3,2,1,0:T(8,128)S(1)} %collective-permute-done.2.refs_0_) | copy-start | bytes 3096580
  62.1 0.9 copy-start.6
  63.0 3.5 %copy-start.4 = (bf16[1024,1280]{1,0:T(8,128)(2,1)S(1)}, bf16[1024,1280]{1,0:T(8,128)(2,1)}, u32[]{:S(2)}) copy-start(bf16[1024,1280]{1,0:T(8,128)(2,1)} %get-tuple-element.47.counts_in) | copy-start | bytes 7864324
  66.5 18.2 %copy-start.1 = (f32[6,128,256]{2,1,0:T(8,128)S(1)}, f32[6,128,256]{2,1,0:T(8,128)}, u32[]{:S(2)}) copy-start(f32[6,128,256]{2,1,0:T(8,128)} %walls.7) | copy-start | bytes 2359300
  66.5 18.2 %copy-start.19 = (s32[256]{0:T(256)S(1)}, s32[256]{0:T(256)}, u32[]{:S(2)}) copy-start(s32[256]{0:T(256)} %param.13) | copy-start | bytes 3076
  72.3 31.5 %all-to-all-start.1 = ((f32[128,1,1280]{2,1,0:T(1,128)}), f32[128,1,1280]{2,1,0:T(1,128)S(1)}, u32[]{:S(2)}, u32[]{:S(2)}) async-start(f32[128,1,1280]{2,1,0:T(1,128)} %bitcast.18), calls=%async_computation.1 | async-start | bytes 1310720 | tf_op jit(solution)/shard_map/all_to_all | solution.py:615
  84.8 1.0 copy-start.9
  89.5 1.2 %copy-start.3 = (f32[7,4,72,128]{3,2,1,0:T(8,128)S(1)}, f32[7,4,72,128]{3,2,1,0:T(8,128)}, u32[]{:S(2)}) copy-start(f32[7,4,72,128]{3,2,1,0:T(8,128)} %copy-done.2) | copy-start | bytes 3096580
  90.8 0.9 copy-start.7
  91.7 12.1 %copy-start.11 = (f32[64,256]{1,0:T(8,128)S(1)}, f32[64,256]{1,0:T(8,128)}, u32[]{:S(2)}) copy-start(f32[64,256]{1,0:T(8,128)} %facade.3) | copy-start | bytes 196612
  91.7 12.1 %copy-start.12 = (f32[128,256]{1,0:T(8,128)S(1)}, f32[128,256]{1,0:T(8,128)}, u32[]{:S(2)}) copy-start(f32[128,256]{1,0:T(8,128)} %get-tuple-element.50.code) | copy-start | bytes 393220
  91.7 12.1 %copy-start.13 = (f32[128,256]{1,0:T(8,128)S(1)}, f32[128,256]{1,0:T(8,128)}, u32[]{:S(2)}) copy-start(f32[128,256]{1,0:T(8,128)} %get-tuple-element.52.column) | copy-start | bytes 393220
  91.7 12.1 %copy-start.15 = (f32[6,256]{1,0:T(8,128)S(1)}, f32[6,256]{1,0:T(8,128)}, u32[]{:S(2)}) copy-start(f32[6,256]{1,0:T(8,128)} %coeff.3) | copy-start | bytes 18436
  103.8 1.1 %copy-start.8 = (f32[6,128,256]{2,1,0:T(8,128)S(1)}, f32[6,128,256]{2,1,0:T(8,128)}, u32[]{:S(2)}) copy-start(f32[6,128,256]{2,1,0:T(8,128)} %get-tuple-element.51.product) | copy-start | bytes 2359300

commit v3 on v2

--- a/solution.py
+++ b/solution.py
@@ -20,7 +20,7 @@
 FLUX_ROWS = 6
 STRIP = 8
 AUX = 2 + FOOT
-EARLY = 1
+NEAR = 2
 
 source_rate = 0.1
 kappa_rate = 0.05
@@ -40,6 +40,9 @@
 
 def whole(shape):
     return pl.BlockSpec(shape, lambda *_: (0,) * len(shape))
+
+
+REMOTE = pl.BlockSpec(memory_space=pltpu.HBM)
 
 
 def halves(x):
@@ -127,48 +130,46 @@
     return out
 
 
-def emit_row(y, field, low, high, pack):
+def emit_row(f, y, field, low, high, pack):
     dst = low if y < HALO else high
-    dst[0, y % HALO, :, :] = field
-    pack[0, y] = pack_row([field[8 * i : 8 * i + 8] for i in range(8)])
-
-
-def prep_kernel(courant, canopy, low, high, pack, coef, coef_strip):
-    for y in range(ROWS_Y):
-        emit_row(y, canopy[0, pl.ds(y, LEV, stride=ROWS_Y), :], low, high, pack)
-
-    @pl.when(pl.program_id(0) == 0)
-    def _():
-        square = (LEV, LEV)
-        diagonal = lax.broadcasted_iota(jnp.int32, square, 0) == lax.broadcasted_iota(jnp.int32, square, 1)
-
-        def column(row):
-            picked = jnp.where(diagonal, jnp.broadcast_to(courant[row : row + 1, :], square), 0.0)
-            return jnp.broadcast_to(jnp.sum(picked, axis=1, keepdims=True), (LEV, LANES))
-
-        cx, cy = column(0), column(1)
-        values = (
-            1.0 - jnp.abs(cx) - jnp.abs(cy) - (4.0 * kappa_rate + 2.0 * vertical_rate),
-            jnp.maximum(cx, 0.0) + kappa_rate,
-            kappa_rate - jnp.minimum(cx, 0.0),
-            jnp.maximum(cy, 0.0) + kappa_rate,
-            kappa_rate - jnp.minimum(cy, 0.0),
-        )
-        block = lane_slot() // 16
-        for k, v in enumerate(values):
-            coef[k] = v
-            strip = v[0:8]
-            for i in range(1, 8):
-                strip = jnp.where(block == i, v[8 * i : 8 * i + 8], strip)
-            coef_strip[k] = strip
-
-
-def half_spec():
-    return pl.BlockSpec((1, HALO, LEV, LANES), lambda i: (i, 0, 0, 0))
-
-
-def pack_spec():
-    return pl.BlockSpec((1, ROWS_Y, STRIP, LANES), lambda i: (i, 0, 0, 0))
+    dst[f, y % HALO, :LEV, :] = field
+    pack[f, y] = pack_row([field[8 * i : 8 * i + 8] for i in range(8)])
+
+
+def prep_kernel(courant_in, canopy, low, high, pack, coef, coef_strip, field, courant, sems):
+    n = field.shape[0]
+    loads = [pltpu.make_async_copy(canopy.at[NEAR + f], field.at[f], sems.at[f]) for f in range(n)]
+    given = pltpu.make_async_copy(courant_in, courant, sems.at[n])
+    given.start()
+    for c in loads:
+        c.start()
+    given.wait()
+    square = (LEV, LEV)
+    diagonal = lax.broadcasted_iota(jnp.int32, square, 0) == lax.broadcasted_iota(jnp.int32, square, 1)
+
+    def column(row):
+        picked = jnp.where(diagonal, jnp.broadcast_to(courant[row : row + 1, :], square), 0.0)
+        return jnp.broadcast_to(jnp.sum(picked, axis=1, keepdims=True), (LEV, LANES))
+
+    cx, cy = column(0), column(1)
+    values = (
+        1.0 - jnp.abs(cx) - jnp.abs(cy) - (4.0 * kappa_rate + 2.0 * vertical_rate),
+        jnp.maximum(cx, 0.0) + kappa_rate,
+        kappa_rate - jnp.minimum(cx, 0.0),
+        jnp.maximum(cy, 0.0) + kappa_rate,
+        kappa_rate - jnp.minimum(cy, 0.0),
+    )
+    block = lane_slot() // 16
+    for k, v in enumerate(values):
+        coef[k] = v
+        strip = v[0:8]
+        for i in range(1, 8):
+            strip = jnp.where(block == i, v[8 * i : 8 * i + 8], strip)
+        coef_strip[k] = strip
+    for f in range(n):
+        loads[f].wait()
+        for y in range(ROWS_Y):
+            emit_row(f, y, field[f, pl.ds(y, LEV, stride=ROWS_Y), :], low, high, pack)
 
 
 def half_shape(n):
@@ -179,18 +180,20 @@
     return jax.ShapeDtypeStruct((n, ROWS_Y, STRIP, LANES), f32)
 
 
-def prep(courant, canopy, first, n):
+def half_spec(n):
+    return pl.BlockSpec((n, HALO, LEV, LANES), lambda i: (0, 0, 0, 0))
+
+
+def prep(courant, canopy):
+    n = canopy.shape[0] - NEAR
     return pl.pallas_call(
         prep_kernel,
-        grid=(n,),
-        in_specs=[
-            whole((2, LEV)),
-            pl.BlockSpec((1, LEV * ROWS_Y, LANES), lambda i: (i + first, 0, 0)),
-        ],
+        grid=(1,),
+        in_specs=[REMOTE, REMOTE],
         out_specs=[
-            half_spec(),
-            half_spec(),
-            pack_spec(),
+            half_spec(n),
+            half_spec(n),
+            whole((n, ROWS_Y, STRIP, LANES)),
             whole((5, LEV, LANES)),
             whole((5, STRIP, LANES)),
         ],
@@ -198,16 +201,21 @@
             half_shape(n),
             half_shape(n),
             pack_shape(n),
-            jax.ShapeDtypeStruct((5, LEV, LANES), f32),
-            jax.ShapeDtypeStruct((5, STRIP, LANES), f32),
+            pltpu.HBM((5, LEV, LANES), f32),
+            pltpu.HBM((5, STRIP, LANES), f32),
+        ],
+        scratch_shapes=[
+            pltpu.VMEM((n, LEV * ROWS_Y, LANES), f32),
+            pltpu.VMEM((2, LEV), f32),
+            pltpu.SemaphoreType.DMA((n + 1,)),
         ],
         compiler_params=params(),
         name="prep",
     )(courant, canopy)
 
 
-def scatter_kernel(recv, canopy, counts_out, low, high, pack, counts, column_s, field_s, xt, field0, sems):
-    load = pltpu.make_async_copy(canopy.at[0], field0, sems.at[0])
+def scatter_kernel(recv, canopy, counts_out, low, high, pack, counts, column_s, field_s, xt, near, sems):
+    load = pltpu.make_async_copy(canopy.at[pl.ds(0, NEAR)], near, sems.at[0])
     load.start()
     aux = recv[pl.ds(CAP // 2, DEV, stride=FLUX_ROWS), :].T
     cell = aux.astype(jnp.int32)
@@ -244,10 +252,12 @@
     sums = both[:DEV] + both[DEV:]
     load.wait()
     for y in range(ROWS_Y):
-        c = field0[pl.ds(y, LEV, stride=ROWS_Y), :]
+        c = near[0, pl.ds(y, LEV, stride=ROWS_Y), :]
         p = sums[:LEV, y * LANES : (y + 1) * LANES]
         q = sums[LEV:, y * LANES : (y + 1) * LANES]
-        emit_row(y, c + (source_rate / FOOT) * (p - q * c), low, high, pack)
+        emit_row(0, y, c + (source_rate / FOOT) * (p - q * c), low, high, pack)
+        for f in range(1, NEAR):
+            emit_row(f, y, near[f, pl.ds(y, LEV, stride=ROWS_Y), :], low, high, pack)
     save.wait()
 
 
@@ -256,19 +266,24 @@
         scatter_kernel,
         grid=(1,),
         in_specs=[whole((DEV * FLUX_ROWS, LANES)), pl.BlockSpec(memory_space=pltpu.HBM)],
-        out_specs=[pl.BlockSpec(memory_space=pltpu.HBM), half_spec(), half_spec(), pack_spec()],
+        out_specs=[
+            REMOTE,
+            half_spec(NEAR),
+            half_spec(NEAR),
+            whole((NEAR, ROWS_Y, STRIP, LANES)),
+        ],
         out_shape=[
             pltpu.HBM((ROWS_Y * LANES, CAP * DEV), bf16),
-            half_shape(1),
-            half_shape(1),
-            pack_shape(1),
+            half_shape(NEAR),
+            half_shape(NEAR),
+            pack_shape(NEAR),
         ],
         scratch_shapes=[
             pltpu.VMEM((ROWS_Y * LANES, CAP * DEV), bf16),
             pltpu.VMEM((LANES, DEV), jnp.int32),
             pltpu.VMEM((LANES, DEV), jnp.int32),
             pltpu.VMEM((2 * DEV, CAP * DEV), bf16),
-            pltpu.VMEM((LEV * ROWS_Y, LANES), f32),
+            pltpu.VMEM((NEAR, LEV * ROWS_Y, LANES), f32),
             pltpu.SemaphoreType.DMA((2,)),
         ],
         compiler_params=params(),
@@ -278,24 +293,26 @@
 
 def merge_kernel(pack, west, east, low_in, high_in, low, high):
     slot = lane_slot() % 16
-    for y in range(ROWS_Y):
-        strip = jnp.where(
-            slot < 4,
-            pltpu.roll(west[0, y], LANES - 8, 1),
-            jnp.where(slot < 12, pack[0, y], pltpu.roll(east[0, y], 8, 1)),
-        )
-        dst = low if y < HALO else high
-        dst[0, y % HALO] = strip
+    for f in range(pack.shape[0]):
+        for y in range(ROWS_Y):
+            strip = jnp.where(
+                slot < 4,
+                pltpu.roll(west[f, y], LANES - 8, 1),
+                jnp.where(slot < 12, pack[f, y], pltpu.roll(east[f, y], 8, 1)),
+            )
+            dst = low if y < HALO else high
+            dst[f, y % HALO] = strip
 
 
 def merge(pack, west, east, low, high):
     n = pack.shape[0]
-    strip_spec = pl.BlockSpec((1, HALO, STRIP, LANES), lambda i: (i, 0, LEV // STRIP, 0))
+    pack_spec = whole((n, ROWS_Y, STRIP, LANES))
+    strip_spec = pl.BlockSpec((n, HALO, STRIP, LANES), lambda i: (0, 0, LEV // STRIP, 0))
     anywhere = pl.BlockSpec(memory_space=pl.ANY)
     return pl.pallas_call(
         merge_kernel,
-        grid=(n,),
-        in_specs=[pack_spec(), pack_spec(), pack_spec(), anywhere, anywhere],
+        grid=(1,),
+        in_specs=[pack_spec, pack_spec, pack_spec, anywhere, anywhere],
         out_specs=[strip_spec, strip_spec],
         out_shape=[half_shape(n), half_shape(n)],
         input_output_aliases={3: 0, 4: 1},
@@ -309,10 +326,15 @@
     return up, [(j, i) for i, j in up]
 
 
-def across_x(low, high, pack):
+def across_x(low, high, pack, beside=None):
     up, down = shifts("gx")
     west, east = lax.ppermute(pack, "gx", up), lax.ppermute(pack, "gx", down)
-    return merge(pack, west, east, low, high)
+    done = None
+    if beside is not None:
+        done = beside()
+        west, east, done = lax.optimization_barrier((west, east, done))
+    low, high = merge(pack, west, east, low, high)
+    return low, high, done
 
 
 def across_y(low, high):
@@ -321,7 +343,7 @@
     return south, low, high, north
 
 
-def substeps(parts, coef, coef_strip, edge, buf, strips, ends, put):
+def substeps(f, parts, coef, coef_strip, edge, buf, strips, ends, put):
     lane = lane_slot()
     sub = lax.broadcasted_iota(jnp.int32, (8, LANES), 0)
     slot = lane % 16
@@ -341,12 +363,12 @@
 
         def main(row, start):
             if step == 1:
-                return parts[row // HALO][0, row % HALO, start : start + 8, :]
+                return parts[row // HALO][f, row % HALO, start : start + 8, :]
             return buf[old, row, start : start + 8, :]
 
         def strip(row):
             if step == 1:
-                return parts[row // HALO][0, row % HALO, LEV : LEV + STRIP, :]
+                return parts[row // HALO][f, row % HALO, LEV : LEV + STRIP, :]
             return strips[old, row]
 
         rows = range(step, total - step)
@@ -397,8 +419,8 @@
             strips[new, row] = keep(row, value * inside)
 
 
-def quarter_spec(first):
-    return pl.BlockSpec((1, HALO, LEV + STRIP, LANES), lambda i: (i + first, 0, 0, 0))
+def quarter_spec(n):
+    return pl.BlockSpec((n, HALO, LEV + STRIP, LANES), lambda i: (i, 0, 0, 0))
 
 
 STENCIL_SCRATCH = [
@@ -416,56 +438,48 @@
     ]
 
 
-def fields_kernel(*refs):
-    south, low, high, north, coef, coef_strip, edge = refs[:7]
-    out, buf, strips, ends = refs[-4:]
-
+def fields_kernel(south, low, high, north, coef, coef_strip, edge, into, out, buf, strips, ends):
     def put(y, at, value):
         out[0, pl.ds(at * ROWS_Y + y, 8, stride=ROWS_Y), :] = value
 
-    substeps((south, low, high, north), coef, coef_strip, edge, buf, strips, ends, put)
-
-
-def fields(parts, coefs, first, n, into=None):
-    operands = [*parts, *coefs]
-    specs = [quarter_spec(first) for _ in parts] + coef_specs()
-    alias = {}
-    if into is not None:
-        alias = {len(operands): 0}
-        operands.append(into)
-        specs.append(pl.BlockSpec(memory_space=pl.ANY))
+    substeps(0, (south, low, high, north), coef, coef_strip, edge, buf, strips, ends, put)
+
+
+def fields(parts, coefs, into):
+    n = parts[0].shape[0]
+    operands = [*parts, *coefs, into]
     return pl.pallas_call(
         fields_kernel,
         grid=(n,),
-        in_specs=specs,
-        out_specs=pl.BlockSpec((1, LEV * ROWS_Y, LANES), lambda i: (i + first + 1, 0, 0)),
-        out_shape=pltpu.HBM((8, LEV * ROWS_Y, LANES), f32),
+        in_specs=[quarter_spec(1) for _ in parts] + coef_specs() + [pl.BlockSpec(memory_space=pltpu.HBM)],
+        out_specs=pl.BlockSpec((1, LEV * ROWS_Y, LANES), lambda i: (i + NEAR, 0, 0)),
+        out_shape=pltpu.HBM(into.shape, f32),
         scratch_shapes=[pltpu.VMEM(s, f32) for s in STENCIL_SCRATCH],
-        input_output_aliases=alias,
+        input_output_aliases={len(operands) - 1: 0},
         compiler_params=params(),
         name="fields",
     )(*operands)
 
 
-def gather_kernel(
-    south, low, high, north, coef, coef_strip, edge, counts_in, fields_in, out, back, *scratch
-):
-    buf, strips, ends, table, counts, humid, sems = scratch
+def gather_kernel(south, low, high, north, coef, coef_strip, edge, counts_in, fields_out, back, *scratch):
+    buf, strips, ends, table, counts, out, sems = scratch
     fetch = pltpu.make_async_copy(counts_in, counts, sems.at[0])
     fetch.start()
-    other = pltpu.make_async_copy(fields_in.at[1], humid, sems.at[1])
-    other.start()
-
-    def put(y, at, value):
-        out[0, pl.ds(at * ROWS_Y + y, 8, stride=ROWS_Y), :] = value
-
-    substeps((south, low, high, north), coef, coef_strip, edge, buf, strips, ends, put)
-    other.wait()
+    save = pltpu.make_async_copy(out, fields_out.at[pl.ds(0, NEAR)], sems.at[1])
+
+    def field(f, carry):
+        def put(y, at, value):
+            out[f, pl.ds(at * ROWS_Y + y, 8, stride=ROWS_Y), :] = value
+
+        substeps(f, (south, low, high, north), coef, coef_strip, edge, buf, strips, ends, put)
+        return carry
+
+    lax.fori_loop(0, NEAR, field, 0)
+    save.start()
     for y in range(ROWS_Y):
         cols = slice(y * LANES, (y + 1) * LANES)
-        pick = pl.ds(y, LEV, stride=ROWS_Y)
-        for k, field in enumerate((out[0, pick, :], humid[pick, :])):
-            hi, lo = halves(field * (1.0 / FOOT))
+        for k in range(NEAR):
+            hi, lo = halves(out[k, pl.ds(y, LEV, stride=ROWS_Y), :] * (1.0 / FOOT))
             table[k * LEV : (k + 1) * LEV, cols] = hi
             table[2 * LEV + k * LEV : 2 * LEV + (k + 1) * LEV, cols] = lo
     fetch.wait()
@@ -473,16 +487,18 @@
     sums = both[: 2 * LEV] + both[2 * LEV :]
     for r in range(CAP):
         back[pl.ds(r, DEV, stride=CAP), :] = sums[:, r * DEV : (r + 1) * DEV].T
-
-
-def gather(parts, coefs, counts, into):
-    field_block = (1, LEV * ROWS_Y, LANES)
-    remote = pl.BlockSpec(memory_space=pltpu.HBM)
+    save.wait()
+
+
+def gather(parts, coefs, counts):
     return pl.pallas_call(
         gather_kernel,
         grid=(1,),
-        in_specs=[quarter_spec(0) for _ in parts] + coef_specs() + [remote, remote],
-        out_specs=[pl.BlockSpec(field_block, lambda i: (0, 0, 0)), whole((DEV * CAP, LANES))],
+        in_specs=[quarter_spec(NEAR) for _ in parts] + coef_specs() + [REMOTE],
+        out_specs=[
+            REMOTE,
+            whole((DEV * CAP, LANES)),
+        ],
         out_shape=[
             pltpu.HBM((8, LEV * ROWS_Y, LANES), f32),
             pltpu.HBM((DEV * CAP, LANES), f32),
@@ -491,89 +507,115 @@
         + [
             pltpu.VMEM((4 * LEV, ROWS_Y * LANES), bf16),
             pltpu.VMEM((ROWS_Y * LANES, CAP * DEV), bf16),
-            pltpu.VMEM((LEV * ROWS_Y, LANES), f32),
+            pltpu.VMEM((NEAR, LEV * ROWS_Y, LANES), f32),
             pltpu.SemaphoreType.DMA((2,)),
         ],
-        input_output_aliases={8: 0},
         compiler_params=params(),
         name="gather",
-    )(*parts, *coefs, counts, into)
-
-
-def walls_kernel(inverses, walls, package, out, column, a, b_hi, b_lo):
-    n = walls.shape[1]
-
-    @pl.when(pl.program_id(0) == 0)
-    def _():
-        chosen = jnp.zeros((n, NB), f32)
+    )(*parts, *coefs, counts)
+
+
+def walls_kernel(inverses, walls, package, product, column, inv_v, wall_v, out, a, b_hi, b_lo, inv_sem, sems, save_sems):
+    surfaces, n, _ = wall_v.shape
+    first = pltpu.make_async_copy(inverses, inv_v, inv_sem)
+    first.start()
+
+    def load(s):
+        return pltpu.make_async_copy(walls.at[s], wall_v.at[s], sems.at[s])
+
+    def save(s):
+        return pltpu.make_async_copy(out.at[s], product.at[s], save_sems.at[s])
+
+    for s in range(surfaces):
+        load(s).start()
+    first.wait()
+
+    chosen = jnp.zeros((n, NB), f32)
+    for p in range(PKG):
+        inv = inv_v[p]
+        hi, lo = halves(inv)
+        a[:n, p * n : (p + 1) * n] = hi
+        a[n:, p * n : (p + 1) * n] = lo
+        chosen = jnp.where(package[...] == p, jnp.broadcast_to(inv[:, 0:1], (n, NB)), chosen)
+    column[...] = chosen
+
+    def surface(s, carry):
+        load(s).wait()
+        w = wall_v[s]
+        w_hi = w.astype(bf16).astype(f32)
+        w_lo = w - w_hi
         for p in range(PKG):
-            inv = inverses[p]
-            hi, lo = halves(inv)
-            a[:n, p * n : (p + 1) * n] = hi
-            a[n:, p * n : (p + 1) * n] = lo
-            chosen = jnp.where(package[...] == p, jnp.broadcast_to(inv[:, 0:1], (n, NB)), chosen)
-        column[...] = chosen
-
-    w = walls[0]
-    w_hi = w.astype(bf16).astype(f32)
-    w_lo = w - w_hi
-    for p in range(PKG):
-        mine = package[...] == p
-        b_hi[p * n : (p + 1) * n, :] = jnp.where(mine, w_hi, 0.0).astype(bf16)
-        b_lo[p * n : (p + 1) * n, :] = jnp.where(mine, w_lo, 0.0).astype(bf16)
-    both = mm(a[...], b_hi[...], NN)
-    out[0] = both[:n] + both[n:] + mm(a[:n, :], b_lo[...], NN)
+            mine = package[...] == p
+            b_hi[p * n : (p + 1) * n, :] = jnp.where(mine, w_hi, 0.0).astype(bf16)
+            b_lo[p * n : (p + 1) * n, :] = jnp.where(mine, w_lo, 0.0).astype(bf16)
+        both = mm(a[...], b_hi[...], NN)
+        out[s] = both[:n] + both[n:] + mm(a[:n, :], b_lo[...], NN)
+        save(s).start()
+        return carry
+
+    lax.fori_loop(0, surfaces, surface, 0)
+    for s in range(surfaces):
+        save(s).wait()
 
 
 def walls_product(inverses, walls, package):
     s, n, _ = walls.shape
     return pl.pallas_call(
         walls_kernel,
-        grid=(s,),
-        in_specs=[
-            whole((PKG, n, n)),
-            pl.BlockSpec((1, n, NB), lambda i: (i, 0, 0)),
-            whole((1, NB)),
-        ],
-        out_specs=[pl.BlockSpec((1, n, NB), lambda i: (i, 0, 0)), whole((n, NB))],
+        grid=(1,),
+        in_specs=[REMOTE, REMOTE, whole((1, NB))],
+        out_specs=[REMOTE, whole((n, NB))],
         out_shape=[pltpu.HBM((s, n, NB), f32), pltpu.HBM((n, NB), f32)],
         scratch_shapes=[
+            pltpu.VMEM((PKG, n, n), f32),
+            pltpu.VMEM((s, n, NB), f32),
+            pltpu.VMEM((s, n, NB), f32),
             pltpu.VMEM((2 * n, PKG * n), bf16),
             pltpu.VMEM((PKG * n, NB), bf16),
             pltpu.VMEM((PKG * n, NB), bf16),
+            pltpu.SemaphoreType.DMA,
+            pltpu.SemaphoreType.DMA((s,)),
+            pltpu.SemaphoreType.DMA((s,)),
         ],
         compiler_params=params(),
         name="walls",
     )(inverses, walls, package)
 
 
-def final_kernel(recv, code, facade, coeff, walls, product, column, air_out, walls_out, xt, value, col, first, sems):
+def final_kernel(recv, code_in, facade_in, coeff_in, walls, product, column_in, air_out, walls_out, *scratch):
+    xt, code, facade, coeff, first, value, column, load_sems, sems = scratch
     surfaces = value.shape[0]
-    loads = [
-        pltpu.make_async_copy(product, value, sems.at[0]),
-        pltpu.make_async_copy(column, col, sems.at[1]),
-        pltpu.make_async_copy(walls.at[:, pl.ds(0, 8), :], first, sems.at[2]),
-    ]
+    pairs = (
+        (code_in, code),
+        (facade_in, facade),
+        (coeff_in, coeff),
+        (walls.at[:, pl.ds(0, 8), :], first),
+        (product, value),
+        (column_in, column),
+    )
+    loads = [pltpu.make_async_copy(src, dst, load_sems.at[i]) for i, (src, dst) in enumerate(pairs)]
     for c in loads:
         c.start()
-    picks = []
     for r in range(CAP):
         hi, lo = halves(recv[pl.ds(r, DEV, stride=CAP), :].T)
         xt[:LANES, r * DEV : (r + 1) * DEV] = hi
         xt[LANES:, r * DEV : (r + 1) * DEV] = lo
+    loads[0].wait()
+    picks = []
+    for r in range(CAP):
         picks.append(jnp.where(code[...] == float(r), 1.0, 0.0).astype(bf16))
     both = mm(xt[...], jnp.concatenate(picks, axis=0), NN)
     air = both[:LANES] + both[LANES:]
     air_out[...] = air
+    for c in loads[1:]:
+        c.wait()
     area = facade[...]
     temp = jnp.sum(area * air[:LEV], axis=0, keepdims=True) / jnp.sum(area, axis=0, keepdims=True)
-    for c in loads:
-        c.wait()
     saves = []
     for s in range(surfaces):
         source = wall_gain * coeff[s : s + 1, :] * (temp - first[s, 0:1, :])
-        value[s] = value[s] + col[...] * source
-        saves.append(pltpu.make_async_copy(value.at[s], walls_out.at[s], sems.at[3 + s]))
+        value[s] = value[s] + column[...] * source
+        saves.append(pltpu.make_async_copy(value.at[s], walls_out.at[s], sems.at[s]))
         saves[s].start()
     for c in saves:
         c.wait()
@@ -581,30 +623,33 @@
 
 def final(recv, code, facade, coeff, walls, product, column):
     s, n, _ = walls.shape
-    remote = pl.BlockSpec(memory_space=pltpu.HBM)
     return pl.pallas_call(
         final_kernel,
         grid=(1,),
         in_specs=[
             whole((DEV * CAP, LANES)),
-            whole((DEV, NB)),
-            whole((LEV, NB)),
-            whole((s, NB)),
-            remote,
-            remote,
-            remote,
-        ],
-        out_specs=[whole((2 * LEV, NB)), remote],
+            REMOTE,
+            REMOTE,
+            REMOTE,
+            REMOTE,
+            REMOTE,
+            REMOTE,
+        ],
+        out_specs=[whole((2 * LEV, NB)), REMOTE],
         out_shape=[
             jax.ShapeDtypeStruct((2 * LEV, NB), f32),
             pltpu.HBM((s, n, NB), f32),
         ],
         scratch_shapes=[
             pltpu.VMEM((2 * LANES, CAP * DEV), bf16),
+            pltpu.VMEM((DEV, NB), f32),
+            pltpu.VMEM((LEV, NB), f32),
+            pltpu.VMEM((s, NB), f32),
+            pltpu.VMEM((s, 8, NB), f32),
             pltpu.VMEM((s, n, NB), f32),
             pltpu.VMEM((n, NB), f32),
-            pltpu.VMEM((s, 8, NB), f32),
-            pltpu.SemaphoreType.DMA((3 + s,)),
+            pltpu.SemaphoreType.DMA((6,)),
+            pltpu.SemaphoreType.DMA((s,)),
         ],
         compiler_params=params(),
         name="final",
@@ -634,23 +679,27 @@
     shape = canopy.shape
     canopy = canopy.reshape(shape[0], LEV * ROWS_Y, LANES)
     edge = inside_edges()
-    send, code = payload(anchor.T, footprint.T, surf_coeff, hbm(walls), facade_area)
+    send, code = payload(hbm(anchor.T), hbm(footprint.T), hbm(surf_coeff), hbm(walls), hbm(facade_area))
     recv = transpose_all(send, FLUX_ROWS)
     later, code = lax.optimization_barrier((canopy, code))
-    low, high, pack, coef, coef_strip = prep(courant, later, 1, shape[0] - 1)
-    coefs = (coef, coef_strip, edge)
-    low, high = across_x(low, high, pack)
+    low, high, pack, coef, coef_strip = prep(hbm(courant), hbm(later))
+    coefs = (hbm(coef), hbm(coef_strip), edge)
+    low, high, _ = across_x(low, high, pack)
     recv, low, high = lax.optimization_barrier((recv, low, high))
-    rest = across_y(low, high)
-    out = fields(rest, coefs, 0, EARLY)
-    product, column = walls_product(inverses, walls, package[None, :])
-    counts, low, high, pack = scatter(recv, hbm(canopy))
-    zeroth = across_y(*across_x(low, high, pack))
-    out, back = gather(zeroth, coefs, counts, out)
+    up, down = shifts("gy")
+    south = lax.ppermute(high, "gy", up)
+    counts, near_low, near_high, pack = scatter(recv, hbm(canopy))
+    near_low, near_high, _ = across_x(near_low, near_high, pack)
+    near_low, near_high, low, walls_later = lax.optimization_barrier((near_low, near_high, low, walls))
+    near = across_y(near_low, near_high)
+    north = lax.ppermute(low, "gy", down)
+    product, column = walls_product(hbm(inverses), hbm(walls_later), hbm(package[None, :]))
+    near, south, product = lax.optimization_barrier((near, south, product))
+    rest = (south, low, high, north)
+    out, back = gather(near, coefs, hbm(counts))
     returned = transpose_all(back, CAP)
-    if EARLY < shape[0] - 1:
-        out = fields(rest, coefs, EARLY, shape[0] - 1 - EARLY, out)
-    air, walls_out = final(returned, code, facade_area, surf_coeff, hbm(walls), product, column)
+    out = fields(rest, coefs, out)
+    air, walls_out = final(returned, hbm(code), hbm(facade_area), hbm(surf_coeff), hbm(walls), hbm(product), hbm(column))
     return out.reshape(shape), air.reshape(2, LEV, NB), walls_out
 
 

time: 109 us -> 93 us (0.85)
  local copies, waits for them, and re-layouts: 11.1 us -> 0 us
  starting transfers between devices: 43.8 us -> 41.2 us
    unnamed x40 -> x0, local copies, waits for them, and re-layouts: 11.1 us -> none
    ppermute x4 -> x2, starting transfers between devices: 10 us -> 3.9 us  [across_y(): south, north = (lax.ppermute(high, 'gy', up), lax.ppermute(low, 'gy', down))]
    ppermute x0 -> x2, starting transfers between devices: none -> 5.33 us  [the longest x1 4.03 us: body(): south = lax.ppermute(high, 'gy', up)]
    ppermute x4 -> x2, waiting for transfers between devices: 5.9 us -> 2.5 us  [across_y(): south, north = (lax.ppermute(high, 'gy', up), lax.ppermute(low, 'gy', down))]
    all_to_all x2, waiting for transfers between devices: 0.01 us -> 3.08 us  [transpose_all(): lax.all_to_all(x.reshape(DEV, 1, rows * LANES), ('gx', 'gy'), split_axis=...]
    all_to_all x2, starting transfers between devices: 23.9 us -> 22.1 us  [transpose_all(): lax.all_to_all(x.reshape(DEV, 1, rows * LANES), ('gx', 'gy'), split_axis=...]
    pallas_call x7 -> x6, Pallas kernels: 28.3 us -> 27.6 us  [the longest x1 12.1 us: fields(): pl.pallas_call(fields_kernel, grid=(n,), in_specs=[quarter_spec(1) for _...]
  transfers between devices with their start and end apart: 10 -> 10, of which waited for: 5 -> 6; matrix products, arithmetic and copies ran while one was open for 0% -> 0% of each run, Pallas kernels for 24% -> 33%
where the time goes in v3:
time: 93 us; the launch traced here: 92.4 us
  starting transfers between devices  41.2 us (44%)
  Pallas kernels  36.4 us (39%)
  waiting for transfers between devices  13.9 us (15%)
    all_to_all x2, starting transfers between devices, transpose_all(): lax.all_to_all(x.reshape(DEV, 1, rows * LANES), ('gx', 'gy'), split_axis=...  22.1 us
    pallas_call x1, Pallas kernels, fields(): pl.pallas_call(fields_kernel, grid=(n,), in_specs=[quarter_spec(1) for _...  12.1 us
    ppermute x4, starting transfers between devices, across_x(): west, east = (lax.ppermute(pack, 'gx', up), lax.ppermute(pack, 'gx', down))  9.91 us
    ppermute x4, waiting for transfers between devices, across_x(): west, east = (lax.ppermute(pack, 'gx', up), lax.ppermute(pack, 'gx', down))  8.33 us
    pallas_call x1, Pallas kernels, gather(): pl.pallas_call(gather_kernel, grid=(1,), in_specs=[quarter_spec(NEAR) for...  6.26 us
    pallas_call x1, Pallas kernels, walls_product(): pl.pallas_call(walls_kernel, grid=(1,), in_specs=[REMOTE, REMOTE, whole((...  5.96 us
    ppermute x1, starting transfers between devices, body(): south = lax.ppermute(high, 'gy', up)  4.03 us
    ppermute x2, starting transfers between devices, across_y(): south, north = (lax.ppermute(high, 'gy', up), lax.ppermute(low, 'gy', down))  3.9 us
  transfers between devices with their start and end apart: 10, of which 6 were waited for; matrix products, arithmetic and copies ran while one was open for 0% of the time, Pallas kernels for 33%

profile of v3, /device:TPU:1, one launch (start us, length us, event | category | flops | bytes accessed | tf_op | source)
XLA Modules:
  0.0 92.4 jit_solution(1257346785793469305)
XLA Ops:
  0.6 2.7 %payload.1 = (f32[768,128]{1,0:T(8,128)}, f32[128,256]{1,0:T(8,128)}) custom-call(s32[1,256]{1,0:T(1,128)} %bitcast.18, s32[8,256]{1,0:T(8,128)} %bitcast.17, f32[6,256]{1,0:T(8,128)} %coeff_in.1, f32[6,128,256]{2,1,0:T(8,128)} %walls.6, f32[64,256]{1,0:T(8,128)} %facade_in.1), custom_call_target="tpu_custom_call" | custom-call | tf_op jit(solution)/shard_map/payload/pallas_call | solution.py:95
  3.3 11.5 %all-to-all-start = ((f32[128,1,768]{2,1,0:T(1,128)}), f32[128,1,768]{2,1,0:T(1,128)S(1)}, u32[]{:S(2)}, u32[]{:S(2)}) async-start(f32[128,1,768]{2,1,0:T(1,128)} %bitcast.16), calls=%async_computation | async-start | bytes 786432 | tf_op jit(solution)/shard_map/all_to_all | solution.py:660
  14.8 3.0 %prep.1 = (f32[6,4,72,128]{3,2,1,0:T(8,128)S(1)}, f32[6,4,72,128]{3,2,1,0:T(8,128)S(1)}, f32[6,8,8,128]{3,2,1,0:T(8,128)S(1)}, f32[5,64,128]{2,1,0:T(8,128)}, f32[5,8,128]{2,1,0:T(8,128)}) custom-call(f32[2,64]{1,0:T(2,128)} %courant_in.1, f32[8,512,128]{2,1,0:T(8,128)} %bitcast.12), custom_call_target="tpu_custom_call" | custom-call | tf_op jit(solution)/shard_map/prep/pallas_call | solution.py:189
  17.8 3.7 %collective-permute-start = (f32[6,8,8,128]{3,2,1,0:T(8,128)S(1)}, f32[6,8,8,128]{3,2,1,0:T(8,128)S(1)}, u32[]{:S(2)}, u32[]{:S(2)}) collective-permute-start(f32[6,8,8,128]{3,2,1,0:T(8,128)S(1)} %get-tuple-element.42.pack), channel_id=1, source_target_pairs={{0,16},{16,32},{32,48},{48,64},{64,80},{80,96},{96,112},{1,17},{17... | collective-permute-start | bytes 589832 | tf_op jit(solution)/shard_map/ppermute | solution.py:331
  21.4 1.9 %collective-permute-start.1 = (f32[6,8,8,128]{3,2,1,0:T(8,128)S(1)}, f32[6,8,8,128]{3,2,1,0:T(8,128)S(1)}, u32[]{:S(2)}, u32[]{:S(2)}) collective-permute-start(f32[6,8,8,128]{3,2,1,0:T(8,128)S(1)} %get-tuple-element.42.pack), channel_id=1, source_target_pairs={{16,0},{32,16},{48,32},{64,48},{80,64},{96,80},{112,96},{17,1},{33... | collective-permute-start | bytes 589832 | tf_op jit(solution)/shard_map/ppermute | solution.py:331
  23.4 1.1 %collective-permute-done.west = f32[6,8,8,128]{3,2,1,0:T(8,128)S(1)} collective-permute-done((f32[6,8,8,128]{3,2,1,0:T(8,128)S(1)}, f32[6,8,8,128]{3,2,1,0:T(8,128)S(1)}, u32[]{:S(2)}, u32[]{:S(2)}) %collective-permute-start) | collective-permute-done | bytes 196640 | tf_op jit(solution)/shard_map/ppermute | solution.py:331
  24.5 3.9 %collective-permute-done.1.east = f32[6,8,8,128]{3,2,1,0:T(8,128)S(1)} collective-permute-done((f32[6,8,8,128]{3,2,1,0:T(8,128)S(1)}, f32[6,8,8,128]{3,2,1,0:T(8,128)S(1)}, u32[]{:S(2)}, u32[]{:S(2)}) %collective-permute-start.1) | collective-permute-done | bytes 196640 | tf_op jit(solution)/shard_map/ppermute | solution.py:331
  28.4 0.2 merge.2
  28.6 0.0 all-to-all-done
  28.6 4.0 %collective-permute-start.6 = (f32[6,4,72,128]{3,2,1,0:T(8,128)S(1)}, f32[6,4,72,128]{3,2,1,0:T(8,128)}, u32[]{:S(2)}, u32[]{:S(2)}) collective-permute-start(f32[6,4,72,128]{3,2,1,0:T(8,128)S(1)} %get-tuple-element.56.high), channel_id=1, source_target_pairs={{0,1},{1,2},{2,3},{3,4},{4,5},{5,6},{6,7},{7,8},{8,9},{9,10},{10,1... | collective-permute-start | bytes 2654216 | tf_op jit(solution)/shard_map/ppermute | solution.py:690
  32.6 3.1 %scatter.1 = (bf16[1024,1280]{1,0:T(8,128)(2,1)}, f32[2,4,72,128]{3,2,1,0:T(8,128)S(1)}, f32[2,4,72,128]{3,2,1,0:T(8,128)S(1)}, f32[2,8,8,128]{3,2,1,0:T(8,128)S(1)}) custom-call(f32[768,128]{1,0:T(8,128)S(1)} %bitcast.11, f32[8,512,128]{2,1,0:T(8,128)} %bitcast.13), custom_call_target="tpu_custom_call" | custom-call | tf_op jit(solution)/shard_map/scatter/pallas_call | solution.py:265
  35.7 2.0 %collective-permute-start.2 = (f32[2,8,8,128]{3,2,1,0:T(8,128)S(1)}, f32[2,8,8,128]{3,2,1,0:T(8,128)S(1)}, u32[]{:S(2)}, u32[]{:S(2)}) collective-permute-start(f32[2,8,8,128]{3,2,1,0:T(8,128)S(1)} %get-tuple-element.48.pack), channel_id=1, source_target_pairs={{0,16},{16,32},{32,48},{48,64},{64,80},{80,96},{96,112},{1,17},{17... | collective-permute-start | bytes 196616 | tf_op jit(solution)/shard_map/ppermute | solution.py:331
  37.8 2.3 %collective-permute-start.3 = (f32[2,8,8,128]{3,2,1,0:T(8,128)S(1)}, f32[2,8,8,128]{3,2,1,0:T(8,128)S(1)}, u32[]{:S(2)}, u32[]{:S(2)}) collective-permute-start(f32[2,8,8,128]{3,2,1,0:T(8,128)S(1)} %get-tuple-element.48.pack), channel_id=1, source_target_pairs={{16,0},{32,16},{48,32},{64,48},{80,64},{96,80},{112,96},{17,1},{33... | collective-permute-start | bytes 196616 | tf_op jit(solution)/shard_map/ppermute | solution.py:331
  40.1 0.0 collective-permute-done.2.west
  40.1 3.3 %collective-permute-done.3.east = f32[2,8,8,128]{3,2,1,0:T(8,128)S(1)} collective-permute-done((f32[2,8,8,128]{3,2,1,0:T(8,128)S(1)}, f32[2,8,8,128]{3,2,1,0:T(8,128)S(1)}, u32[]{:S(2)}, u32[]{:S(2)}) %collective-permute-start.3) | collective-permute-done | bytes 65568 | tf_op jit(solution)/shard_map/ppermute | solution.py:331
  43.3 0.1 merge.3
  43.4 2.6 %collective-permute-start.4 = (f32[2,4,72,128]{3,2,1,0:T(8,128)S(1)}, f32[2,4,72,128]{3,2,1,0:T(8,128)S(1)}, u32[]{:S(2)}, u32[]{:S(2)}) collective-permute-start(f32[2,4,72,128]{3,2,1,0:T(8,128)S(1)} %get-tuple-element.65.high), channel_id=1, source_target_pairs={{0,1},{1,2},{2,3},{3,4},{4,5},{5,6},{6,7},{7,8},{8,9},{9,10},{10,1... | collective-permute-start | bytes 884744 | tf_op jit(solution)/shard_map/ppermute | solution.py:342
  46.1 1.3 %collective-permute-start.5 = (f32[2,4,72,128]{3,2,1,0:T(8,128)S(1)}, f32[2,4,72,128]{3,2,1,0:T(8,128)S(1)}, u32[]{:S(2)}, u32[]{:S(2)}) collective-permute-start(f32[2,4,72,128]{3,2,1,0:T(8,128)S(1)} %get-tuple-element.64.low), channel_id=1, source_target_pairs={{1,0},{2,1},{3,2},{4,3},{5,4},{6,5},{7,6},{8,7},{9,8},{10,9},{11,1... | collective-permute-start | bytes 884744 | tf_op jit(solution)/shard_map/ppermute | solution.py:342
  47.4 1.3 %collective-permute-start.7 = (f32[6,4,72,128]{3,2,1,0:T(8,128)S(1)}, f32[6,4,72,128]{3,2,1,0:T(8,128)}, u32[]{:S(2)}, u32[]{:S(2)}) collective-permute-start(f32[6,4,72,128]{3,2,1,0:T(8,128)S(1)} %get-tuple-element.60.low), channel_id=1, source_target_pairs={{1,0},{2,1},{3,2},{4,3},{5,4},{6,5},{7,6},{8,7},{9,8},{10,9},{11,1... | collective-permute-start | bytes 2654216 | tf_op jit(solution)/shard_map/ppermute | solution.py:695
  48.7 6.0 %walls.4 = (f32[6,128,256]{2,1,0:T(8,128)}, f32[128,256]{1,0:T(8,128)}) custom-call(f32[8,128,128]{2,1,0:T(8,128)} %inverses.1, f32[6,128,256]{2,1,0:T(8,128)} %walls.6, s32[1,256]{1,0:T(1,128)} %bitcast.19), custom_call_target="tpu_custom_call" | custom-call | tf_op jit(solution)/shard_map/walls/pallas_call | solution.py:563
  54.6 1.9 %collective-permute-done.4.south = f32[2,4,72,128]{3,2,1,0:T(8,128)S(1)} collective-permute-done((f32[2,4,72,128]{3,2,1,0:T(8,128)S(1)}, f32[2,4,72,128]{3,2,1,0:T(8,128)S(1)}, u32[]{:S(2)}, u32[]{:S(2)}) %collective-permute-start.4) | collective-permute-done | bytes 294944 | tf_op jit(solution)/shard_map/ppermute | solution.py:342
  56.6 0.6 collective-permute-done.5.north
  57.2 0.0 collective-permute-done.6.south
  57.2 6.3 %gather.1 = (f32[8,512,128]{2,1,0:T(8,128)}, f32[1280,128]{1,0:T(8,128)}) custom-call(f32[2,4,72,128]{3,2,1,0:T(8,128)S(1)} %collective-permute-done.4.south, f32[2,4,72,128]{3,2,1,0:T(8,128)S(1)} %get-tuple-element.64.low, f32[2,4,72,128]{3,2,1,0:T(8,128)S(1)} %get-tuple-element.65.high, f32[2,4,72,128]{3,2,1,0:T(8,128)S(1)} %collective-permute-done.5.north, ...), custom_call_target="tpu_custom_call" | custom-call | tf_op jit(solution)/shard_map/gather/pallas_call | solution.py:494
  63.4 10.6 %all-to-all-start.1 = ((f32[128,1,1280]{2,1,0:T(1,128)}), f32[128,1,1280]{2,1,0:T(1,128)S(1)}, u32[]{:S(2)}, u32[]{:S(2)}) async-start(f32[128,1,1280]{2,1,0:T(1,128)} %bitcast.15), calls=%async_computation.1 | async-start | bytes 1310720 | tf_op jit(solution)/shard_map/all_to_all | solution.py:660
  74.0 0.0 collective-permute-done.7.north
  74.0 12.1 %fields.1 = f32[8,512,128]{2,1,0:T(8,128)} custom-call(f32[6,4,72,128]{3,2,1,0:T(8,128)} %collective-permute-done.6.south, f32[6,4,72,128]{3,2,1,0:T(8,128)S(1)} %get-tuple-element.60.low, f32[6,4,72,128]{3,2,1,0:T(8,128)S(1)} %get-tuple-element.56.high, f32[6,4,72,128]{3,2,1,0:T(8,128)} %collective-permute-done.7.north, ...), custom_call_target="tpu_custom_call", output_to_operand_aliasing={{}: (7, {})} | custom-call | tf_op jit(solution)/shard_map/fields/pallas_call | solution.py:451
  86.2 3.1 %all-to-all-done.1 = f32[128,1,1280]{2,1,0:T(1,128)S(1)} async-done(((f32[128,1,1280]{2,1,0:T(1,128)}), f32[128,1,1280]{2,1,0:T(1,128)S(1)}, u32[]{:S(2)}, u32[]{:S(2)}) %all-to-all-start.1) | async-done | bytes 655392 | tf_op jit(solution)/shard_map/all_to_all | solution.py:660
  89.3 3.1 %final.1 = (f32[128,256]{1,0:T(8,128)}, f32[6,128,256]{2,1,0:T(8,128)}) custom-call(f32[1280,128]{1,0:T(8,128)S(1)} %bitcast.10, f32[128,256]{1,0:T(8,128)} %get-tuple-element.70.code_in, f32[64,256]{1,0:T(8,128)} %facade_in.1, f32[6,256]{1,0:T(8,128)} %coeff_in.1, f32[6,128,256]{2,1,0:T(8,128)} %walls.6, f32[6,128,256]{2,1,0:T(8,128)} %get-tuple-element.71.product, ...), custom_call_target="tpu_custom_call" | custom-call | tf_op jit(solution)/shard_map/final/pallas_call | solution.py:626
  (1 shorter events, 0.0 us)
Async XLA Ops:
  3.3 25.3 %all-to-all-start = ((f32[128,1,768]{2,1,0:T(1,128)}), f32[128,1,768]{2,1,0:T(1,128)S(1)}, u32[]{:S(2)}, u32[]{:S(2)}) async-start(f32[128,1,768]{2,1,0:T(1,128)} %bitcast.16), calls=%async_computation | async-start | bytes 786432 | tf_op jit(solution)/shard_map/all_to_all | solution.py:660
  17.8 6.7 %collective-permute-start = (f32[6,8,8,128]{3,2,1,0:T(8,128)S(1)}, f32[6,8,8,128]{3,2,1,0:T(8,128)S(1)}, u32[]{:S(2)}, u32[]{:S(2)}) collective-permute-start(f32[6,8,8,128]{3,2,1,0:T(8,128)S(1)} %get-tuple-element.42.pack), channel_id=1, source_target_pairs={{0,16},{16,32},{32,48},{48,64},{64,80},{80,96},{96,112},{1,17},{17... | collective-permute-start | bytes 589832 | tf_op jit(solution)/shard_map/ppermute | solution.py:331
  21.4 7.0 %collective-permute-start.1 = (f32[6,8,8,128]{3,2,1,0:T(8,128)S(1)}, f32[6,8,8,128]{3,2,1,0:T(8,128)S(1)}, u32[]{:S(2)}, u32[]{:S(2)}) collective-permute-start(f32[6,8,8,128]{3,2,1,0:T(8,128)S(1)} %get-tuple-element.42.pack), channel_id=1, source_target_pairs={{16,0},{32,16},{48,32},{64,48},{80,64},{96,80},{112,96},{17,1},{33... | collective-permute-start | bytes 589832 | tf_op jit(solution)/shard_map/ppermute | solution.py:331
  28.6 28.5 %collective-permute-start.6 = (f32[6,4,72,128]{3,2,1,0:T(8,128)S(1)}, f32[6,4,72,128]{3,2,1,0:T(8,128)}, u32[]{:S(2)}, u32[]{:S(2)}) collective-permute-start(f32[6,4,72,128]{3,2,1,0:T(8,128)S(1)} %get-tuple-element.56.high), channel_id=1, source_target_pairs={{0,1},{1,2},{2,3},{3,4},{4,5},{5,6},{6,7},{7,8},{8,9},{9,10},{10,1... | collective-permute-start | bytes 2654216 | tf_op jit(solution)/shard_map/ppermute | solution.py:690
  35.7 4.3 %collective-permute-start.2 = (f32[2,8,8,128]{3,2,1,0:T(8,128)S(1)}, f32[2,8,8,128]{3,2,1,0:T(8,128)S(1)}, u32[]{:S(2)}, u32[]{:S(2)}) collective-permute-start(f32[2,8,8,128]{3,2,1,0:T(8,128)S(1)} %get-tuple-element.48.pack), channel_id=1, source_target_pairs={{0,16},{16,32},{32,48},{48,64},{64,80},{80,96},{96,112},{1,17},{17... | collective-permute-start | bytes 196616 | tf_op jit(solution)/shard_map/ppermute | solution.py:331
  37.8 5.6 %collective-permute-start.3 = (f32[2,8,8,128]{3,2,1,0:T(8,128)S(1)}, f32[2,8,8,128]{3,2,1,0:T(8,128)S(1)}, u32[]{:S(2)}, u32[]{:S(2)}) collective-permute-start(f32[2,8,8,128]{3,2,1,0:T(8,128)S(1)} %get-tuple-element.48.pack), channel_id=1, source_target_pairs={{16,0},{32,16},{48,32},{64,48},{80,64},{96,80},{112,96},{17,1},{33... | collective-permute-start | bytes 196616 | tf_op jit(solution)/shard_map/ppermute | solution.py:331
  43.4 13.1 %collective-permute-start.4 = (f32[2,4,72,128]{3,2,1,0:T(8,128)S(1)}, f32[2,4,72,128]{3,2,1,0:T(8,128)S(1)}, u32[]{:S(2)}, u32[]{:S(2)}) collective-permute-start(f32[2,4,72,128]{3,2,1,0:T(8,128)S(1)} %get-tuple-element.65.high), channel_id=1, source_target_pairs={{0,1},{1,2},{2,3},{3,4},{4,5},{5,6},{6,7},{7,8},{8,9},{9,10},{10,1... | collective-permute-start | bytes 884744 | tf_op jit(solution)/shard_map/ppermute | solution.py:342
  46.1 11.1 %collective-permute-start.5 = (f32[2,4,72,128]{3,2,1,0:T(8,128)S(1)}, f32[2,4,72,128]{3,2,1,0:T(8,128)S(1)}, u32[]{:S(2)}, u32[]{:S(2)}) collective-permute-start(f32[2,4,72,128]{3,2,1,0:T(8,128)S(1)} %get-tuple-element.64.low), channel_id=1, source_target_pairs={{1,0},{2,1},{3,2},{4,3},{5,4},{6,5},{7,6},{8,7},{9,8},{10,9},{11,1... | collective-permute-start | bytes 884744 | tf_op jit(solution)/shard_map/ppermute | solution.py:342
  47.4 26.7 %collective-permute-start.7 = (f32[6,4,72,128]{3,2,1,0:T(8,128)S(1)}, f32[6,4,72,128]{3,2,1,0:T(8,128)}, u32[]{:S(2)}, u32[]{:S(2)}) collective-permute-start(f32[6,4,72,128]{3,2,1,0:T(8,128)S(1)} %get-tuple-element.60.low), channel_id=1, source_target_pairs={{1,0},{2,1},{3,2},{4,3},{5,4},{6,5},{7,6},{8,7},{9,8},{10,9},{11,1... | collective-permute-start | bytes 2654216 | tf_op jit(solution)/shard_map/ppermute | solution.py:695
  63.4 25.8 %all-to-all-start.1 = ((f32[128,1,1280]{2,1,0:T(1,128)}), f32[128,1,1280]{2,1,0:T(1,128)S(1)}, u32[]{:S(2)}, u32[]{:S(2)}) async-start(f32[128,1,1280]{2,1,0:T(1,128)} %bitcast.15), calls=%async_computation.1 | async-start | bytes 1310720 | tf_op jit(solution)/shard_map/all_to_all | solution.py:660

commit v4 on v3

--- a/solution.py
+++ b/solution.py
@@ -133,7 +133,11 @@
 def emit_row(f, y, field, low, high, pack):
     dst = low if y < HALO else high
     dst[f, y % HALO, :LEV, :] = field
-    pack[f, y] = pack_row([field[8 * i : 8 * i + 8] for i in range(8)])
+    row = pack_row([field[8 * i : 8 * i + 8] for i in range(8)])
+    if y < HALO:
+        pack[f, y] = row
+    else:
+        pack[f, y - HALO] = pack[f, y - HALO] + pltpu.roll(row, 8, 1)
 
 
 def prep_kernel(courant_in, canopy, low, high, pack, coef, coef_strip, field, courant, sems):
@@ -177,7 +181,7 @@
 
 
 def pack_shape(n):
-    return jax.ShapeDtypeStruct((n, ROWS_Y, STRIP, LANES), f32)
+    return jax.ShapeDtypeStruct((n, HALO, STRIP, LANES), f32)
 
 
 def half_spec(n):
@@ -193,7 +197,7 @@
         out_specs=[
             half_spec(n),
             half_spec(n),
-            whole((n, ROWS_Y, STRIP, LANES)),
+            whole((n, HALO, STRIP, LANES)),
             whole((5, LEV, LANES)),
             whole((5, STRIP, LANES)),
         ],
@@ -270,7 +274,7 @@
             REMOTE,
             half_spec(NEAR),
             half_spec(NEAR),
-            whole((NEAR, ROWS_Y, STRIP, LANES)),
+            whole((NEAR, HALO, STRIP, LANES)),
         ],
         out_shape=[
             pltpu.HBM((ROWS_Y * LANES, CAP * DEV), bf16),
@@ -295,18 +299,18 @@
     slot = lane_slot() % 16
     for f in range(pack.shape[0]):
         for y in range(ROWS_Y):
-            strip = jnp.where(
-                slot < 4,
-                pltpu.roll(west[f, y], LANES - 8, 1),
-                jnp.where(slot < 12, pack[f, y], pltpu.roll(east[f, y], 8, 1)),
-            )
+            w, own, e = west[f, y % HALO], pack[f, y % HALO], east[f, y % HALO]
+            if y < HALO:
+                w, e = pltpu.roll(w, LANES - 8, 1), pltpu.roll(e, 8, 1)
+            else:
+                w, own = pltpu.roll(w, LANES - 16, 1), pltpu.roll(own, LANES - 8, 1)
             dst = low if y < HALO else high
-            dst[f, y % HALO] = strip
+            dst[f, y % HALO] = jnp.where(slot < 4, w, jnp.where(slot < 12, own, e))
 
 
 def merge(pack, west, east, low, high):
     n = pack.shape[0]
-    pack_spec = whole((n, ROWS_Y, STRIP, LANES))
+    pack_spec = whole((n, HALO, STRIP, LANES))
     strip_spec = pl.BlockSpec((n, HALO, STRIP, LANES), lambda i: (0, 0, LEV // STRIP, 0))
     anywhere = pl.BlockSpec(memory_space=pl.ANY)
     return pl.pallas_call(
@@ -539,15 +543,15 @@
         chosen = jnp.where(package[...] == p, jnp.broadcast_to(inv[:, 0:1], (n, NB)), chosen)
     column[...] = chosen
 
+    masks = [jnp.where(package[...] == p, 1.0, 0.0) for p in range(PKG)]
+
     def surface(s, carry):
         load(s).wait()
-        w = wall_v[s]
-        w_hi = w.astype(bf16).astype(f32)
-        w_lo = w - w_hi
+        w_hi, w_lo = halves(wall_v[s])
         for p in range(PKG):
-            mine = package[...] == p
-            b_hi[p * n : (p + 1) * n, :] = jnp.where(mine, w_hi, 0.0).astype(bf16)
-            b_lo[p * n : (p + 1) * n, :] = jnp.where(mine, w_lo, 0.0).astype(bf16)
+            mine = jnp.broadcast_to(masks[p], (n, NB)).astype(bf16)
+            b_hi[p * n : (p + 1) * n, :] = w_hi * mine
+            b_lo[p * n : (p + 1) * n, :] = w_lo * mine
         both = mm(a[...], b_hi[...], NN)
         out[s] = both[:n] + both[n:] + mm(a[:n, :], b_lo[...], NN)
         save(s).start()

time: 93 us -> 92.2 us (level)
    ppermute x4, waiting for transfers between devices: 8.33 us -> 7.07 us  [across_x(): west, east = (lax.ppermute(pack, 'gx', up), lax.ppermute(pack, 'gx', down))]
  transfers between devices with their start and end apart: 10 -> 10, of which waited for: 6 -> 5; matrix products, arithmetic and copies ran while one was open for 0% -> 0% of each run, Pallas kernels for 33% -> 34%
where the time goes in v4:
time: 92.2 us; the launch traced here: 91.3 us
  starting transfers between devices  40.6 us (44%)
  Pallas kernels  36.7 us (40%)
  waiting for transfers between devices  13.3 us (14%)
    all_to_all x2, starting transfers between devices, transpose_all(): lax.all_to_all(x.reshape(DEV, 1, rows * LANES), ('gx', 'gy'), split_axis=...  21.5 us
    pallas_call x1, Pallas kernels, fields(): pl.pallas_call(fields_kernel, grid=(n,), in_specs=[quarter_spec(1) for _...  12.1 us
    ppermute x4, starting transfers between devices, across_x(): west, east = (lax.ppermute(pack, 'gx', up), lax.ppermute(pack, 'gx', down))  9.91 us
    ppermute x4, waiting for transfers between devices, across_x(): west, east = (lax.ppermute(pack, 'gx', up), lax.ppermute(pack, 'gx', down))  7.07 us
    pallas_call x1, Pallas kernels, gather(): pl.pallas_call(gather_kernel, grid=(1,), in_specs=[quarter_spec(NEAR) for...  6.26 us
    pallas_call x1, Pallas kernels, walls_product(): pl.pallas_call(walls_kernel, grid=(1,), in_specs=[REMOTE, REMOTE, whole((...  5.95 us
    ppermute x1, starting transfers between devices, body(): south = lax.ppermute(high, 'gy', up)  3.96 us
    ppermute x2, starting transfers between devices, across_y(): south, north = (lax.ppermute(high, 'gy', up), lax.ppermute(low, 'gy', down))  3.9 us
  transfers between devices with their start and end apart: 10, of which 5 were waited for; matrix products, arithmetic and copies ran while one was open for 0% of the time, Pallas kernels for 34%

profile of v4, /device:TPU:1, one launch (start us, length us, event | category | flops | bytes accessed | tf_op | source)
XLA Modules:
  0.0 91.3 jit_solution(3080078326078983357)
XLA Ops:
  0.6 2.7 %payload.1 = (f32[768,128]{1,0:T(8,128)}, f32[128,256]{1,0:T(8,128)}) custom-call(s32[1,256]{1,0:T(1,128)} %bitcast.18, s32[8,256]{1,0:T(8,128)} %bitcast.17, f32[6,256]{1,0:T(8,128)} %coeff_in.1, f32[6,128,256]{2,1,0:T(8,128)} %walls.6, f32[64,256]{1,0:T(8,128)} %facade_in.1), custom_call_target="tpu_custom_call" | custom-call | tf_op jit(solution)/shard_map/payload/pallas_call | solution.py:95
  3.3 11.5 %all-to-all-start = ((f32[128,1,768]{2,1,0:T(1,128)}), f32[128,1,768]{2,1,0:T(1,128)S(1)}, u32[]{:S(2)}, u32[]{:S(2)}) async-start(f32[128,1,768]{2,1,0:T(1,128)} %bitcast.16), calls=%async_computation | async-start | bytes 786432 | tf_op jit(solution)/shard_map/all_to_all | solution.py:664
  14.8 3.2 %prep.1 = (f32[6,4,72,128]{3,2,1,0:T(8,128)S(1)}, f32[6,4,72,128]{3,2,1,0:T(8,128)S(1)}, f32[6,4,8,128]{3,2,1,0:T(8,128)S(1)}, f32[5,64,128]{2,1,0:T(8,128)}, f32[5,8,128]{2,1,0:T(8,128)}) custom-call(f32[2,64]{1,0:T(2,128)} %courant_in.1, f32[8,512,128]{2,1,0:T(8,128)} %bitcast.12), custom_call_target="tpu_custom_call" | custom-call | tf_op jit(solution)/shard_map/prep/pallas_call | solution.py:193
  18.0 3.7 %collective-permute-start = (f32[6,4,8,128]{3,2,1,0:T(8,128)S(1)}, f32[6,4,8,128]{3,2,1,0:T(8,128)S(1)}, u32[]{:S(2)}, u32[]{:S(2)}) collective-permute-start(f32[6,4,8,128]{3,2,1,0:T(8,128)S(1)} %get-tuple-element.42.pack), channel_id=1, source_target_pairs={{0,16},{16,32},{32,48},{48,64},{64,80},{80,96},{96,112},{1,17},{17... | collective-permute-start | bytes 294920 | tf_op jit(solution)/shard_map/ppermute | solution.py:335
  21.7 1.9 %collective-permute-start.1 = (f32[6,4,8,128]{3,2,1,0:T(8,128)S(1)}, f32[6,4,8,128]{3,2,1,0:T(8,128)S(1)}, u32[]{:S(2)}, u32[]{:S(2)}) collective-permute-start(f32[6,4,8,128]{3,2,1,0:T(8,128)S(1)} %get-tuple-element.42.pack), channel_id=1, source_target_pairs={{16,0},{32,16},{48,32},{64,48},{80,64},{96,80},{112,96},{17,1},{33... | collective-permute-start | bytes 294920 | tf_op jit(solution)/shard_map/ppermute | solution.py:335
  23.6 0.0 collective-permute-done.west
  23.7 4.1 %collective-permute-done.1.east = f32[6,4,8,128]{3,2,1,0:T(8,128)S(1)} collective-permute-done((f32[6,4,8,128]{3,2,1,0:T(8,128)S(1)}, f32[6,4,8,128]{3,2,1,0:T(8,128)S(1)}, u32[]{:S(2)}, u32[]{:S(2)}) %collective-permute-start.1) | collective-permute-done | bytes 98336 | tf_op jit(solution)/shard_map/ppermute | solution.py:335
  27.7 0.2 merge.2
  27.9 0.0 all-to-all-done
  27.9 4.0 %collective-permute-start.6 = (f32[6,4,72,128]{3,2,1,0:T(8,128)S(1)}, f32[6,4,72,128]{3,2,1,0:T(8,128)}, u32[]{:S(2)}, u32[]{:S(2)}) collective-permute-start(f32[6,4,72,128]{3,2,1,0:T(8,128)S(1)} %get-tuple-element.56.high), channel_id=1, source_target_pairs={{0,1},{1,2},{2,3},{3,4},{4,5},{5,6},{6,7},{7,8},{8,9},{9,10},{10,1... | collective-permute-start | bytes 2654216 | tf_op jit(solution)/shard_map/ppermute | solution.py:694
  31.9 3.1 %scatter.1 = (bf16[1024,1280]{1,0:T(8,128)(2,1)}, f32[2,4,72,128]{3,2,1,0:T(8,128)S(1)}, f32[2,4,72,128]{3,2,1,0:T(8,128)S(1)}, f32[2,4,8,128]{3,2,1,0:T(8,128)S(1)}) custom-call(f32[768,128]{1,0:T(8,128)S(1)} %bitcast.11, f32[8,512,128]{2,1,0:T(8,128)} %bitcast.13), custom_call_target="tpu_custom_call" | custom-call | tf_op jit(solution)/shard_map/scatter/pallas_call | solution.py:269
  34.9 2.1 %collective-permute-start.2 = (f32[2,4,8,128]{3,2,1,0:T(8,128)S(1)}, f32[2,4,8,128]{3,2,1,0:T(8,128)S(1)}, u32[]{:S(2)}, u32[]{:S(2)}) collective-permute-start(f32[2,4,8,128]{3,2,1,0:T(8,128)S(1)} %get-tuple-element.48.pack), channel_id=1, source_target_pairs={{0,16},{16,32},{32,48},{48,64},{64,80},{80,96},{96,112},{1,17},{17... | collective-permute-start | bytes 98312 | tf_op jit(solution)/shard_map/ppermute | solution.py:335
  37.1 2.2 %collective-permute-start.3 = (f32[2,4,8,128]{3,2,1,0:T(8,128)S(1)}, f32[2,4,8,128]{3,2,1,0:T(8,128)S(1)}, u32[]{:S(2)}, u32[]{:S(2)}) collective-permute-start(f32[2,4,8,128]{3,2,1,0:T(8,128)S(1)} %get-tuple-element.48.pack), channel_id=1, source_target_pairs={{16,0},{32,16},{48,32},{64,48},{80,64},{96,80},{112,96},{17,1},{33... | collective-permute-start | bytes 98312 | tf_op jit(solution)/shard_map/ppermute | solution.py:335
  39.3 0.0 collective-permute-done.2.west
  39.3 3.0 %collective-permute-done.3.east = f32[2,4,8,128]{3,2,1,0:T(8,128)S(1)} collective-permute-done((f32[2,4,8,128]{3,2,1,0:T(8,128)S(1)}, f32[2,4,8,128]{3,2,1,0:T(8,128)S(1)}, u32[]{:S(2)}, u32[]{:S(2)}) %collective-permute-start.3) | collective-permute-done | bytes 32800 | tf_op jit(solution)/shard_map/ppermute | solution.py:335
  42.3 0.1 merge.3
  42.4 2.6 %collective-permute-start.4 = (f32[2,4,72,128]{3,2,1,0:T(8,128)S(1)}, f32[2,4,72,128]{3,2,1,0:T(8,128)S(1)}, u32[]{:S(2)}, u32[]{:S(2)}) collective-permute-start(f32[2,4,72,128]{3,2,1,0:T(8,128)S(1)} %get-tuple-element.65.high), channel_id=1, source_target_pairs={{0,1},{1,2},{2,3},{3,4},{4,5},{5,6},{6,7},{7,8},{8,9},{9,10},{10,1... | collective-permute-start | bytes 884744 | tf_op jit(solution)/shard_map/ppermute | solution.py:346
  45.0 1.3 %collective-permute-start.5 = (f32[2,4,72,128]{3,2,1,0:T(8,128)S(1)}, f32[2,4,72,128]{3,2,1,0:T(8,128)S(1)}, u32[]{:S(2)}, u32[]{:S(2)}) collective-permute-start(f32[2,4,72,128]{3,2,1,0:T(8,128)S(1)} %get-tuple-element.64.low), channel_id=1, source_target_pairs={{1,0},{2,1},{3,2},{4,3},{5,4},{6,5},{7,6},{8,7},{9,8},{10,9},{11,1... | collective-permute-start | bytes 884744 | tf_op jit(solution)/shard_map/ppermute | solution.py:346
  46.3 1.3 %collective-permute-start.7 = (f32[6,4,72,128]{3,2,1,0:T(8,128)S(1)}, f32[6,4,72,128]{3,2,1,0:T(8,128)}, u32[]{:S(2)}, u32[]{:S(2)}) collective-permute-start(f32[6,4,72,128]{3,2,1,0:T(8,128)S(1)} %get-tuple-element.60.low), channel_id=1, source_target_pairs={{1,0},{2,1},{3,2},{4,3},{5,4},{6,5},{7,6},{8,7},{9,8},{10,9},{11,1... | collective-permute-start | bytes 2654216 | tf_op jit(solution)/shard_map/ppermute | solution.py:699
  47.6 6.0 %walls.4 = (f32[6,128,256]{2,1,0:T(8,128)}, f32[128,256]{1,0:T(8,128)}) custom-call(f32[8,128,128]{2,1,0:T(8,128)} %inverses.1, f32[6,128,256]{2,1,0:T(8,128)} %walls.6, s32[1,256]{1,0:T(1,128)} %bitcast.19), custom_call_target="tpu_custom_call" | custom-call | tf_op jit(solution)/shard_map/walls/pallas_call | solution.py:567
  53.6 3.1 %collective-permute-done.4.south = f32[2,4,72,128]{3,2,1,0:T(8,128)S(1)} collective-permute-done((f32[2,4,72,128]{3,2,1,0:T(8,128)S(1)}, f32[2,4,72,128]{3,2,1,0:T(8,128)S(1)}, u32[]{:S(2)}, u32[]{:S(2)}) %collective-permute-start.4) | collective-permute-done | bytes 294944 | tf_op jit(solution)/shard_map/ppermute | solution.py:346
  56.7 0.0 collective-permute-done.5.north
  56.7 0.0 collective-permute-done.6.south
  56.7 6.3 %gather.1 = (f32[8,512,128]{2,1,0:T(8,128)}, f32[1280,128]{1,0:T(8,128)}) custom-call(f32[2,4,72,128]{3,2,1,0:T(8,128)S(1)} %collective-permute-done.4.south, f32[2,4,72,128]{3,2,1,0:T(8,128)S(1)} %get-tuple-element.64.low, f32[2,4,72,128]{3,2,1,0:T(8,128)S(1)} %get-tuple-element.65.high, f32[2,4,72,128]{3,2,1,0:T(8,128)S(1)} %collective-permute-done.5.north, ...), custom_call_target="tpu_custom_call" | custom-call | tf_op jit(solution)/shard_map/gather/pallas_call | solution.py:498
  62.9 10.0 %all-to-all-start.1 = ((f32[128,1,1280]{2,1,0:T(1,128)}), f32[128,1,1280]{2,1,0:T(1,128)S(1)}, u32[]{:S(2)}, u32[]{:S(2)}) async-start(f32[128,1,1280]{2,1,0:T(1,128)} %bitcast.15), calls=%async_computation.1 | async-start | bytes 1310720 | tf_op jit(solution)/shard_map/all_to_all | solution.py:664
  73.0 0.3 collective-permute-done.7.north
  73.2 12.1 %fields.1 = f32[8,512,128]{2,1,0:T(8,128)} custom-call(f32[6,4,72,128]{3,2,1,0:T(8,128)} %collective-permute-done.6.south, f32[6,4,72,128]{3,2,1,0:T(8,128)S(1)} %get-tuple-element.60.low, f32[6,4,72,128]{3,2,1,0:T(8,128)S(1)} %get-tuple-element.56.high, f32[6,4,72,128]{3,2,1,0:T(8,128)} %collective-permute-done.7.north, ...), custom_call_target="tpu_custom_call", output_to_operand_aliasing={{}: (7, {})} | custom-call | tf_op jit(solution)/shard_map/fields/pallas_call | solution.py:455
  85.3 2.9 %all-to-all-done.1 = f32[128,1,1280]{2,1,0:T(1,128)S(1)} async-done(((f32[128,1,1280]{2,1,0:T(1,128)}), f32[128,1,1280]{2,1,0:T(1,128)S(1)}, u32[]{:S(2)}, u32[]{:S(2)}) %all-to-all-start.1) | async-done | bytes 655392 | tf_op jit(solution)/shard_map/all_to_all | solution.py:664
  88.2 3.1 %final.1 = (f32[128,256]{1,0:T(8,128)}, f32[6,128,256]{2,1,0:T(8,128)}) custom-call(f32[1280,128]{1,0:T(8,128)S(1)} %bitcast.10, f32[128,256]{1,0:T(8,128)} %get-tuple-element.70.code_in, f32[64,256]{1,0:T(8,128)} %facade_in.1, f32[6,256]{1,0:T(8,128)} %coeff_in.1, f32[6,128,256]{2,1,0:T(8,128)} %walls.6, f32[6,128,256]{2,1,0:T(8,128)} %get-tuple-element.71.product, ...), custom_call_target="tpu_custom_call" | custom-call | tf_op jit(solution)/shard_map/final/pallas_call | solution.py:630
  (1 shorter events, 0.0 us)
Async XLA Ops:
  3.3 24.6 %all-to-all-start = ((f32[128,1,768]{2,1,0:T(1,128)}), f32[128,1,768]{2,1,0:T(1,128)S(1)}, u32[]{:S(2)}, u32[]{:S(2)}) async-start(f32[128,1,768]{2,1,0:T(1,128)} %bitcast.16), calls=%async_computation | async-start | bytes 786432 | tf_op jit(solution)/shard_map/all_to_all | solution.py:664
  18.0 5.6 %collective-permute-start = (f32[6,4,8,128]{3,2,1,0:T(8,128)S(1)}, f32[6,4,8,128]{3,2,1,0:T(8,128)S(1)}, u32[]{:S(2)}, u32[]{:S(2)}) collective-permute-start(f32[6,4,8,128]{3,2,1,0:T(8,128)S(1)} %get-tuple-element.42.pack), channel_id=1, source_target_pairs={{0,16},{16,32},{32,48},{48,64},{64,80},{80,96},{96,112},{1,17},{17... | collective-permute-start | bytes 294920 | tf_op jit(solution)/shard_map/ppermute | solution.py:335
  21.7 6.0 %collective-permute-start.1 = (f32[6,4,8,128]{3,2,1,0:T(8,128)S(1)}, f32[6,4,8,128]{3,2,1,0:T(8,128)S(1)}, u32[]{:S(2)}, u32[]{:S(2)}) collective-permute-start(f32[6,4,8,128]{3,2,1,0:T(8,128)S(1)} %get-tuple-element.42.pack), channel_id=1, source_target_pairs={{16,0},{32,16},{48,32},{64,48},{80,64},{96,80},{112,96},{17,1},{33... | collective-permute-start | bytes 294920 | tf_op jit(solution)/shard_map/ppermute | solution.py:335
  27.9 28.8 %collective-permute-start.6 = (f32[6,4,72,128]{3,2,1,0:T(8,128)S(1)}, f32[6,4,72,128]{3,2,1,0:T(8,128)}, u32[]{:S(2)}, u32[]{:S(2)}) collective-permute-start(f32[6,4,72,128]{3,2,1,0:T(8,128)S(1)} %get-tuple-element.56.high), channel_id=1, source_target_pairs={{0,1},{1,2},{2,3},{3,4},{4,5},{5,6},{6,7},{7,8},{8,9},{9,10},{10,1... | collective-permute-start | bytes 2654216 | tf_op jit(solution)/shard_map/ppermute | solution.py:694
  34.9 4.3 %collective-permute-start.2 = (f32[2,4,8,128]{3,2,1,0:T(8,128)S(1)}, f32[2,4,8,128]{3,2,1,0:T(8,128)S(1)}, u32[]{:S(2)}, u32[]{:S(2)}) collective-permute-start(f32[2,4,8,128]{3,2,1,0:T(8,128)S(1)} %get-tuple-element.48.pack), channel_id=1, source_target_pairs={{0,16},{16,32},{32,48},{48,64},{64,80},{80,96},{96,112},{1,17},{17... | collective-permute-start | bytes 98312 | tf_op jit(solution)/shard_map/ppermute | solution.py:335
  37.1 5.2 %collective-permute-start.3 = (f32[2,4,8,128]{3,2,1,0:T(8,128)S(1)}, f32[2,4,8,128]{3,2,1,0:T(8,128)S(1)}, u32[]{:S(2)}, u32[]{:S(2)}) collective-permute-start(f32[2,4,8,128]{3,2,1,0:T(8,128)S(1)} %get-tuple-element.48.pack), channel_id=1, source_target_pairs={{16,0},{32,16},{48,32},{64,48},{80,64},{96,80},{112,96},{17,1},{33... | collective-permute-start | bytes 98312 | tf_op jit(solution)/shard_map/ppermute | solution.py:335
  42.4 14.3 %collective-permute-start.4 = (f32[2,4,72,128]{3,2,1,0:T(8,128)S(1)}, f32[2,4,72,128]{3,2,1,0:T(8,128)S(1)}, u32[]{:S(2)}, u32[]{:S(2)}) collective-permute-start(f32[2,4,72,128]{3,2,1,0:T(8,128)S(1)} %get-tuple-element.65.high), channel_id=1, source_target_pairs={{0,1},{1,2},{2,3},{3,4},{4,5},{5,6},{6,7},{7,8},{8,9},{9,10},{10,1... | collective-permute-start | bytes 884744 | tf_op jit(solution)/shard_map/ppermute | solution.py:346
  45.0 11.7 %collective-permute-start.5 = (f32[2,4,72,128]{3,2,1,0:T(8,128)S(1)}, f32[2,4,72,128]{3,2,1,0:T(8,128)S(1)}, u32[]{:S(2)}, u32[]{:S(2)}) collective-permute-start(f32[2,4,72,128]{3,2,1,0:T(8,128)S(1)} %get-tuple-element.64.low), channel_id=1, source_target_pairs={{1,0},{2,1},{3,2},{4,3},{5,4},{6,5},{7,6},{8,7},{9,8},{10,9},{11,1... | collective-permute-start | bytes 884744 | tf_op jit(solution)/shard_map/ppermute | solution.py:346
  46.3 26.9 %collective-permute-start.7 = (f32[6,4,72,128]{3,2,1,0:T(8,128)S(1)}, f32[6,4,72,128]{3,2,1,0:T(8,128)}, u32[]{:S(2)}, u32[]{:S(2)}) collective-permute-start(f32[6,4,72,128]{3,2,1,0:T(8,128)S(1)} %get-tuple-element.60.low), channel_id=1, source_target_pairs={{1,0},{2,1},{3,2},{4,3},{5,4},{6,5},{7,6},{8,7},{9,8},{10,9},{11,1... | collective-permute-start | bytes 2654216 | tf_op jit(solution)/shard_map/ppermute | solution.py:699
  62.9 25.3 %all-to-all-start.1 = ((f32[128,1,1280]{2,1,0:T(1,128)}), f32[128,1,1280]{2,1,0:T(1,128)S(1)}, u32[]{:S(2)}, u32[]{:S(2)}) async-start(f32[128,1,1280]{2,1,0:T(1,128)} %bitcast.15), calls=%async_computation.1 | async-start | bytes 1310720 | tf_op jit(solution)/shard_map/all_to_all | solution.py:664

commit v5 on v4

--- a/solution.py
+++ b/solution.py
@@ -362,6 +362,36 @@
             return value * edge[1]
         return value
 
+    table, sides, spread = ends
+    starts = [0, 14, 26, 36]
+
+    def strip(step, row):
+        if step == 1:
+            return parts[row // HALO][f, row % HALO, LEV : LEV + STRIP, :]
+        return strips[(step + 1) % 2, row]
+
+    for step in range(1, SUB + 1):
+        c0, cw, ce, cs, cn = (coef_strip[k] for k in range(5))
+        here, after = strip(step, step - 1), strip(step, step)
+        for row in range(step, total - step):
+            before, here, after = here, after, strip(step, row + 1)
+            at = 8 * (starts[step - 1] + row - step)
+            table[at : at + 8, :] = jnp.where(slot == 3, here, pltpu.roll(here, LANES - 10, 1))
+            if step == SUB:
+                continue
+            down = pltpu.roll(here, 1, 0)
+            below = jnp.where(sub == 0, jnp.where(lane < 16, here, pltpu.roll(down, 16, 1)), down)
+            lift = pltpu.roll(here, 7, 0)
+            above = jnp.where(sub == 7, jnp.where(lane >= LANES - 16, here, pltpu.roll(lift, LANES - 16, 1)), lift)
+            value = (
+                (c0 * here + cw * pltpu.roll(here, 1, 1))
+                + (ce * pltpu.roll(here, LANES - 1, 1) + cs * before)
+                + (cn * after + vertical_rate * (above + below))
+            )
+            strips[step % 2, row] = keep(row, value * inside)
+    hi, lo = halves(table[...])
+    sides[...] = mm(jnp.concatenate([hi, lo], axis=1), spread[...], NN)
+
     for step in range(1, SUB + 1):
         old, new = (step + 1) % 2, step % 2
 
@@ -370,20 +400,11 @@
                 return parts[row // HALO][f, row % HALO, start : start + 8, :]
             return buf[old, row, start : start + 8, :]
 
-        def strip(row):
-            if step == 1:
-                return parts[row // HALO][f, row % HALO, LEV : LEV + STRIP, :]
-            return strips[old, row]
-
-        rows = range(step, total - step)
-        for row in rows:
-            side = strip(row)
-            ends[row] = jnp.where(slot == 3, side, pltpu.roll(side, LANES - 10, 1))
         for i in range(8):
             at = 8 * i
             c0, cw, ce, cs, cn = (coef[k, at : at + 8, :] for k in range(5))
             here, after = main(step - 1, at), main(step, at)
-            for row in rows:
+            for row in range(step, total - step):
                 before, here, after = here, after, main(row + 1, at)
                 if i == 0:
                     below = jnp.where(sub == 0, here, pltpu.roll(here, 1, 0))
@@ -393,7 +414,8 @@
                     above = jnp.where(sub == 7, here, pltpu.roll(here, 7, 0))
                 else:
                     above = pltpu.roll(jnp.where(sub == 0, main(row, at + 8), here), 7, 0)
-                side = pltpu.roll(ends[row], (LANES - 16 * i - 3) % LANES, 1)
+                line = 8 * (starts[step - 1] + row - step)
+                side = sides[line : line + 8, i * LANES : (i + 1) * LANES]
                 left = jnp.where(first, side, pltpu.roll(here, 1, 1))
                 right = jnp.where(last, side, pltpu.roll(here, LANES - 1, 1))
                 value = (
@@ -405,22 +427,16 @@
                     put(row - HALO, at, value)
                 else:
                     buf[new, row, at : at + 8, :] = keep(row, value)
-        if step == SUB:
-            break
-        c0, cw, ce, cs, cn = (coef_strip[k] for k in range(5))
-        here, after = strip(step - 1), strip(step)
-        for row in rows:
-            before, here, after = here, after, strip(row + 1)
-            down = pltpu.roll(here, 1, 0)
-            below = jnp.where(sub == 0, jnp.where(lane < 16, here, pltpu.roll(down, 16, 1)), down)
-            lift = pltpu.roll(here, 7, 0)
-            above = jnp.where(sub == 7, jnp.where(lane >= LANES - 16, here, pltpu.roll(lift, LANES - 16, 1)), lift)
-            value = (
-                (c0 * here + cw * pltpu.roll(here, 1, 1))
-                + (ce * pltpu.roll(here, LANES - 1, 1) + cs * before)
-                + (cn * after + vertical_rate * (above + below))
-            )
-            strips[new, row] = keep(row, value * inside)
+
+
+def fill_spread(spread):
+    shape = (2 * LANES, 8 * LANES)
+    src = lax.broadcasted_iota(jnp.int32, shape, 0) & (LANES - 1)
+    col = lax.broadcasted_iota(jnp.int32, shape, 1)
+    lane = col & (LANES - 1)
+    base = lax.shift_right_logical(col, jnp.full_like(col, 7)) * 16
+    hit = ((lane == 0) & (src == base + 3)) | ((lane == LANES - 1) & (src == base + 2))
+    spread[...] = jnp.where(hit, 1.0, 0.0).astype(bf16)
 
 
 def quarter_spec(n):
@@ -428,9 +444,11 @@
 
 
 STENCIL_SCRATCH = [
-    (2, ROWS_Y + 2 * HALO, LEV, LANES),
-    (2, ROWS_Y + 2 * HALO, STRIP, LANES),
-    (ROWS_Y + 2 * HALO, STRIP, LANES),
+    pltpu.VMEM((2, ROWS_Y + 2 * HALO, LEV, LANES), f32),
+    pltpu.VMEM((2, ROWS_Y + 2 * HALO, STRIP, LANES), f32),
+    pltpu.VMEM((8 * 44, LANES), f32),
+    pltpu.VMEM((8 * 44, 8 * LANES), f32),
+    pltpu.VMEM((2 * LANES, 8 * LANES), bf16),
 ]
 
 
@@ -442,7 +460,11 @@
     ]
 
 
-def fields_kernel(south, low, high, north, coef, coef_strip, edge, into, out, buf, strips, ends):
+def fields_kernel(south, low, high, north, coef, coef_strip, edge, into, out, buf, strips, *ends):
+    @pl.when(pl.program_id(0) == 0)
+    def _():
+        fill_spread(ends[2])
+
     def put(y, at, value):
         out[0, pl.ds(at * ROWS_Y + y, 8, stride=ROWS_Y), :] = value
 
@@ -458,7 +480,7 @@
         in_specs=[quarter_spec(1) for _ in parts] + coef_specs() + [pl.BlockSpec(memory_space=pltpu.HBM)],
         out_specs=pl.BlockSpec((1, LEV * ROWS_Y, LANES), lambda i: (i + NEAR, 0, 0)),
         out_shape=pltpu.HBM(into.shape, f32),
-        scratch_shapes=[pltpu.VMEM(s, f32) for s in STENCIL_SCRATCH],
+        scratch_shapes=STENCIL_SCRATCH,
         input_output_aliases={len(operands) - 1: 0},
         compiler_params=params(),
         name="fields",
@@ -466,7 +488,8 @@
 
 
 def gather_kernel(south, low, high, north, coef, coef_strip, edge, counts_in, fields_out, back, *scratch):
-    buf, strips, ends, table, counts, out, sems = scratch
+    buf, strips, *ends, table, counts, out, sems = scratch
+    fill_spread(ends[2])
     fetch = pltpu.make_async_copy(counts_in, counts, sems.at[0])
     fetch.start()
     save = pltpu.make_async_copy(out, fields_out.at[pl.ds(0, NEAR)], sems.at[1])
@@ -507,7 +530,7 @@
             pltpu.HBM((8, LEV * ROWS_Y, LANES), f32),
             pltpu.HBM((DEV * CAP, LANES), f32),
         ],
-        scratch_shapes=[pltpu.VMEM(s, f32) for s in STENCIL_SCRATCH]
+        scratch_shapes=STENCIL_SCRATCH
         + [
             pltpu.VMEM((4 * LEV, ROWS_Y * LANES), bf16),
             pltpu.VMEM((ROWS_Y * LANES, CAP * DEV), bf16),

time: 92.2 us -> 91.5 us (level)
  Pallas kernels: 36.7 us -> 34 us
  waiting for transfers between devices: 13.3 us -> 15.5 us
    pallas_call x1, Pallas kernels: 12.1 us -> 9.93 us  [fields(): pl.pallas_call(fields_kernel, grid=(n,), in_specs=[quarter_spec(1) for _...]
    all_to_all x2, waiting for transfers between devices: 2.86 us -> 4.63 us  [transpose_all(): lax.all_to_all(x.reshape(DEV, 1, rows * LANES), ('gx', 'gy'), split_axis=...]
  transfers between devices with their start and end apart: 10 -> 10, of which waited for: 5 -> 5; matrix products, arithmetic and copies ran while one was open for 0% -> 0% of each run, Pallas kernels for 34% -> 31%
where the time goes in v5:
time: 91.5 us; the launch traced here: 90.9 us
  starting transfers between devices  40.6 us (44%)
  Pallas kernels  34 us (37%)
  waiting for transfers between devices  15.5 us (17%)
    all_to_all x2, starting transfers between devices, transpose_all(): lax.all_to_all(x.reshape(DEV, 1, rows * LANES), ('gx', 'gy'), split_axis=...  21.5 us
    pallas_call x1, Pallas kernels, fields(): pl.pallas_call(fields_kernel, grid=(n,), in_specs=[quarter_spec(1) for _...  9.93 us
    ppermute x4, starting transfers between devices, across_x(): west, east = (lax.ppermute(pack, 'gx', up), lax.ppermute(pack, 'gx', down))  9.91 us
    ppermute x4, waiting for transfers between devices, across_x(): west, east = (lax.ppermute(pack, 'gx', up), lax.ppermute(pack, 'gx', down))  7.07 us
    pallas_call x1, Pallas kernels, walls_product(): pl.pallas_call(walls_kernel, grid=(1,), in_specs=[REMOTE, REMOTE, whole((...  5.95 us
    pallas_call x1, Pallas kernels, gather(): pl.pallas_call(gather_kernel, grid=(1,), in_specs=[quarter_spec(NEAR) for...  5.82 us
    all_to_all x2, waiting for transfers between devices, transpose_all(): lax.all_to_all(x.reshape(DEV, 1, rows * LANES), ('gx', 'gy'), split_axis=...  4.63 us
    ppermute x1, starting transfers between devices, body(): south = lax.ppermute(high, 'gy', up)  3.96 us
  transfers between devices with their start and end apart: 10, of which 5 were waited for; matrix products, arithmetic and copies ran while one was open for 0% of the time, Pallas kernels for 31%

profile of v5, /device:TPU:1, one launch (start us, length us, event | category | flops | bytes accessed | tf_op | source)
XLA Modules:
  0.0 90.9 jit_solution(12300566438095758424)
XLA Ops:
  0.6 2.7 %payload.1 = (f32[768,128]{1,0:T(8,128)}, f32[128,256]{1,0:T(8,128)}) custom-call(s32[1,256]{1,0:T(1,128)} %bitcast.18, s32[8,256]{1,0:T(8,128)} %bitcast.17, f32[6,256]{1,0:T(8,128)} %coeff_in.1, f32[6,128,256]{2,1,0:T(8,128)} %walls.6, f32[64,256]{1,0:T(8,128)} %facade_in.1), custom_call_target="tpu_custom_call" | custom-call | tf_op jit(solution)/shard_map/payload/pallas_call | solution.py:95
  3.3 11.5 %all-to-all-start = ((f32[128,1,768]{2,1,0:T(1,128)}), f32[128,1,768]{2,1,0:T(1,128)S(1)}, u32[]{:S(2)}, u32[]{:S(2)}) async-start(f32[128,1,768]{2,1,0:T(1,128)} %bitcast.16), calls=%async_computation | async-start | bytes 786432 | tf_op jit(solution)/shard_map/all_to_all | solution.py:687
  14.8 3.2 %prep.1 = (f32[6,4,72,128]{3,2,1,0:T(8,128)S(1)}, f32[6,4,72,128]{3,2,1,0:T(8,128)S(1)}, f32[6,4,8,128]{3,2,1,0:T(8,128)S(1)}, f32[5,64,128]{2,1,0:T(8,128)}, f32[5,8,128]{2,1,0:T(8,128)}) custom-call(f32[2,64]{1,0:T(2,128)} %courant_in.1, f32[8,512,128]{2,1,0:T(8,128)} %bitcast.12), custom_call_target="tpu_custom_call" | custom-call | tf_op jit(solution)/shard_map/prep/pallas_call | solution.py:193
  18.0 3.7 %collective-permute-start = (f32[6,4,8,128]{3,2,1,0:T(8,128)S(1)}, f32[6,4,8,128]{3,2,1,0:T(8,128)S(1)}, u32[]{:S(2)}, u32[]{:S(2)}) collective-permute-start(f32[6,4,8,128]{3,2,1,0:T(8,128)S(1)} %get-tuple-element.42.pack), channel_id=1, source_target_pairs={{0,16},{16,32},{32,48},{48,64},{64,80},{80,96},{96,112},{1,17},{17... | collective-permute-start | bytes 294920 | tf_op jit(solution)/shard_map/ppermute | solution.py:335
  21.7 1.9 %collective-permute-start.1 = (f32[6,4,8,128]{3,2,1,0:T(8,128)S(1)}, f32[6,4,8,128]{3,2,1,0:T(8,128)S(1)}, u32[]{:S(2)}, u32[]{:S(2)}) collective-permute-start(f32[6,4,8,128]{3,2,1,0:T(8,128)S(1)} %get-tuple-element.42.pack), channel_id=1, source_target_pairs={{16,0},{32,16},{48,32},{64,48},{80,64},{96,80},{112,96},{17,1},{33... | collective-permute-start | bytes 294920 | tf_op jit(solution)/shard_map/ppermute | solution.py:335
  23.6 0.0 collective-permute-done.west
  23.7 4.1 %collective-permute-done.1.east = f32[6,4,8,128]{3,2,1,0:T(8,128)S(1)} collective-permute-done((f32[6,4,8,128]{3,2,1,0:T(8,128)S(1)}, f32[6,4,8,128]{3,2,1,0:T(8,128)S(1)}, u32[]{:S(2)}, u32[]{:S(2)}) %collective-permute-start.1) | collective-permute-done | bytes 98336 | tf_op jit(solution)/shard_map/ppermute | solution.py:335
  27.7 0.2 merge.2
  27.9 0.0 all-to-all-done
  27.9 4.0 %collective-permute-start.6 = (f32[6,4,72,128]{3,2,1,0:T(8,128)S(1)}, f32[6,4,72,128]{3,2,1,0:T(8,128)}, u32[]{:S(2)}, u32[]{:S(2)}) collective-permute-start(f32[6,4,72,128]{3,2,1,0:T(8,128)S(1)} %get-tuple-element.56.high), channel_id=1, source_target_pairs={{0,1},{1,2},{2,3},{3,4},{4,5},{5,6},{6,7},{7,8},{8,9},{9,10},{10,1... | collective-permute-start | bytes 2654216 | tf_op jit(solution)/shard_map/ppermute | solution.py:717
  31.9 3.1 %scatter.1 = (bf16[1024,1280]{1,0:T(8,128)(2,1)}, f32[2,4,72,128]{3,2,1,0:T(8,128)S(1)}, f32[2,4,72,128]{3,2,1,0:T(8,128)S(1)}, f32[2,4,8,128]{3,2,1,0:T(8,128)S(1)}) custom-call(f32[768,128]{1,0:T(8,128)S(1)} %bitcast.11, f32[8,512,128]{2,1,0:T(8,128)} %bitcast.13), custom_call_target="tpu_custom_call" | custom-call | tf_op jit(solution)/shard_map/scatter/pallas_call | solution.py:269
  34.9 2.1 %collective-permute-start.2 = (f32[2,4,8,128]{3,2,1,0:T(8,128)S(1)}, f32[2,4,8,128]{3,2,1,0:T(8,128)S(1)}, u32[]{:S(2)}, u32[]{:S(2)}) collective-permute-start(f32[2,4,8,128]{3,2,1,0:T(8,128)S(1)} %get-tuple-element.48.pack), channel_id=1, source_target_pairs={{0,16},{16,32},{32,48},{48,64},{64,80},{80,96},{96,112},{1,17},{17... | collective-permute-start | bytes 98312 | tf_op jit(solution)/shard_map/ppermute | solution.py:335
  37.1 2.2 %collective-permute-start.3 = (f32[2,4,8,128]{3,2,1,0:T(8,128)S(1)}, f32[2,4,8,128]{3,2,1,0:T(8,128)S(1)}, u32[]{:S(2)}, u32[]{:S(2)}) collective-permute-start(f32[2,4,8,128]{3,2,1,0:T(8,128)S(1)} %get-tuple-element.48.pack), channel_id=1, source_target_pairs={{16,0},{32,16},{48,32},{64,48},{80,64},{96,80},{112,96},{17,1},{33... | collective-permute-start | bytes 98312 | tf_op jit(solution)/shard_map/ppermute | solution.py:335
  39.3 0.0 collective-permute-done.2.west
  39.3 3.0 %collective-permute-done.3.east = f32[2,4,8,128]{3,2,1,0:T(8,128)S(1)} collective-permute-done((f32[2,4,8,128]{3,2,1,0:T(8,128)S(1)}, f32[2,4,8,128]{3,2,1,0:T(8,128)S(1)}, u32[]{:S(2)}, u32[]{:S(2)}) %collective-permute-start.3) | collective-permute-done | bytes 32800 | tf_op jit(solution)/shard_map/ppermute | solution.py:335
  42.3 0.1 merge.3
  42.4 2.6 %collective-permute-start.4 = (f32[2,4,72,128]{3,2,1,0:T(8,128)S(1)}, f32[2,4,72,128]{3,2,1,0:T(8,128)S(1)}, u32[]{:S(2)}, u32[]{:S(2)}) collective-permute-start(f32[2,4,72,128]{3,2,1,0:T(8,128)S(1)} %get-tuple-element.65.high), channel_id=1, source_target_pairs={{0,1},{1,2},{2,3},{3,4},{4,5},{5,6},{6,7},{7,8},{8,9},{9,10},{10,1... | collective-permute-start | bytes 884744 | tf_op jit(solution)/shard_map/ppermute | solution.py:346
  45.0 1.3 %collective-permute-start.5 = (f32[2,4,72,128]{3,2,1,0:T(8,128)S(1)}, f32[2,4,72,128]{3,2,1,0:T(8,128)S(1)}, u32[]{:S(2)}, u32[]{:S(2)}) collective-permute-start(f32[2,4,72,128]{3,2,1,0:T(8,128)S(1)} %get-tuple-element.64.low), channel_id=1, source_target_pairs={{1,0},{2,1},{3,2},{4,3},{5,4},{6,5},{7,6},{8,7},{9,8},{10,9},{11,1... | collective-permute-start | bytes 884744 | tf_op jit(solution)/shard_map/ppermute | solution.py:346
  46.3 1.3 %collective-permute-start.7 = (f32[6,4,72,128]{3,2,1,0:T(8,128)S(1)}, f32[6,4,72,128]{3,2,1,0:T(8,128)}, u32[]{:S(2)}, u32[]{:S(2)}) collective-permute-start(f32[6,4,72,128]{3,2,1,0:T(8,128)S(1)} %get-tuple-element.60.low), channel_id=1, source_target_pairs={{1,0},{2,1},{3,2},{4,3},{5,4},{6,5},{7,6},{8,7},{9,8},{10,9},{11,1... | collective-permute-start | bytes 2654216 | tf_op jit(solution)/shard_map/ppermute | solution.py:722
  47.6 6.0 %walls.4 = (f32[6,128,256]{2,1,0:T(8,128)}, f32[128,256]{1,0:T(8,128)}) custom-call(f32[8,128,128]{2,1,0:T(8,128)} %inverses.1, f32[6,128,256]{2,1,0:T(8,128)} %walls.6, s32[1,256]{1,0:T(1,128)} %bitcast.19), custom_call_target="tpu_custom_call" | custom-call | tf_op jit(solution)/shard_map/walls/pallas_call | solution.py:590
  53.6 3.1 %collective-permute-done.4.south = f32[2,4,72,128]{3,2,1,0:T(8,128)S(1)} collective-permute-done((f32[2,4,72,128]{3,2,1,0:T(8,128)S(1)}, f32[2,4,72,128]{3,2,1,0:T(8,128)S(1)}, u32[]{:S(2)}, u32[]{:S(2)}) %collective-permute-start.4) | collective-permute-done | bytes 294944 | tf_op jit(solution)/shard_map/ppermute | solution.py:346
  56.7 0.0 collective-permute-done.5.north
  56.7 0.0 collective-permute-done.6.south
  56.7 5.8 %gather.1 = (f32[8,512,128]{2,1,0:T(8,128)}, f32[1280,128]{1,0:T(8,128)}) custom-call(f32[2,4,72,128]{3,2,1,0:T(8,128)S(1)} %collective-permute-done.4.south, f32[2,4,72,128]{3,2,1,0:T(8,128)S(1)} %get-tuple-element.64.low, f32[2,4,72,128]{3,2,1,0:T(8,128)S(1)} %get-tuple-element.65.high, f32[2,4,72,128]{3,2,1,0:T(8,128)S(1)} %collective-permute-done.5.north, ...), custom_call_target="tpu_custom_call" | custom-call | tf_op jit(solution)/shard_map/gather/pallas_call | solution.py:521
  62.5 10.0 %all-to-all-start.1 = ((f32[128,1,1280]{2,1,0:T(1,128)}), f32[128,1,1280]{2,1,0:T(1,128)S(1)}, u32[]{:S(2)}, u32[]{:S(2)}) async-start(f32[128,1,1280]{2,1,0:T(1,128)} %bitcast.15), calls=%async_computation.1 | async-start | bytes 1310720 | tf_op jit(solution)/shard_map/all_to_all | solution.py:687
  72.5 0.7 collective-permute-done.7.north
  73.2 9.9 %fields.1 = f32[8,512,128]{2,1,0:T(8,128)} custom-call(f32[6,4,72,128]{3,2,1,0:T(8,128)} %collective-permute-done.6.south, f32[6,4,72,128]{3,2,1,0:T(8,128)S(1)} %get-tuple-element.60.low, f32[6,4,72,128]{3,2,1,0:T(8,128)S(1)} %get-tuple-element.56.high, f32[6,4,72,128]{3,2,1,0:T(8,128)} %collective-permute-done.7.north, ...), custom_call_target="tpu_custom_call", output_to_operand_aliasing={{}: (7, {})} | custom-call | tf_op jit(solution)/shard_map/fields/pallas_call | solution.py:477
  83.1 4.6 %all-to-all-done.1 = f32[128,1,1280]{2,1,0:T(1,128)S(1)} async-done(((f32[128,1,1280]{2,1,0:T(1,128)}), f32[128,1,1280]{2,1,0:T(1,128)S(1)}, u32[]{:S(2)}, u32[]{:S(2)}) %all-to-all-start.1) | async-done | bytes 655392 | tf_op jit(solution)/shard_map/all_to_all | solution.py:687
  87.8 3.1 %final.1 = (f32[128,256]{1,0:T(8,128)}, f32[6,128,256]{2,1,0:T(8,128)}) custom-call(f32[1280,128]{1,0:T(8,128)S(1)} %bitcast.10, f32[128,256]{1,0:T(8,128)} %get-tuple-element.70.code_in, f32[64,256]{1,0:T(8,128)} %facade_in.1, f32[6,256]{1,0:T(8,128)} %coeff_in.1, f32[6,128,256]{2,1,0:T(8,128)} %walls.6, f32[6,128,256]{2,1,0:T(8,128)} %get-tuple-element.71.product, ...), custom_call_target="tpu_custom_call" | custom-call | tf_op jit(solution)/shard_map/final/pallas_call | solution.py:653
  (1 shorter events, 0.0 us)
Async XLA Ops:
  3.3 24.6 %all-to-all-start = ((f32[128,1,768]{2,1,0:T(1,128)}), f32[128,1,768]{2,1,0:T(1,128)S(1)}, u32[]{:S(2)}, u32[]{:S(2)}) async-start(f32[128,1,768]{2,1,0:T(1,128)} %bitcast.16), calls=%async_computation | async-start | bytes 786432 | tf_op jit(solution)/shard_map/all_to_all | solution.py:687
  18.0 5.6 %collective-permute-start = (f32[6,4,8,128]{3,2,1,0:T(8,128)S(1)}, f32[6,4,8,128]{3,2,1,0:T(8,128)S(1)}, u32[]{:S(2)}, u32[]{:S(2)}) collective-permute-start(f32[6,4,8,128]{3,2,1,0:T(8,128)S(1)} %get-tuple-element.42.pack), channel_id=1, source_target_pairs={{0,16},{16,32},{32,48},{48,64},{64,80},{80,96},{96,112},{1,17},{17... | collective-permute-start | bytes 294920 | tf_op jit(solution)/shard_map/ppermute | solution.py:335
  21.7 6.0 %collective-permute-start.1 = (f32[6,4,8,128]{3,2,1,0:T(8,128)S(1)}, f32[6,4,8,128]{3,2,1,0:T(8,128)S(1)}, u32[]{:S(2)}, u32[]{:S(2)}) collective-permute-start(f32[6,4,8,128]{3,2,1,0:T(8,128)S(1)} %get-tuple-element.42.pack), channel_id=1, source_target_pairs={{16,0},{32,16},{48,32},{64,48},{80,64},{96,80},{112,96},{17,1},{33... | collective-permute-start | bytes 294920 | tf_op jit(solution)/shard_map/ppermute | solution.py:335
  27.9 28.8 %collective-permute-start.6 = (f32[6,4,72,128]{3,2,1,0:T(8,128)S(1)}, f32[6,4,72,128]{3,2,1,0:T(8,128)}, u32[]{:S(2)}, u32[]{:S(2)}) collective-permute-start(f32[6,4,72,128]{3,2,1,0:T(8,128)S(1)} %get-tuple-element.56.high), channel_id=1, source_target_pairs={{0,1},{1,2},{2,3},{3,4},{4,5},{5,6},{6,7},{7,8},{8,9},{9,10},{10,1... | collective-permute-start | bytes 2654216 | tf_op jit(solution)/shard_map/ppermute | solution.py:717
  34.9 4.3 %collective-permute-start.2 = (f32[2,4,8,128]{3,2,1,0:T(8,128)S(1)}, f32[2,4,8,128]{3,2,1,0:T(8,128)S(1)}, u32[]{:S(2)}, u32[]{:S(2)}) collective-permute-start(f32[2,4,8,128]{3,2,1,0:T(8,128)S(1)} %get-tuple-element.48.pack), channel_id=1, source_target_pairs={{0,16},{16,32},{32,48},{48,64},{64,80},{80,96},{96,112},{1,17},{17... | collective-permute-start | bytes 98312 | tf_op jit(solution)/shard_map/ppermute | solution.py:335
  37.1 5.2 %collective-permute-start.3 = (f32[2,4,8,128]{3,2,1,0:T(8,128)S(1)}, f32[2,4,8,128]{3,2,1,0:T(8,128)S(1)}, u32[]{:S(2)}, u32[]{:S(2)}) collective-permute-start(f32[2,4,8,128]{3,2,1,0:T(8,128)S(1)} %get-tuple-element.48.pack), channel_id=1, source_target_pairs={{16,0},{32,16},{48,32},{64,48},{80,64},{96,80},{112,96},{17,1},{33... | collective-permute-start | bytes 98312 | tf_op jit(solution)/shard_map/ppermute | solution.py:335
  42.4 14.3 %collective-permute-start.4 = (f32[2,4,72,128]{3,2,1,0:T(8,128)S(1)}, f32[2,4,72,128]{3,2,1,0:T(8,128)S(1)}, u32[]{:S(2)}, u32[]{:S(2)}) collective-permute-start(f32[2,4,72,128]{3,2,1,0:T(8,128)S(1)} %get-tuple-element.65.high), channel_id=1, source_target_pairs={{0,1},{1,2},{2,3},{3,4},{4,5},{5,6},{6,7},{7,8},{8,9},{9,10},{10,1... | collective-permute-start | bytes 884744 | tf_op jit(solution)/shard_map/ppermute | solution.py:346
  45.0 11.7 %collective-permute-start.5 = (f32[2,4,72,128]{3,2,1,0:T(8,128)S(1)}, f32[2,4,72,128]{3,2,1,0:T(8,128)S(1)}, u32[]{:S(2)}, u32[]{:S(2)}) collective-permute-start(f32[2,4,72,128]{3,2,1,0:T(8,128)S(1)} %get-tuple-element.64.low), channel_id=1, source_target_pairs={{1,0},{2,1},{3,2},{4,3},{5,4},{6,5},{7,6},{8,7},{9,8},{10,9},{11,1... | collective-permute-start | bytes 884744 | tf_op jit(solution)/shard_map/ppermute | solution.py:346
  46.3 26.9 %collective-permute-start.7 = (f32[6,4,72,128]{3,2,1,0:T(8,128)S(1)}, f32[6,4,72,128]{3,2,1,0:T(8,128)}, u32[]{:S(2)}, u32[]{:S(2)}) collective-permute-start(f32[6,4,72,128]{3,2,1,0:T(8,128)S(1)} %get-tuple-element.60.low), channel_id=1, source_target_pairs={{1,0},{2,1},{3,2},{4,3},{5,4},{6,5},{7,6},{8,7},{9,8},{10,9},{11,1... | collective-permute-start | bytes 2654216 | tf_op jit(solution)/shard_map/ppermute | solution.py:722
  62.5 25.3 %all-to-all-start.1 = ((f32[128,1,1280]{2,1,0:T(1,128)}), f32[128,1,1280]{2,1,0:T(1,128)S(1)}, u32[]{:S(2)}, u32[]{:S(2)}) async-start(f32[128,1,1280]{2,1,0:T(1,128)} %bitcast.15), calls=%async_computation.1 | async-start | bytes 1310720 | tf_op jit(solution)/shard_map/all_to_all | solution.py:687
